TPU v7x, 32 devices: a whole 2x2x4 slice. The times are simulated.
32 devices in a mesh: seq: 4 (over x, core), batch: 8 (over z, y).
Axes of the slice: x: 2, y: 2, z: 4, core: 2. Of those that a mesh axis runs over, the one named last changes fastest.
Arguments:
- hidden_in: bfloat16 [32768, 768], P(('seq', 'batch')), may hold values from -6 to 6
- seq_lengths: int32 [32, 2], P(('seq', 'batch')), may hold values from 0 to 1023, as said below
- head_swap: int32 [12], replicated, may hold values from 0 to 1, as said below
- place: int32 [32768], P(('seq', 'batch')), may hold values from -1 to 28671, as said below
- w_qkv: bfloat16 [768, 2304], replicated, may hold values from -0.21875 to 0.21875
- qv_bias: float32 [1536], replicated, may hold values from -3 to 3
- w_out: bfloat16 [768, 768], replicated, may hold values from -0.875 to 0.875
- out_bias: float32 [768], replicated, may hold values from -2 to 2
- norm1_gain: float32 [768], replicated, may hold values from 0.25 to 1.75
- norm1_bias: float32 [768], replicated, may hold values from -2 to 2
- w_in: bfloat16 [768, 3072], replicated, may hold values from -0.21875 to 0.21875
- in_bias: float32 [3072], replicated, may hold values from -3 to 3
- w_down: bfloat16 [3072, 768], replicated, may hold values from -0.109375 to 0.109375
- down_bias: float32 [768], replicated, may hold values from -2 to 2
- norm2_gain: float32 [768], replicated, may hold values from 0.25 to 1.75
- norm2_bias: float32 [768], replicated, may hold values from -2 to 2
- cotangent: bfloat16 [28672, 768], P(('seq', 'batch')), may hold values from -6 to 6
Outputs:
- mixed: bfloat16 [28672, 768], P(('seq', 'batch'))
- input_grad: bfloat16 [32768, 768], P(('seq', 'batch'))
- grad_w_qkv: float32 [768, 2304], P('seq')
- grad_qv_bias: float32 [1536], P('seq')
- grad_w_out: float32 [768, 768], P('seq')
- grad_out_bias: float32 [768], P('seq')
- grad_norm1_gain: float32 [768], P('seq')
- grad_norm1_bias: float32 [768], P('seq')
- grad_w_in: float32 [768, 3072], P('seq')
- grad_in_bias: float32 [3072], P('seq')
- grad_w_down: float32 [3072, 768], P('seq')
- grad_down_bias: float32 [768], P('seq')
- grad_norm2_gain: float32 [768], P('seq')
- grad_norm2_bias: float32 [768], P('seq')
Inputs may be any that keep to these rules, and one draw needn't show every extreme that they name: seq_lengths[g,1] = 0 marks a long group, with seq_lengths[g,0] from 769 to 1023; otherwise both entries lie from 385 to 511. The lengths of all groups sum to 28672. `head_swap`: at least one head has 0 and at least one has 1. place is -1 exactly on padding rows and maps the live rows one to one onto 0 to 28671; rows k * 896 to (k + 1) * 896 - 1 form device k's share, and the live rows of one row group map to at most 32 rows of one share, exactly 32 for some group and share.
All inputs are finite; a program needn't handle non-finite values.
Results may differ from a plain program's by a relative error of at most 0.02.
Values may be sent and summed in bfloat16 or wider, within the bound.
No kernel may reach another device: no remote copies, remote signals or barrier semaphores. Data moves between devices by JAX's collectives and lax.ppermute only.
A program may use at most 192 MiB of HBM per device.

v0:
```python
import jax
import jax.numpy as jnp
from jax import lax
from jax.sharding import PartitionSpec as P

EPS = 1e-05
BIG = 1e30


def norm_forward(inputs, gain_vec, bias_vec):
    center = inputs - jnp.mean(inputs, axis=-1, keepdims=True)
    inverse = lax.rsqrt(jnp.mean(center * center, axis=-1, keepdims=True) + EPS)
    normed = center * inverse
    return (normed * gain_vec + bias_vec, normed, inverse)


def norm_backward(upstream, normed, inverse, gain_vec):
    scaled = upstream * gain_vec
    inner = (
        scaled
        - jnp.mean(scaled, axis=-1, keepdims=True)
        - normed * jnp.mean(scaled * normed, axis=-1, keepdims=True)
    )
    return (inner * inverse, jnp.sum(upstream * normed, axis=0), jnp.sum(upstream, axis=0))


def gelu_slope(inputs):
    return (
        0.5 * (1.0 + lax.erf(inputs * 0.7071067811865476))
        + inputs * jnp.exp(-0.5 * inputs * inputs) * 0.3989422804014327
    )


def block_masks(lengths, swaps, row_count):
    half_rows = row_count // 2
    quarter_rows = row_count // 4
    is_long = lengths[1] == 0
    positions = jnp.arange(half_rows, dtype=jnp.int32)
    first_ok = positions < lengths[0]
    second_ok = jnp.where(is_long, positions + half_rows < lengths[0], positions < lengths[1])
    key_ok = jnp.stack([first_ok, second_ok])
    swapped = swaps == 1
    cross_pair = jnp.logical_and(is_long, swapped)
    key_pick = jnp.where(cross_pair[:, None, None], key_ok[::-1][None], key_ok[None])
    band_index = positions // quarter_rows
    same_band = band_index[:, None] == band_index[None, :]
    band_ok = jnp.logical_or(is_long, same_band[None] != swapped[:, None, None])
    return (cross_pair, jnp.logical_and(band_ok[:, None], key_pick[:, :, None, :]))


def split_heads(columns, head_count):
    row_count, model_width = columns.shape
    return columns.reshape(2, row_count // 2, head_count, model_width // head_count).transpose(
        2, 0, 1, 3
    )


def join_heads(blocked):
    head_count, halves, half_rows, head_size = blocked.shape
    return blocked.transpose(1, 2, 0, 3).reshape(halves * half_rows, head_count * head_size)


def pick_half(cross_pair, blocked):
    return jnp.where(cross_pair[:, None, None, None], blocked[:, ::-1], blocked)


def contract_rows(left_op, right_op):
    return lax.dot_general(
        left_op, right_op, (((0,), (0,)), ((), ())), preferred_element_type=jnp.float32
    )


def times_transpose(left_op, right_op):
    return lax.dot_general(
        left_op, right_op, (((1,), (1,)), ((), ())), preferred_element_type=jnp.float32
    )


def score_block(queries, keys_sel, allowed, score_scale):
    raw_scores = (
        jnp.einsum("hbid,hbjd->hbij", queries, keys_sel, preferred_element_type=jnp.float32)
        * score_scale
    )
    return jnp.where(allowed, raw_scores, -BIG)


def body(
    hidden_in,
    seq_lengths,
    head_swap,
    place,
    w_qkv,
    qv_bias,
    w_out,
    out_bias,
    norm1_gain,
    norm1_bias,
    w_in,
    in_bias,
    w_down,
    down_bias,
    norm2_gain,
    norm2_bias,
    cotangent,
):
    row_count, model_width = hidden_in.shape
    head_count = head_swap.shape[0]
    score_scale = (model_width // head_count) ** (-0.5)
    devices = lax.axis_size(("seq", "batch"))
    capacity = (row_count + devices - 1) // devices
    ffn_rows = cotangent.shape[0]
    cross_pair, allowed = block_masks(seq_lengths[0], head_swap, row_count)
    zero_bias = jnp.zeros((model_width,), jnp.float32)
    bias_three = jnp.concatenate([qv_bias[:model_width], zero_bias, qv_bias[model_width:]])
    projected = (jnp.dot(hidden_in, w_qkv, preferred_element_type=jnp.float32) + bias_three).astype(
        jnp.bfloat16
    )
    queries = split_heads(projected[:, :model_width], head_count)
    keys_sel = pick_half(
        cross_pair, split_heads(projected[:, model_width : 2 * model_width], head_count)
    )
    values_sel = pick_half(cross_pair, split_heads(projected[:, 2 * model_width :], head_count))
    masked = score_block(queries, keys_sel, allowed, score_scale)
    top_score = jnp.max(masked, axis=-1, keepdims=True)
    exp_scores = jnp.exp(masked - top_score)
    log_total = top_score + jnp.log(jnp.sum(exp_scores, axis=-1, keepdims=True))
    soft_low = (exp_scores / jnp.sum(exp_scores, axis=-1, keepdims=True)).astype(jnp.bfloat16)
    context = join_heads(
        jnp.einsum("hbij,hbjd->hbid", soft_low, values_sel, preferred_element_type=jnp.float32)
    ).astype(jnp.bfloat16)
    attn = jnp.dot(context, w_out, preferred_element_type=jnp.float32) + out_bias
    first_out, normed_one, inverse_one = norm_forward(
        hidden_in.astype(jnp.float32) + attn, norm1_gain, norm1_bias
    )
    first_low = first_out.astype(jnp.bfloat16)
    is_live = place >= 0
    target_dev = jnp.where(is_live, place // ffn_rows, 0)
    columns = jnp.arange(devices, dtype=jnp.int32)
    onehot = jnp.logical_and(target_dev[:, None] == columns[None, :], is_live[:, None]).astype(
        jnp.float32
    )
    positions = jnp.arange(row_count, dtype=jnp.int32)
    lower_ones = (positions[:, None] >= positions[None, :]).astype(jnp.float32)
    running = jnp.dot(lower_ones, onehot, preferred_element_type=jnp.float32)
    pair_rank = (jnp.sum(running * onehot, axis=1) - 1.0).astype(jnp.int32)
    send_slot = jnp.where(is_live, target_dev * capacity + pair_rank, devices * capacity)
    outgoing = (
        jnp.zeros((devices * capacity, model_width), jnp.bfloat16)
        .at[send_slot]
        .set(first_low, mode="drop")
    )
    out_target = (
        jnp.full((devices * capacity,), ffn_rows, jnp.int32)
        .at[send_slot]
        .set(place % ffn_rows, mode="drop")
    )
    incoming, in_target = (
        lax.all_to_all(outgoing, ("seq", "batch"), split_axis=0, concat_axis=0, tiled=True),
        lax.all_to_all(out_target, ("seq", "batch"), split_axis=0, concat_axis=0, tiled=True),
    )
    moved = (
        jnp.zeros((ffn_rows, model_width), jnp.bfloat16).at[in_target].set(incoming, mode="drop")
    )
    pre_act = jnp.dot(moved, w_in, preferred_element_type=jnp.float32) + in_bias
    hidden = jax.nn.gelu(pre_act, approximate=False).astype(jnp.bfloat16)
    branch = jnp.dot(hidden, w_down, preferred_element_type=jnp.float32) + down_bias
    mixed, normed_two, inverse_two = norm_forward(
        moved.astype(jnp.float32) + branch, norm2_gain, norm2_bias
    )
    g_pre_two, g_norm2_gain, g_norm2_bias = norm_backward(
        cotangent.astype(jnp.float32), normed_two, inverse_two, norm2_gain
    )
    g_branch = g_pre_two.astype(jnp.bfloat16)
    g_down_bias = jnp.sum(g_branch.astype(jnp.float32), axis=0)
    g_w_down = contract_rows(hidden, g_branch)
    g_act = (times_transpose(g_branch, w_down) * gelu_slope(pre_act)).astype(jnp.bfloat16)
    g_in_bias = jnp.sum(g_act.astype(jnp.float32), axis=0)
    g_w_in = contract_rows(moved, g_act)
    g_moved = (g_pre_two + times_transpose(g_act, w_in)).astype(jnp.bfloat16)
    has_target = in_target < ffn_rows
    g_back = jnp.take(g_moved, jnp.minimum(in_target, ffn_rows - 1), axis=0)
    g_back = jnp.where(has_target[:, None], g_back, jnp.zeros_like(g_back))
    returned = lax.all_to_all(g_back, ("seq", "batch"), split_axis=0, concat_axis=0, tiled=True)
    g_first = jnp.take(returned, jnp.minimum(send_slot, devices * capacity - 1), axis=0)
    g_first = jnp.where(is_live[:, None], g_first, jnp.zeros_like(g_first)).astype(jnp.float32)
    g_pre_one, g_norm1_gain, g_norm1_bias = norm_backward(
        g_first, normed_one, inverse_one, norm1_gain
    )
    g_attn = g_pre_one.astype(jnp.bfloat16)
    g_out_bias = jnp.sum(g_attn.astype(jnp.float32), axis=0)
    g_w_out = contract_rows(context, g_attn)
    g_context = split_heads(times_transpose(g_attn, w_out).astype(jnp.bfloat16), head_count)
    soft_again = jnp.exp(score_block(queries, keys_sel, allowed, score_scale) - log_total)
    soft_again_low = soft_again.astype(jnp.bfloat16)
    g_values_sel = jnp.einsum(
        "hbij,hbid->hbjd", soft_again_low, g_context, preferred_element_type=jnp.float32
    )
    g_soft = jnp.einsum(
        "hbid,hbjd->hbij", g_context, values_sel, preferred_element_type=jnp.float32
    )
    g_scores = (
        soft_again * (g_soft - jnp.sum(soft_again * g_soft, axis=-1, keepdims=True))
    ).astype(jnp.bfloat16)
    g_queries = (
        jnp.einsum("hbij,hbjd->hbid", g_scores, keys_sel, preferred_element_type=jnp.float32)
        * score_scale
    )
    g_keys_sel = (
        jnp.einsum("hbij,hbid->hbjd", g_scores, queries, preferred_element_type=jnp.float32)
        * score_scale
    )
    g_projected = jnp.concatenate(
        [
            join_heads(g_queries),
            join_heads(pick_half(cross_pair, g_keys_sel)),
            join_heads(pick_half(cross_pair, g_values_sel)),
        ],
        axis=1,
    ).astype(jnp.bfloat16)
    g_proj_wide = g_projected.astype(jnp.float32)
    g_qv_bias = jnp.concatenate(
        [
            jnp.sum(g_proj_wide[:, :model_width], axis=0),
            jnp.sum(g_proj_wide[:, 2 * model_width :], axis=0),
        ]
    )
    g_w_qkv = contract_rows(hidden_in, g_projected)
    input_grad = (times_transpose(g_projected, w_qkv) + g_pre_one).astype(jnp.bfloat16)
    shares = (
        lax.psum_scatter(
            g_w_qkv.astype(jnp.bfloat16), "seq", scatter_dimension=0, tiled=True
        ).astype(jnp.float32),
        lax.psum_scatter(
            g_qv_bias.astype(jnp.bfloat16), "seq", scatter_dimension=0, tiled=True
        ).astype(jnp.float32),
        lax.psum_scatter(
            g_w_out.astype(jnp.bfloat16), "seq", scatter_dimension=0, tiled=True
        ).astype(jnp.float32),
        lax.psum_scatter(
            g_out_bias.astype(jnp.bfloat16), "seq", scatter_dimension=0, tiled=True
        ).astype(jnp.float32),
        lax.psum_scatter(
            g_norm1_gain.astype(jnp.bfloat16), "seq", scatter_dimension=0, tiled=True
        ).astype(jnp.float32),
        lax.psum_scatter(
            g_norm1_bias.astype(jnp.bfloat16), "seq", scatter_dimension=0, tiled=True
        ).astype(jnp.float32),
        lax.psum_scatter(
            g_w_in.astype(jnp.bfloat16), "seq", scatter_dimension=0, tiled=True
        ).astype(jnp.float32),
        lax.psum_scatter(
            g_in_bias.astype(jnp.bfloat16), "seq", scatter_dimension=0, tiled=True
        ).astype(jnp.float32),
        lax.psum_scatter(
            g_w_down.astype(jnp.bfloat16), "seq", scatter_dimension=0, tiled=True
        ).astype(jnp.float32),
        lax.psum_scatter(
            g_down_bias.astype(jnp.bfloat16), "seq", scatter_dimension=0, tiled=True
        ).astype(jnp.float32),
        lax.psum_scatter(
            g_norm2_gain.astype(jnp.bfloat16), "seq", scatter_dimension=0, tiled=True
        ).astype(jnp.float32),
        lax.psum_scatter(
            g_norm2_bias.astype(jnp.bfloat16), "seq", scatter_dimension=0, tiled=True
        ).astype(jnp.float32),
    )
    totals = (
        lax.psum(shares[0].astype(jnp.bfloat16), "batch").astype(jnp.float32),
        lax.psum(shares[1].astype(jnp.bfloat16), "batch").astype(jnp.float32),
        lax.psum(shares[2].astype(jnp.bfloat16), "batch").astype(jnp.float32),
        lax.psum(shares[3].astype(jnp.bfloat16), "batch").astype(jnp.float32),
        lax.psum(shares[4].astype(jnp.bfloat16), "batch").astype(jnp.float32),
        lax.psum(shares[5].astype(jnp.bfloat16), "batch").astype(jnp.float32),
        lax.psum(shares[6].astype(jnp.bfloat16), "batch").astype(jnp.float32),
        lax.psum(shares[7].astype(jnp.bfloat16), "batch").astype(jnp.float32),
        lax.psum(shares[8].astype(jnp.bfloat16), "batch").astype(jnp.float32),
        lax.psum(shares[9].astype(jnp.bfloat16), "batch").astype(jnp.float32),
        lax.psum(shares[10].astype(jnp.bfloat16), "batch").astype(jnp.float32),
        lax.psum(shares[11].astype(jnp.bfloat16), "batch").astype(jnp.float32),
    )
    return (
        mixed.astype(jnp.bfloat16),
        input_grad,
        totals[0],
        totals[1],
        totals[2],
        totals[3],
        totals[4],
        totals[5],
        totals[6],
        totals[7],
        totals[8],
        totals[9],
        totals[10],
        totals[11],
    )


def solution(mesh):
    in_specs = (
        P(("seq", "batch"), None),
        P(("seq", "batch"), None),
        P(),
        P(("seq", "batch")),
        P(),
        P(),
        P(),
        P(),
        P(),
        P(),
        P(),
        P(),
        P(),
        P(),
        P(),
        P(),
        P(("seq", "batch"), None),
    )
    out_specs = (
        P(("seq", "batch"), None),
        P(("seq", "batch"), None),
        P("seq", None),
        P("seq"),
        P("seq", None),
        P("seq"),
        P("seq"),
        P("seq"),
        P("seq", None),
        P("seq"),
        P("seq", None),
        P("seq"),
        P("seq"),
        P("seq"),
    )
    return jax.shard_map(body, mesh=mesh, in_specs=in_specs, out_specs=out_specs, check_vma=False)
```

profile of v0, /device:TPU:0, one launch (start us, length us, event | category | flops | bytes accessed | tf_op | source)
XLA Modules:
  0.0 752.1 jit_solution(6968527874258142202)
XLA Ops:
  16.4 7.3 all-to-all-start
  72.0 11.0 %fusion.80 = (f32[12,2,512]{2,1,0:T(2,128)S(1)}, f32[12,2,512,512]{2,3,1,0:T(8,128)}) fusion(bf16[12,2,512,64]{2,3,1,0:T(8,128)(2,1)S(1)} %get-tuple-element.119, bf16[2,512,12,64]{1,0,3,2:T(2,128)(2,1)S(1)} %copy-done.14, pred[12,2,512]{2,1,0:T(4,128)(4,1)S(1)} %broadcast_select_fusion, pred[12,512,512]{1,2,0:T(8,128)(4,1)S(1)} %compare_or_fusion), kind=kOutput, calls=%fused_computation.172 | convolution fusion | flops 830459904 | bytes 31518720 | tf_op jit(solution)/shard_map/hbid,hbjd->hbij/dot_general | solution.py:81
  83.1 10.1 %fusion = f32[12,2,512]{2,1,0:T(2,128)S(1)} fusion(f32[12,2,512,512]{2,3,1,0:T(8,128)} %get-tuple-element.126, f32[12,2,512]{2,1,0:T(2,128)S(1)} %get-tuple-element.125), kind=kLoop, calls=%fused_computation.11 | loop fusion | flops 12570624 | bytes 25264128 | tf_op jit(solution)/shard_map/reduce_sum | solution.py:127
  93.2 11.1 %fusion.46 = bf16[2,512,12,64]{1,3,0,2:T(8,128)(2,1)S(1)} fusion(bf16[12,2,512,64]{2,3,1,0:T(8,128)(2,1)S(1)} %get-tuple-element.120, f32[12,2,512,512]{2,3,1,0:T(8,128)} %get-tuple-element.126, f32[12,2,512]{2,1,0:T(2,128)S(1)} %fusion, f32[12,2,512]{2,1,0:T(2,128)S(1)} %get-tuple-element.125), kind=kOutput, calls=%fused_computation.99 | convolution fusion | flops 824967168 | bytes 28409856 | tf_op jit(solution)/shard_map/hbij,hbjd->hbid/dot_general | solution.py:129
  137.2 29.4 %all-to-all-done.1 = bf16[32,32,768]{2,1,0:T(8,128)(2,1)} async-done(((bf16[32,32,768]{2,1,0:T(8,128)(2,1)}), bf16[32,32,768]{2,1,0:T(8,128)(2,1)}, u32[]{:S(2)}, u32[]{:S(2)}) %all-to-all-start.1) | async-done | bytes 1572896 | tf_op jit(solution)/shard_map/all_to_all | solution.py:158
  176.2 30.5 %fusion.8 = (bf16[896,3072]{1,0:T(8,128)(2,1)S(1)}, f32[896,3072]{1,0:T(8,128)}) fusion(f32[3072]{0:T(1024)} %param.28, bf16[896,768]{1,0:T(8,128)(2,1)} %scatter_custom_fusion.2, bf16[768,3072]{1,0:T(8,128)(2,1)} %param.27), kind=kOutput, calls=%fused_computation.21 | convolution fusion | flops 4409524224 | bytes 22622208 | tf_op jit(solution)/shard_map/dot_general | solution.py:164
  206.7 8.9 %fusion.82 = (f32[896]{0:T(1024)S(1)}, f32[896,768]{0,1:T(8,128)S(1)}) fusion(f32[768]{0:T(1024)S(1)} %copy-done.56, bf16[896,3072]{1,0:T(8,128)(2,1)S(1)} %get-tuple-element.129, bf16[3072,768]{1,0:T(8,128)(2,1)} %param.29, bf16[896,768]{0,1:T(8,128)(2,1)S(1)} %copy-done.22), kind=kOutput, calls=%fused_computation.174 | convolution fusion | flops 4230609920 | bytes 14359040 | tf_op jit(solution)/shard_map/dot_general | solution.py:166
  221.8 11.6 %fusion.83 = (bf16[3072]{0:T(1024)(128)(2,1)}, bf16[896,3072]{1,0:T(8,128)(2,1)S(1)}) fusion(f32[896,3072]{1,0:T(8,128)} %get-tuple-element.130, f32[3072]{0:T(1024)S(1)} %copy-done.54, bf16[896,768]{0,1:T(8,128)(2,1)S(1)} %get-tuple-element.99, bf16[3072,768]{1,0:T(8,128)(2,1)S(1)} %bitcast.124), kind=kOutput, calls=%fused_computation.175 | convolution fusion | flops 4260885504 | bytes 22628352 | tf_op jit(solution)/shard_map/dot_general | solution.py:74
  259.8 37.3 %all-to-all-done.2 = bf16[32,32,768]{2,1,0:T(8,128)(2,1)} async-done(((bf16[32,32,768]{2,1,0:T(8,128)(2,1)}), bf16[32,32,768]{2,1,0:T(8,128)(2,1)}, u32[]{:S(2)}, u32[]{:S(2)}) %all-to-all-start.2) | async-done | bytes 1572896 | tf_op jit(solution)/shard_map/all_to_all | solution.py:183
  323.8 11.9 %fusion.2 = bf16[12,2,512,64]{2,3,1,0:T(8,128)(2,1)} fusion(f32[12,2,512,512]{2,3,1,0:T(8,128)} %get-tuple-element.126, f32[12,2,512]{2,1,0:T(2,128)} %bitcast.114, bf16[12,2,512,64]{2,1,3,0:T(2,128)(2,1)} %bitcast.101), kind=kOutput, calls=%fused_computation.15 | convolution fusion | flops 817889280 | bytes 28360704 | tf_op jit(solution)/shard_map/hbij,hbid->hbjd/dot_general | solution.py:195
  335.6 20.4 %multiply_reduce_fusion = (f32[12,2,512]{2,1,0:T(2,128)}, f32[12,2,512,512]{2,3,1,0:T(8,128)}) fusion(f32[12,2,512,512]{2,3,1,0:T(8,128)} %get-tuple-element.126, f32[12,2,512]{2,1,0:T(2,128)} %bitcast.115, bf16[12,2,512,64]{2,3,1,0:T(8,128)(2,1)} %copy-done.13, bf16[12,2,512,64]{2,1,3,0:T(2,128)(2,1)} %bitcast.102), kind=kOutput, calls=%fused_computation.6 | convolution fusion | flops 824168448 | bytes 53575680 | tf_op jit(solution)/shard_map/hbid,hbjd->hbij/dot_general | solution.py:198
  356.1 17.2 %multiply_convert_fusion = bf16[12,2,512,512]{2,3,1,0:T(8,128)(2,1)S(1)} fusion(f32[12,2,512,512]{2,3,1,0:T(8,128)} %get-tuple-element.134, f32[12,2,512,512]{2,3,1,0:T(8,128)} %get-tuple-element.126, f32[12,2,512]{2,1,0:T(2,128)} %get-tuple-element.133, f32[12,2,512]{2,1,0:T(2,128)} %bitcast.116), kind=kLoop, calls=%fused_computation.5 | loop fusion | flops 25165824 | bytes 63012864 | tf_op jit(solution)/shard_map/convert_element_type | solution.py:203
  381.1 10.5 %fusion.42 = f32[12,2,512,64]{2,3,1,0:T(8,128)} fusion(bf16[12,2,512,512]{2,3,1,0:T(8,128)(2,1)} %copy-done.1, bf16[2,512,12,64]{1,0,3,2:T(2,128)(2,1)} %reshape.290), kind=kOutput, calls=%fused_computation.90 | convolution fusion | flops 805306368 | bytes 17301504 | tf_op jit(solution)/shard_map/hbij,hbid->hbjd/dot_general | solution.py:209
  419.6 9.8 %convolution_convert_fusion = bf16[3072,768]{1,0:T(8,128)(2,1)} fusion(bf16[896,3072]{1,0:T(8,128)(2,1)} %copy-done.58, bf16[896,768]{0,1:T(8,128)(2,1)} %copy-done.21), kind=kOutput, calls=%fused_computation.44 | convolution fusion | flops 4230217728 | bytes 11599872 | tf_op jit(solution)/shard_map/dot_general | solution.py:68
  429.5 9.6 %convolution_convert_fusion.1 = bf16[768,3072]{1,0:T(8,128)(2,1)} fusion(bf16[896,768]{1,0:T(8,128)(2,1)} %scatter_custom_fusion.2, bf16[896,3072]{1,0:T(8,128)(2,1)} %copy-done.57), kind=kOutput, calls=%fused_computation.45 | convolution fusion | flops 4230217728 | bytes 11599872 | tf_op jit(solution)/shard_map/dot_general | solution.py:68
  439.2 14.1 %reduce-scatter.13.cloned.1.call-done = bf16[192,2304]{1,0:T(8,128)(2,1)} async-done(((bf16[768,2304]{1,0:T(8,128)(2,1)}), bf16[192,2304]{1,0:T(8,128)(2,1)}) %reduce-scatter.13.cloned.1.call-update) | async-done | bytes 884752
  455.8 26.5 %reduce-scatter.7.cloned.1.call-done = bf16[192,768]{1,0:T(8,128)(2,1)} async-done(((bf16[768,768]{1,0:T(8,128)(2,1)}), bf16[192,768]{1,0:T(8,128)(2,1)}) %reduce-scatter.7.cloned.1.call-update) | async-done | bytes 294928 | tf_op jit(solution)/shard_map/reduce_scatter | solution.py:236
  482.4 50.4 %reduce-scatter.11.cloned.1.call-done = bf16[768,768]{1,0:T(8,128)(2,1)} async-done(((bf16[3072,768]{1,0:T(8,128)(2,1)}), bf16[768,768]{1,0:T(8,128)(2,1)}) %reduce-scatter.11.cloned.1.call-update) | async-done | bytes 1179664 | tf_op jit(solution)/shard_map/reduce_scatter | solution.py:254
  532.8 50.5 %reduce-scatter.9.cloned.1.call-done = bf16[192,3072]{1,0:T(8,128)(2,1)} async-done(((bf16[768,3072]{1,0:T(8,128)(2,1)}), bf16[192,3072]{1,0:T(8,128)(2,1)}) %reduce-scatter.9.cloned.1.call-update) | async-done | bytes 1179664 | tf_op jit(solution)/shard_map/reduce_scatter | solution.py:248
  591.2 7.9 %convert_element_type.183 = f32[1024,2304]{0,1:T(8,128)} convert(bf16[1024,2304]{0,1:T(8,128)(2,1)} %copy-done.9) | non-fusion elementwise | flops 2359296 | bytes 14155776 | tf_op jit(solution)/shard_map/convert_element_type | solution.py:220
  599.1 7.9 %add_convert_fusion.1 = bf16[1024,768]{0,1:T(8,128)(2,1)} fusion(bf16[768,2304]{1,0:T(8,128)(2,1)S(1)} %copy-done, bf16[1024,2304]{0,1:T(8,128)(2,1)} %copy-done.9, f32[1024]{0:T(1024)S(1)} %broadcast_multiply_fusion.3, f32[1024]{0:T(1024)S(1)} %copy-done.29, f32[1024,768]{0,1:T(8,128)S(1)} %copy-done.4, f32[1024]{0:T(1024)S(1)} %copy-done.27, ...), kind=kOutput, calls=%fused_computation.68 | convolution fusion | flops 3633315840 | bytes 14570496 | tf_op jit(solution)/shard_map/dot_general | solution.py:74
  612.8 12.2 %all-reduce.10 = (bf16[1536]{0:T(1024)(128)(2,1)}, bf16[768]{0:T(1024)(128)(2,1)}, bf16[768]{0:T(1024)(128)(2,1)}, bf16[768]{0:T(1024)(128)(2,1)}, bf16[3072]{0:...) all-reduce(bf16[1536]{0:T(1024)(128)(2,1)S(1)} %pad_maximum_fusion., ...), channel_id=3, replica_groups=mesh['seq'=4,'batch'=8] {'seq'}, use_global_device_ids=true, to_apply=%region_19.20.clone | all-reduce | flops 9216 | bytes 36864
  634.1 22.0 %all-reduce.8 = (bf16[384]{0:T(512)(128)(2,1)S(1)}, bf16[192]{0:T(256)(128)(2,1)}, bf16[192]{0:T(256)(128)(2,1)}, bf16[192]{0:T(256)(128)(2,1)}, bf16[768]{0:T(1...) all-reduce(bf16[384]{0:T(512)(128)(2,1)S(1)} %dynamic-slice.1, ...), channel_id=1, replica_groups=mesh['seq'=4,'batch'=8] {'batch'}, use_global_device_ids=true, to_apply=%region_20.21 | all-reduce | flops 2304 | bytes 9216 | tf_op jit(solution)/shard_map/psum | solution.py:269
  664.6 71.6 %all-reduce.13.cloned.1.call-done = (bf16[192,2304]{0,1:T(8,128)(2,1)}, bf16[192,768]{1,0:T(8,128)(2,1)}, bf16[192,3072]{1,0:T(8,128)(2,1)}, bf16[768,768]{1,0:T(8,128)(2,1)}) async-done(((bf16[192,2304]{0,1:T(8,128)(2,1)}, bf16[192,768]{1,0:T(8,128)(2,1)}, bf16[192,3072]{1,0:T(8,128)(2,1)}, bf16[768,768]{1,0:T(8,128)(2,1)}), (bf16[192,2304]{0,1:T(8,128)(2,1)}, bf16[192,768]{1,0:T(8,128)(2,1)}, ...) | async-done | bytes 3538960 | tf_op jit(solution)/shard_map/psum | solution.py:268
  (253 shorter events, 234.6 us)
Async XLA Ops:
  7.2 30.9 %copy-start = (bf16[768,2304]{1,0:T(8,128)(2,1)S(1)}, bf16[768,2304]{1,0:T(8,128)(2,1)}, u32[]{:S(2)}) copy-start(bf16[768,2304]{1,0:T(8,128)(2,1)} %param.21) | copy-start | bytes 10616836
  16.4 105.4 %all-to-all-start = ((s32[32,32,1]{1,2,0:T(1,128)}), s32[32,32,1]{1,2,0:T(1,128)S(1)}, u32[]{:S(2)}, u32[]{:S(2)}) async-start(s32[32,32,1]{1,2,0:T(1,128)} %all_to_all.22), calls=%async_computation | async-start | bytes 32768 | tf_op jit(solution)/shard_map/all_to_all | solution.py:159
  72.0 11.1 %copy-start.11 = (bf16[12,2,512,64]{2,3,1,0:T(8,128)(2,1)}, bf16[12,2,512,64]{2,3,1,0:T(8,128)(2,1)S(1)}, u32[]{:S(2)}) copy-start(bf16[12,2,512,64]{2,3,1,0:T(8,128)(2,1)S(1)} %get-tuple-element.119) | copy-start | bytes 4718596
  72.0 21.2 %copy-start.13 = (bf16[12,2,512,64]{2,3,1,0:T(8,128)(2,1)}, bf16[12,2,512,64]{2,3,1,0:T(8,128)(2,1)S(1)}, u32[]{:S(2)}) copy-start(bf16[12,2,512,64]{2,3,1,0:T(8,128)(2,1)S(1)} %get-tuple-element.120) | copy-start | bytes 4718596
  83.1 10.2 %copy-start.24 = (f32[12,2,512]{2,1,0:T(2,128)}, f32[12,2,512]{2,1,0:T(2,128)S(1)}, u32[]{:S(2)}) copy-start(f32[12,2,512]{2,1,0:T(2,128)S(1)} %get-tuple-element.125) | copy-start | bytes 147460
  93.2 11.1 %copy-start.25 = (f32[12,2,512]{2,1,0:T(2,128)}, f32[12,2,512]{2,1,0:T(2,128)S(1)}, u32[]{:S(2)}) copy-start(f32[12,2,512]{2,1,0:T(2,128)S(1)} %fusion) | copy-start | bytes 147460
  121.8 44.8 %all-to-all-start.1 = ((bf16[32,32,768]{2,1,0:T(8,128)(2,1)}), bf16[32,32,768]{2,1,0:T(8,128)(2,1)}, u32[]{:S(2)}, u32[]{:S(2)}) async-start(bf16[32,32,768]{2,1,0:T(8,128)(2,1)} %bitcast.103), calls=%async_computation.1 | async-start | bytes 3145728 | tf_op jit(solution)/shard_map/all_to_all | solution.py:158
  176.2 30.5 %copy-start.22 = (bf16[896,768]{0,1:T(8,128)(2,1)S(1)}, bf16[896,768]{0,1:T(8,128)(2,1)}, u32[]{:S(2)}) copy-start(bf16[896,768]{0,1:T(8,128)(2,1)} %copy.117) | copy-start | bytes 4128772
  176.2 30.5 %copy-start.56 = (f32[768]{0:T(1024)S(1)}, f32[768]{0:T(1024)}, u32[]{:S(2)}) copy-start(f32[768]{0:T(1024)} %param.30) | copy-start | bytes 9220
  206.7 9.0 %copy-start.58 = (bf16[896,3072]{1,0:T(8,128)(2,1)}, bf16[896,3072]{1,0:T(8,128)(2,1)S(1)}, u32[]{:S(2)}) copy-start(bf16[896,3072]{1,0:T(8,128)(2,1)S(1)} %get-tuple-element.129) | copy-start | bytes 16515076
  206.7 9.3 %copy-start.33 = (f32[768]{0:T(1024)S(1)}, f32[768]{0:T(1024)}, u32[]{:S(2)}) copy-start(f32[768]{0:T(1024)} %param.31) | copy-start | bytes 9220
  206.7 9.3 %copy-start.50 = (f32[768]{0:T(1024)S(1)}, f32[768]{0:T(1024)}, u32[]{:S(2)}) copy-start(f32[768]{0:T(1024)} %param.32) | copy-start | bytes 9220
  220.0 15.8 %slice-start.2 = ((s8[4718592]{0:T(1024)(128)(4,1)}), s8[4194304]{0:T(1024)(128)(4,1)S(1)}, s32[]{:S(2)}) async-start(s8[4718592]{0:T(1024)(128)(4,1)} %bitcast.125), calls=%async_computation.14 | async-start | bytes 8388608
  221.8 11.6 %copy-start.21 = (bf16[896,768]{0,1:T(8,128)(2,1)}, bf16[896,768]{0,1:T(8,128)(2,1)S(1)}, u32[]{:S(2)}) copy-start(bf16[896,768]{0,1:T(8,128)(2,1)S(1)} %get-tuple-element.99) | copy-start | bytes 4128772
  221.8 14.0 %slice-start.3 = ((s8[4718592]{0:T(1024)(128)(4,1)}), s8[524288]{0:T(1024)(128)(4,1)S(1)}, s32[]{:S(2)}) async-start(s8[4718592]{0:T(1024)(128)(4,1)} %bitcast.125), calls=%async_computation.15 | async-start | bytes 1048576
  235.8 9.5 %copy-start.37 = (s32[1024]{0:T(1024)S(1)}, s32[1024]{0:T(1024)}, u32[]{:S(2)}) copy-start(s32[1024]{0:T(1024)} %broadcast_clamp_fusion) | copy-start | bytes 12292
  252.4 44.8 %copy-start.36 = (s32[1024]{0:T(1024)S(1)}, s32[1024]{0:T(1024)}, u32[]{:S(2)}) copy-start(s32[1024]{0:T(1024)} %get-tuple-element.113) | copy-start | bytes 12292
  254.9 42.3 %all-to-all-start.2 = ((bf16[32,32,768]{2,1,0:T(8,128)(2,1)}), bf16[32,32,768]{2,1,0:T(8,128)(2,1)}, u32[]{:S(2)}, u32[]{:S(2)}) async-start(bf16[32,32,768]{2,1,0:T(8,128)(2,1)} %select_select_fusion.1), calls=%async_computation.2 | async-start | bytes 3145728 | tf_op jit(solution)/shard_map/all_to_all | solution.py:183
  258.3 195.0 %reduce-scatter.13.cloned.1.call-start = ((), (), s32[]{:S(2)}) async-start(), calls=%async_computation.10 | async-start | bytes 4423680
  356.1 21.8 %copy-start.12 = (bf16[12,2,512,64]{2,3,1,0:T(8,128)(2,1)S(1)}, bf16[12,2,512,64]{2,3,1,0:T(8,128)(2,1)}, u32[]{:S(2)}) copy-start(bf16[12,2,512,64]{2,3,1,0:T(8,128)(2,1)} %copy-done.11) | copy-start | bytes 4718596
  415.2 67.2 %reduce-scatter.7.cloned.1.call-start = ((), (), s32[]{:S(2)}) async-start(), calls=%async_computation.7 | async-start | bytes 1474560 | tf_op jit(solution)/shard_map/reduce_scatter | solution.py:236
  419.6 113.2 %reduce-scatter.11.cloned.1.call-start = ((), (), s32[]{:S(2)}) async-start(), calls=%async_computation.9 | async-start | bytes 5898240 | tf_op jit(solution)/shard_map/reduce_scatter | solution.py:254
  429.5 153.7 %reduce-scatter.9.cloned.1.call-start = ((), (), s32[]{:S(2)}) async-start(), calls=%async_computation.8 | async-start | bytes 5898240 | tf_op jit(solution)/shard_map/reduce_scatter | solution.py:248
  439.1 297.1 %all-reduce.13.cloned.1.call-start = ((), (), s32[]{:S(2)}) async-start(), calls=%async_computation.11 | async-start | bytes 7667712 | tf_op jit(solution)/shard_map/psum | solution.py:268
  (47 other events, 163.7 us)
Sparse Core Ops, SparseCore 0:
  415.3 37.9 reduce-scatter.12
  456.6 25.7 reduce-scatter.6
  484.9 47.8 reduce-scatter.10
  535.3 47.8 reduce-scatter.8
  587.7 148.5 all-reduce.12
where the time goes:
time: 763 us; the launch traced here: 752 us
  waiting for transfers between devices  280 us (37%)
  matrix products  174 us (23%)
  local copies, waits for them, and re-layouts  133 us (17%)
  other arithmetic  96.9 us (13%)
  blocking collectives  34.2 us (4%)
  between operations  17.7 us (2%)
  starting transfers between devices  16.9 us (2%)
    psum x1, waiting for transfers between devices, body(): lax.psum(shares[0].astype(jnp.bfloat16), 'batch').astype(jnp.float32)  71.6 us
    reduce_scatter x1, waiting for transfers between devices, body(): lax.psum_scatter(g_w_in.astype(jnp.bfloat16), 'seq', scatter_dimension=0,...  50.5 us
    reduce_scatter x1, waiting for transfers between devices, body(): lax.psum_scatter(g_w_down.astype(jnp.bfloat16), 'seq', scatter_dimension=...  50.4 us
    unnamed x148, local copies, waits for them, and re-layouts  46.7 us
    all_to_all x1, waiting for transfers between devices, body(): lax.all_to_all(g_back, ('seq', 'batch'), split_axis=0, concat_axis=0, til...  37.3 us
    dot_general x1, matrix products, body(): pre_act = jnp.dot(moved, w_in, preferred_element_type=jnp.float32) + in_bias  30.5 us
    all_to_all x1, waiting for transfers between devices, body(): lax.all_to_all(outgoing, ('seq', 'batch'), split_axis=0, concat_axis=0, t...  29.4 us
    dot_general x4, matrix products, contract_rows(): lax.dot_general(left_op, right_op, (((0,), (0,)), ((), ())), preferred_el...  29.2 us
  transfers between devices with their start and end apart: 8, of which 7 were waited for; matrix products, arithmetic and copies ran while one was open for 23% of the time, Pallas kernels for 0%

commit v1 on v0

v1 whole, which is shorter than its diff:
```python
import functools

import jax
import jax.numpy as jnp
from jax import lax
from jax.experimental import pallas as pl
from jax.experimental.pallas import tpu as pltpu
from jax.sharding import PartitionSpec as P

EPS = 1e-05
BIG = 1e30
BF = jnp.bfloat16
F32 = jnp.float32
I32 = jnp.int32
MIB = 1 << 20

NN = (((1,), (0,)), ((), ()))
NT = (((1,), (1,)), ((), ()))
TN = (((0,), (0,)), ((), ()))


def mm(left_op, right_op, dims):
    return lax.dot_general(left_op, right_op, dims, preferred_element_type=F32)


def sds(shape, dtype):
    return jax.ShapeDtypeStruct(shape, dtype)


def whole_block(shape):
    zeros = (0,) * len(shape)
    return pl.BlockSpec(shape, lambda *_: zeros)


def smem():
    return pl.BlockSpec(memory_space=pltpu.SMEM)


class Chain:
    def __init__(self):
        self.last = None

    def link(self, outs):
        flat = jax.tree.leaves(outs)
        self.last = min(flat, key=lambda a: a.size * a.dtype.itemsize)


def call(chain, body, name, *, grid, in_specs, out_specs, out_shape, scratch=(), prefetch=0,
         aliases=None, vmem=56):
    count = prefetch + len(in_specs)
    before = [] if chain.last is None else [chain.last]

    def ordered(*refs):
        body(*refs[:count], *refs[count + len(before) :])

    kernel = pl.pallas_call(
        ordered,
        name=name,
        grid_spec=pltpu.PrefetchScalarGridSpec(
            num_scalar_prefetch=prefetch,
            grid=grid,
            in_specs=list(in_specs) + [pl.BlockSpec(memory_space=pl.ANY)] * len(before),
            out_specs=out_specs,
            scratch_shapes=list(scratch),
        ),
        out_shape=out_shape,
        input_output_aliases=aliases or {},
        compiler_params=pltpu.CompilerParams(
            vmem_limit_bytes=vmem * MIB, dimension_semantics=("arbitrary",) * len(grid)
        ),
        cost_estimate=pl.CostEstimate(flops=1, bytes_accessed=1, transcendentals=0),
    )

    def run(*args):
        outs = kernel(*args, *before)
        chain.link(outs)
        return outs

    return run


def slot_of(rel):
    return jnp.where(rel == 0, 3, jnp.where(rel == 3, 0, rel))


def floor_div(values, divisor):
    return jnp.floor((values.astype(F32) + 0.5) * (1.0 / divisor)).astype(I32)


def route_kernel(ffn_rows, capacity, place_ref, slot_ref, target_ref):
    devices = target_ref.shape[0]
    rows = place_ref.shape[1]
    place = place_ref[...]
    live = place >= 0
    dev = jnp.where(live, floor_div(place, ffn_rows), -1)
    local = place - dev * ffn_rows
    hit = lax.broadcasted_iota(I32, (devices, rows), 0) == dev
    onehot = hit.astype(F32)
    upper = (
        lax.broadcasted_iota(I32, (rows, rows), 0) <= lax.broadcasted_iota(I32, (rows, rows), 1)
    ).astype(F32).astype(BF)
    running = mm(onehot.astype(BF), upper, NN)
    rank = (jnp.sum(running * onehot, axis=0, keepdims=True) - 1.0).astype(I32)
    slot_ref[...] = jnp.where(live, dev * capacity + rank, devices * capacity)
    ranked = (lax.broadcasted_iota(I32, (capacity, rows), 0) == rank).astype(F32).astype(BF)
    high = (local >> 5).astype(F32)
    low = (local & 31).astype(F32)
    filled = mm(onehot.astype(BF), ranked, NT)
    high_at = mm((onehot * high).astype(BF), ranked, NT)
    low_at = mm((onehot * low).astype(BF), ranked, NT)
    target = (high_at * 32.0 + low_at).astype(I32)
    target_ref[...] = jnp.where(filled > 0.5, target, ffn_rows)


def expand_targets(target, capacity):
    devices = target.shape[0]
    slots = devices * capacity
    lane = lax.broadcasted_iota(I32, (capacity, slots), 1)
    lane_dev = floor_div(lane, capacity)
    spread = ((lane - lane_dev * capacity) == lax.broadcasted_iota(I32, (capacity, slots), 0)).astype(
        F32
    ).astype(BF)
    high = mm((target >> 5).astype(F32).astype(BF), spread, NN)
    low = mm((target & 31).astype(F32).astype(BF), spread, NN)
    wide = high * 32.0 + low
    own_dev = floor_div(lax.broadcasted_iota(I32, (devices, slots), 1), capacity)
    own = own_dev == lax.broadcasted_iota(I32, (devices, slots), 0)
    return jnp.sum(jnp.where(own, wide, 0.0), axis=0, keepdims=True).astype(I32)


def onehot_rows(row_index, row_count):
    lanes = row_index.shape[1]
    return (lax.broadcasted_iota(I32, (row_count, lanes), 0) == row_index).astype(F32).astype(BF)


def onehot_cols(row_index, col_count):
    rows = row_index.shape[1]
    column = jnp.broadcast_to(row_index.astype(F32), (128, rows)).T[:, :1].astype(I32)
    return (lax.broadcasted_iota(I32, (rows, col_count), 1) == column).astype(F32).astype(BF)


def gather_kernel(capacity, target_ref, cot_ref, out_ref, row_ref):
    row = expand_targets(target_ref[...], capacity)
    row_ref[...] = row
    chosen = onehot_cols(row, cot_ref.shape[0])
    out_ref[...] = mm(chosen, cot_ref[...], NN).astype(BF)


def place_kernel(row_ref, in_ref, out_ref):
    chosen = onehot_rows(row_ref[...], out_ref.shape[0])
    out_ref[...] = mm(chosen, in_ref[...], NN).astype(BF)


def norm_rows(values):
    center = values - jnp.mean(values, axis=-1, keepdims=True)
    inverse = lax.rsqrt(jnp.mean(center * center, axis=-1, keepdims=True) + EPS)
    return center * inverse, inverse


def attend_heads(
    head_base, heads, len_ref, swap_ref, x_ref, wq_ref, wk_ref, wv_ref, bq, bv,
    q_ref, k_ref, v_ref, ctx_ref, soft_ref, linv_ref,
):
    rows = x_ref.shape[0]
    half = rows // 2
    quarter = rows // 4
    cols = q_ref.shape[1]
    x = x_ref[...]
    q_ref[...] = (mm(x, wq_ref[...], NN) + bq).astype(BF)
    k_ref[...] = mm(x, wk_ref[...], NN).astype(BF)
    v_ref[...] = (mm(x, wv_ref[...], NN) + bv).astype(BF)
    head_size = cols // heads
    scale = head_size ** (-0.5)
    len0, len1 = len_ref[0, 0], len_ref[0, 1]
    is_long = len1 == 0
    lane = lax.broadcasted_iota(I32, (1, 128), 1)
    row = lax.broadcasted_iota(I32, (half, 1), 0)
    row_quarter = (row >= quarter).astype(I32)
    per_pair = 128 // head_size
    for pair in range(heads // per_pair):
        cut = slice(pair * 128, pair * 128 + 128)
        for b in range(2):
            q_rows = slice(b * half, (b + 1) * half)
            q_blk = q_ref[q_rows, cut] * jnp.asarray(scale, BF)
            out_blk = linv_blk = None
            for sub in range(per_pair):
                h = pair * per_pair + sub
                swapped = swap_ref[head_base + h] == 1
                cross = jnp.logical_and(is_long, swapped)
                kb = jnp.where(cross, 1 - b, b)
                limit = jnp.where(is_long, len0 - kb * half, jnp.where(kb == 0, len0, len1))
                mine = jnp.logical_and(lane >= sub * head_size, lane < (sub + 1) * head_size)
                spare = ((sub + 1) % per_pair) * head_size
                key_rows = pl.ds(pl.multiple_of(kb * half, half), half)
                k_one = jnp.where(mine, k_ref[key_rows, cut].astype(F32), 0.0)
                q_one = jnp.where(mine, q_blk.astype(F32), 0.0)
                for part in range(2):
                    other = jnp.where(swapped, 1 - part, part)
                    band_ok = jnp.logical_or(is_long, row_quarter == other)
                    bias = jnp.where(jnp.logical_and(band_ok, row < limit), 0.0, -BIG)
                    at = lane == spare + part
                    k_one = jnp.where(at, bias, k_one)
                    q_one = jnp.where(at, jnp.where(row_quarter == part, 1.0, 0.0), q_one)
                scores = mm(q_one.astype(BF), k_one.astype(BF), NT)
                top = jnp.max(scores, axis=1, keepdims=True)
                weights = jnp.exp(scores - top)
                linv = 1.0 / jnp.sum(weights, axis=1, keepdims=True)
                soft = weights.astype(BF)
                soft_ref[h, b] = soft
                mixed = mm(soft, v_ref[key_rows, cut], NN) * linv
                out_blk = mixed if out_blk is None else jnp.where(mine, mixed, out_blk)
                linv_blk = (
                    jnp.broadcast_to(linv, mixed.shape)
                    if linv_blk is None
                    else jnp.where(mine, linv, linv_blk)
                )
            ctx_ref[q_rows, cut] = out_blk.astype(BF)
            linv_ref[q_rows, cut] = linv_blk


def attend_first_kernel(
    heads, ids_ref, len_ref, swap_ref, x_ref, wq_ref, wk_ref, wv_ref, b_ref,
    q_ref, k_ref, v_ref, ctx_ref, soft_ref, linv_ref, xt_ref,
):
    cols = q_ref.shape[1]
    width = x_ref.shape[1]
    bq = b_ref[pl.ds(0, cols)].reshape(1, -1)
    bv = b_ref[pl.ds(width, cols)].reshape(1, -1)
    attend_heads(
        0, heads, len_ref, swap_ref, x_ref, wq_ref, wk_ref, wv_ref, bq, bv,
        q_ref, k_ref, v_ref, ctx_ref, soft_ref, linv_ref,
    )
    write_turned(x_ref[...], ids_ref[0], xt_ref)


def attend_rest_kernel(
    heads, ids_ref, len_ref, swap_ref, x_ref, wq_ref, wk_ref, wv_ref, b_ref, ctx0_ref, wo0_ref,
    wo_ref, ob_ref, gain_ref, shift_ref,
    q_ref, k_ref, v_ref, ctx_ref, soft_ref, linv_ref, first_ref, normed_ref, inv_ref, ctxt_ref,
    acc_ref, ctx_all,
):
    step = pl.program_id(0)
    cols = q_ref.shape[1]
    width = x_ref.shape[1]
    group = step + 1
    bq = b_ref[pl.ds(pl.multiple_of(group * cols, cols), cols)].reshape(1, -1)
    bv = b_ref[pl.ds(pl.multiple_of(width + group * cols, cols), cols)].reshape(1, -1)
    attend_heads(
        group * heads, heads, len_ref, swap_ref, x_ref, wq_ref, wk_ref, wv_ref, bq, bv,
        q_ref, k_ref, v_ref, ctx_ref, soft_ref, linv_ref,
    )
    ctx = ctx_ref[...]
    part_sum = mm(ctx, wo_ref[...], NN)
    ctx_all[:, pl.ds(pl.multiple_of(group * cols, cols), cols)] = ctx

    @pl.when(step == 0)
    def _():
        ctx_all[:, :cols] = ctx0_ref[...]
        acc_ref[...] = part_sum + mm(ctx0_ref[...], wo0_ref[...], NN)

    @pl.when(step > 0)
    def _():
        acc_ref[...] += part_sum

    @pl.when(step == pl.num_programs(0) - 1)
    def _():
        attn = acc_ref[...] + ob_ref[...].reshape(1, -1)
        normed, inverse = norm_rows(x_ref[...].astype(F32) + attn)
        normed_ref[...] = normed
        inv_ref[...] = inverse
        first = normed * gain_ref[...].reshape(1, -1) + shift_ref[...].reshape(1, -1)
        first_ref[...] = first.astype(BF)
        write_turned(ctx_all[...], ids_ref[0], ctxt_ref)


def write_turned(values, seq_id, out_ref):
    turned = values.T
    quarter = turned.shape[0] // 4
    for q in range(4):
        at = slot_of(jnp.bitwise_xor(seq_id, q))
        out_ref[pl.ds(pl.multiple_of(at * quarter, quarter), quarter), :] = turned[
            q * quarter : (q + 1) * quarter
        ]


def ffn_kernel(
    ids_ref, x_ref, wi_ref, bi_ref, wd_ref, bd_ref, gain_ref, shift_ref, slot_ref,
    hid_ref, slope_ref, normed_ref, inv_ref, out_ref, xt_ref, acc_ref,
):
    step = pl.program_id(0)
    steps = pl.num_programs(0)
    x = x_ref[...]
    blk = wi_ref.shape[1]
    pre = mm(x, wi_ref[...], NN) + bi_ref[pl.ds(pl.multiple_of(step * blk, blk), blk)].reshape(1, -1)
    phi = 0.5 * (1.0 + lax.erf(pre * 0.7071067811865476))
    hid = (pre * phi).astype(BF)
    hid_ref[...] = hid
    slope_ref[...] = (phi + pre * jnp.exp(-0.5 * pre * pre) * 0.3989422804014327).astype(BF)
    part_sum = mm(hid, wd_ref[...], NN)

    @pl.when(step == 0)
    def _():
        acc_ref[...] = part_sum
        write_turned(x, ids_ref[0], xt_ref)

    @pl.when(step > 0)
    def _():
        acc_ref[...] += part_sum

    @pl.when(step == steps - 1)
    def _():
        branch = acc_ref[...] + bd_ref[...].reshape(1, -1)
        normed, inverse = norm_rows(x_ref[...].astype(F32) + branch)
        normed_ref[...] = normed
        inv_ref[...] = inverse
        mixed = (normed * gain_ref[...].reshape(1, -1) + shift_ref[...].reshape(1, -1)).astype(BF)
        chosen = onehot_rows(slot_ref[...], out_ref.shape[0])
        out_ref[...] = mm(chosen, mixed, NN).astype(BF)


def norm_back(upstream, normed, inverse, gain):
    scaled = upstream * gain
    inner = (
        scaled
        - jnp.mean(scaled, axis=-1, keepdims=True)
        - normed * jnp.mean(scaled * normed, axis=-1, keepdims=True)
    )
    return inner * inverse


def put_rows(ref, *rows):
    for at, row in enumerate(rows):
        ref[at : at + 1, :] = row


def down_back_kernel(
    ids_ref, slot_ref, in_ref, normed_ref, inv_ref, gain_ref, wd_ref, slope_ref, hid_ref,
    pre_ref, branch_ref, vec_ref, act_ref, bias_ref, gw_ref,
):
    @pl.when(pl.program_id(0) == 0)
    def _():
        chosen = onehot_cols(slot_ref[...], in_ref.shape[0])
        cot = mm(chosen, in_ref[...], NN)
        normed = normed_ref[...]
        g_pre = norm_back(cot, normed, inv_ref[...], gain_ref[...].reshape(1, -1))
        pre_ref[...] = g_pre
        branch = g_pre.astype(BF)
        branch_ref[...] = branch
        put_rows(
            vec_ref,
            jnp.sum(cot * normed, axis=0, keepdims=True),
            jnp.sum(cot, axis=0, keepdims=True),
            jnp.sum(branch.astype(F32), axis=0, keepdims=True),
        )

    branch = branch_ref[...]
    g_act = (mm(branch, wd_ref[...], NT) * slope_ref[...].astype(F32)).astype(BF)
    act_ref[...] = g_act
    bias_ref[...] = jnp.sum(g_act.astype(F32), axis=0, keepdims=True)
    gw_ref[0] = mm(hid_ref[...], branch, TN).astype(BF)


def act_back_kernel(ids_ref, branch_ref, wd_ref, slope_ref, old_act, act_ref, bias_ref):
    g_act = (mm(branch_ref[...], wd_ref[...], NT) * slope_ref[...].astype(F32)).astype(BF)
    act_ref[...] = g_act
    bias_ref[...] = jnp.sum(g_act.astype(F32), axis=0, keepdims=True)


def down_grad_kernel(ids_ref, hid_ref, branch_ref, mate_ref, send_ref, keep_ref):
    own = mm(hid_ref[...], branch_ref[...], TN).astype(BF).astype(F32)
    total = (own + mate_ref[0].astype(F32)).astype(BF)

    @pl.when(pl.program_id(0) == 0)
    def _():
        send_ref[...] = total

    @pl.when(pl.program_id(0) == 1)
    def _():
        keep_ref[...] = total


def in_grad_kernel(xt_ref, act_ref, gw_ref):
    gw_ref[...] = mm(xt_ref[...], act_ref[...], NN).astype(BF)


def in_grad_add_kernel(xt_ref, act_ref, mate_ref, send_ref, keep_ref):
    own = mm(xt_ref[...], act_ref[...], NN).astype(BF).astype(F32)
    total = (own + mate_ref[...].astype(F32)).astype(BF)
    rows = send_ref.shape[0]
    send_ref[...] = total[:rows]
    keep_ref[...] = total[rows:]


def first_back_kernel(
    pre2_ref, act_ref, wi_ref, normed_ref, inv_ref, gain_ref, wo_ref, ctxt_ref, linv0_ref, linv_ref,
    pre1_ref, gctx_ref, vec_ref, gw_far, gw_near, acc_ref,
):
    step = pl.program_id(0)
    part_sum = mm(act_ref[...], wi_ref[...], NT)

    @pl.when(step == 0)
    def _():
        acc_ref[...] = part_sum

    @pl.when(step > 0)
    def _():
        acc_ref[...] += part_sum

    @pl.when(step == pl.num_programs(0) - 1)
    def _():
        g_first = (pre2_ref[...] + acc_ref[...]).astype(BF).astype(F32)
        normed = normed_ref[...]
        g_pre = norm_back(g_first, normed, inv_ref[...], gain_ref[...].reshape(1, -1))
        pre1_ref[...] = g_pre
        g_attn = g_pre.astype(BF)
        put_rows(
            vec_ref,
            jnp.sum(g_first * normed, axis=0, keepdims=True),
            jnp.sum(g_first, axis=0, keepdims=True),
            jnp.sum(g_attn.astype(F32), axis=0, keepdims=True),
        )
        g_ctx = mm(g_attn, wo_ref[...], NT)
        cols = linv0_ref.shape[1]
        gctx_ref[:, :cols] = (g_ctx[:, :cols] * linv0_ref[...]).astype(BF)
        gctx_ref[:, cols:] = (g_ctx[:, cols:] * linv_ref[...]).astype(BF)
        cut = ctxt_ref.shape[0] // 2
        gw_far[...] = mm(ctxt_ref[:cut], g_attn, NN).astype(BF)
        gw_near[...] = mm(ctxt_ref[cut:], g_attn, NN).astype(BF)


def attend_back_kernel(
    head_base, heads, len_ref, swap_ref, q_ref, k_ref, v_ref, soft_ref, gctx_ref, ctx_ref, xt_ref,
    proj_ref, vec_ref, gw_far, gw_near, gq_s, gk_s, gv_s,
):
    step = pl.program_id(0)
    rows = q_ref.shape[0]
    half = rows // 2
    head_size = 128 // heads
    scale = head_size ** (-0.5)
    is_long = len_ref[0, 1] == 0
    lane = lax.broadcasted_iota(I32, (1, 128), 1)
    for sub in range(heads):
        swapped = swap_ref[head_base + step * heads + sub] == 1
        cross = jnp.logical_and(is_long, swapped)
        mine = jnp.logical_and(lane >= sub * head_size, lane < (sub + 1) * head_size)
        for b in range(2):
            q_rows = slice(b * half, (b + 1) * half)
            kb = jnp.where(cross, 1 - b, b)
            key_rows = pl.ds(pl.multiple_of(kb * half, half), half)
            soft = soft_ref[sub, b]
            up = gctx_ref[q_rows, :]
            up_one = jnp.where(mine, up, jnp.zeros_like(up))
            inner = jnp.sum(
                up_one.astype(F32) * ctx_ref[q_rows, :].astype(F32), axis=1, keepdims=True
            )
            g_soft = mm(up_one, v_ref[key_rows, :], NT)
            g_scores = (soft.astype(F32) * (g_soft - inner)).astype(BF)
            g_q = mm(g_scores, k_ref[key_rows, :], NN) * scale
            g_k = mm(g_scores, q_ref[q_rows, :], TN) * scale
            g_v = mm(soft, up, TN)
            if sub == 0:
                gq_s[q_rows, :] = g_q
                gk_s[key_rows, :] = g_k
                gv_s[key_rows, :] = g_v
            else:
                gq_s[q_rows, :] = jnp.where(mine, g_q, gq_s[q_rows, :])
                gk_s[key_rows, :] = jnp.where(mine, g_k, gk_s[key_rows, :])
                gv_s[key_rows, :] = jnp.where(mine, g_v, gv_s[key_rows, :])
    cols = proj_ref.shape[1] // 3
    for at, ref in enumerate((gq_s, gk_s, gv_s)):
        low = ref[...].astype(BF)
        out_cols = pl.ds(pl.multiple_of(at * cols + step * 128, 128), 128)
        proj_ref[:, out_cols] = low
        vec_ref[:, out_cols] = jnp.sum(low.astype(F32), axis=0, keepdims=True)

    @pl.when(step == pl.num_programs(0) - 1)
    def _():
        proj = proj_ref[...]
        cut = xt_ref.shape[0] // 2
        gw_far[...] = mm(xt_ref[:cut], proj, NN).astype(BF)
        gw_near[...] = mm(xt_ref[cut:], proj, NN).astype(BF)


def input_grad_kernel(groups, *refs):
    proj_refs, (wq_ref, wk_ref, wv_ref, pre_ref, out_ref, acc_ref) = refs[:groups], refs[groups:]
    step = pl.program_id(0)
    cols = wq_ref.shape[1]

    @pl.when(step == 0)
    def _():
        acc_ref[...] = pre_ref[...]

    for at, proj_ref in enumerate(proj_refs):

        @pl.when(step == at)
        def _():
            acc_ref[...] += (
                mm(proj_ref[:, :cols], wq_ref[...], NT)
                + mm(proj_ref[:, cols : 2 * cols], wk_ref[...], NT)
                + mm(proj_ref[:, 2 * cols :], wv_ref[...], NT)
            )

    @pl.when(step == groups - 1)
    def _():
        out_ref[...] = acc_ref[...].astype(BF)


def vector_kernel(
    groups, ids_ref, vec2_ref, bias_a, bias_b, vec1_ref, *refs
):
    proj_refs, (far_ref, near_ref) = refs[:groups], refs[groups:]
    seq_id = ids_ref[0]
    far_ref[...] = jnp.zeros_like(far_ref)
    near_ref[...] = jnp.zeros_like(near_ref)
    width = vec1_ref.shape[1]
    cols = width // groups
    wide = jnp.concatenate(
        [ref[:, :cols] for ref in proj_refs] + [ref[:, 2 * cols :] for ref in proj_refs], axis=1
    )
    for q in range(4):
        rel = jnp.bitwise_xor(seq_id, q)
        odd = (rel & 1) == 1
        hid_q = slice(q * (bias_a.shape[1] // 4), (q + 1) * (bias_a.shape[1] // 4))
        rows = [jnp.where(odd, bias_a[:, hid_q], bias_b[:, hid_q])]
        qv = width // 2
        rows.append(wide[:, q * qv : (q + 1) * qv])
        part = slice(q * (width // 4), (q + 1) * (width // 4))
        for ref in (vec2_ref, vec1_ref):
            for at in range(3):
                rows.append(ref[at : at + 1, part])

        def store(out_ref, at):
            base = at * (out_ref.shape[0] // 2)
            for r, row in enumerate(rows):
                out_ref[base + r : base + r + 1, : row.shape[1]] = row.astype(BF)

        for at, want in enumerate((3, 1)):
            pl.when(rel == want)(functools.partial(store, far_ref, at))
        for at, want in enumerate((2, 0)):
            pl.when(rel == want)(functools.partial(store, near_ref, at))


def first_add_kernel(sizes, *refs):
    count = len(sizes)
    owns, mates = refs[:count], refs[count : 2 * count]
    send_ref, keep_ref = refs[2 * count :]
    base = 0
    for own, mate, rows in zip(owns, mates, sizes):
        if mate is None:
            total = own[...]
        else:
            total = (own[...].astype(F32) + mate[...].astype(F32)).astype(BF)
        send_ref[base : base + rows, :] = total[:rows]
        keep_ref[base : base + rows, :] = total[rows:]
        base += rows


def split_cols_kernel(ids_ref, keep_ref, got_ref, mine_ref, other_ref):
    total = (keep_ref[...].astype(F32) + got_ref[...].astype(F32)).astype(BF)
    half = mine_ref.shape[1]
    second = (ids_ref[1] & 1) == 1
    left, right = total[:, :half], total[:, half:]
    mine_ref[...] = jnp.where(second, right, left)
    other_ref[...] = jnp.where(second, left, right)


def split_rows_kernel(ids_ref, keep_ref, got_ref, mine_ref, other_ref):
    half = mine_ref.shape[0]
    bit = (ids_ref[1] >> 1) & 1

    def part(at):
        rows = pl.ds(pl.multiple_of(at * half, half), half)
        return (keep_ref[rows, :].astype(F32) + got_ref[rows, :].astype(F32)).astype(BF)

    mine_ref[...] = part(bit)
    other_ref[...] = part(1 - bit)


def add_kernel(left_ref, right_ref, out_ref):
    out_ref[...] = (left_ref[...].astype(F32) + right_ref[...].astype(F32)).astype(BF)


def join_kernel(ids_ref, own_ref, near_ref, far_own_ref, far_near_ref, out_ref):
    half_rows, half_cols = own_ref.shape
    second = (ids_ref[1] & 1) == 1
    bit = (ids_ref[1] >> 1) & 1
    for rel, (mine, other) in enumerate(((own_ref, far_own_ref), (near_ref, far_near_ref))):
        at = jnp.bitwise_xor(bit, rel)
        rows = pl.ds(pl.multiple_of(at * half_rows, half_rows), half_rows)
        a, b = mine[...].astype(F32), other[...].astype(F32)
        out_ref[rows, :half_cols] = jnp.where(second, b, a)
        out_ref[rows, half_cols:] = jnp.where(second, a, b)


def join_into(ids_ref, refs, out_ref):
    own_ref, near_ref, far_own_ref, far_near_ref = refs
    half_rows, half_cols = own_ref.shape
    second = (ids_ref[1] & 1) == 1
    bit = (ids_ref[1] >> 1) & 1
    for rel, (mine, other) in enumerate(((own_ref, far_own_ref), (near_ref, far_near_ref))):
        at = jnp.bitwise_xor(bit, rel)
        rows = pl.ds(pl.multiple_of(at * half_rows, half_rows), half_rows)
        a, b = mine[...].astype(F32), other[...].astype(F32)
        out_ref[rows, :half_cols] = jnp.where(second, b, a)
        out_ref[rows, half_cols:] = jnp.where(second, a, b)


def join_kernel(ids_ref, own_ref, near_ref, far_own_ref, far_near_ref, out_ref):
    join_into(ids_ref, (own_ref, near_ref, far_own_ref, far_near_ref), out_ref)


def attend_join_kernel(groups, ids_ref, *refs):
    a_refs, b_refs = refs[:4], refs[4:8]
    gwq_ref, gwo_ref, qv_ref, hid_ref = refs[8:12]
    vec_refs, (a_all, b_all) = refs[12:18], refs[18:]
    join_into(ids_ref, a_refs, a_all)
    join_into(ids_ref, b_refs, b_all)
    part, width = gwo_ref.shape
    cols = width // groups
    gwo_ref[...] = a_all[:part, :]
    places = [(a_all, part)] + [(b_all, part * at) for at in range(groups - 1)]
    for g, (ref, base) in enumerate(places):
        for at in range(3):
            gwq_ref[:, at * width + g * cols : at * width + (g + 1) * cols] = ref[
                base : base + part, at * cols : (at + 1) * cols
            ]
    base = part * (groups - 1)
    hid_ref[...] = b_all[base, :]
    qv_ref[...] = b_all[base + 1, : qv_ref.shape[0]]
    for at, ref in enumerate(vec_refs):
        ref[...] = b_all[base + 2 + at, : ref.shape[0]]


def exchange(values, axis, mask):
    count = lax.axis_size(axis)
    return lax.ppermute(values, axis, [(i, i ^ mask) for i in range(count)])


def simple(chain, body, name, args, out_shape, prefetch=0, vmem=56, scratch=()):
    tensors = args[prefetch:]
    return call(
        chain,
        body,
        name,
        grid=(1,),
        in_specs=[whole_block(a.shape) for a in tensors],
        out_specs=[whole_block(o.shape) for o in out_shape],
        out_shape=out_shape,
        prefetch=prefetch,
        vmem=vmem,
        scratch=scratch,
    )(*args)


class Share:
    def __init__(self, chain, ids, name, send, keep):
        self.chain, self.ids, self.name = chain, ids, name
        self.keep, self.got = keep, exchange(send, "seq", 2)
        self.shape = keep.shape

    def halve(self, kernel, shape, label, mask):
        self.keep, other = simple(
            self.chain, kernel, self.name + label, (self.ids, self.keep, self.got),
            [sds(shape, BF)] * 2, 1,
        )
        self.got = exchange(other, "batch", mask)

    def step_y(self):
        rows, cols = self.shape
        self.halve(split_cols_kernel, (rows, cols // 2), "_y", 1)

    def step_z(self):
        rows, cols = self.shape
        self.halve(split_rows_kernel, (rows // 2, cols // 2), "_z", 2)

    def add(self, label):
        (self.keep,) = simple(
            self.chain, add_kernel, self.name + label, (self.keep, self.got),
            [sds(self.keep.shape, BF)],
        )

    def step_far(self):
        mask = 4
        while mask <= lax.axis_size("batch") // 2:
            self.add("_a")
            self.got = exchange(self.keep, "batch", mask)
            mask *= 2

    def step_back(self):
        self.add("_f")
        near = exchange(self.keep, "batch", 2)
        far_own = exchange(self.keep, "batch", 1)
        self.pieces = (self.keep, near, far_own, exchange(near, "batch", 1))

    def join(self):
        (whole,) = simple(
            self.chain, join_kernel, self.name + "_j", (self.ids, *self.pieces),
            [sds(self.shape, F32)], 1,
        )
        return whole


def body(
    hidden_in, seq_lengths, head_swap, place, w_qkv, qv_bias, w_out, out_bias, norm1_gain,
    norm1_bias, w_in, in_bias, w_down, down_bias, norm2_gain, norm2_bias, cotangent,
):
    rows, width = hidden_in.shape
    ff = w_in.shape[1]
    ffn_rows = cotangent.shape[0]
    devices = lax.axis_size(("seq", "batch"))
    capacity = (rows + devices - 1) // devices
    slots = devices * capacity
    head_count = head_swap.shape[0]
    head_size = width // head_count
    half = rows // 2
    cols = 256
    groups = width // cols
    heads = cols // head_size
    pair = 128 // head_size
    ids = jnp.stack([lax.axis_index("seq"), lax.axis_index("batch")]).astype(I32)
    chain = Chain()

    slot_row, out_target = simple(
        chain,
        functools.partial(route_kernel, ffn_rows, capacity),
        "route",
        (place.reshape(1, -1),),
        [sds((1, rows), I32), sds((devices, capacity), I32)],
    )
    in_target = lax.all_to_all(out_target, ("seq", "batch"), split_axis=0, concat_axis=0, tiled=True)

    low, wide = sds((rows, width), BF), sds((rows, width), F32)
    vec_spec = whole_block((width,))
    some = lambda count, dtype: sds((rows, count * cols), dtype)
    col = lambda base: pl.BlockSpec((width, cols), lambda g, *_: (0, base + g))
    out_col = pl.BlockSpec((rows, cols), lambda g, *_: (0, g))
    soft_spec = pl.BlockSpec((heads, 2, half, half), lambda g, *_: (g, 0, 0, 0))
    head_outs = [out_col] * 4 + [soft_spec, out_col]
    head_shapes = lambda count: [some(count, BF)] * 4 + [
        sds((count * heads, 2, half, half), BF), some(count, F32)
    ]
    head_args = (ids, seq_lengths, head_swap, hidden_in, w_qkv, w_qkv, w_qkv, qv_bias)
    head_specs = lambda first: [
        smem(), smem(), whole_block((rows, width)), col(first), col(groups + first),
        col(2 * groups + first), whole_block((2 * width,)),
    ]
    *first_heads, x_turned = call(
        chain,
        functools.partial(attend_first_kernel, heads),
        "attend_first",
        grid=(1,),
        in_specs=head_specs(0),
        out_specs=head_outs + [whole_block((width, rows))],
        out_shape=head_shapes(1) + [sds((width, rows), BF)],
        prefetch=1,
    )(*head_args)
    context0, linv0 = first_heads[3], first_heads[5]
    cot_out, in_row = simple(
        chain,
        functools.partial(gather_kernel, capacity),
        "cot_gather",
        (in_target, cotangent),
        [sds((slots, width), BF), sds((1, slots), I32)],
    )
    cot_in = lax.all_to_all(cot_out, ("seq", "batch"), split_axis=0, concat_axis=0, tiled=True)
    *rest_heads, first_low, normed1, inv1, ctx_turned = call(
        chain,
        functools.partial(attend_rest_kernel, heads),
        "attend_rest",
        grid=(groups - 1,),
        in_specs=head_specs(1)
        + [
            whole_block((rows, cols)), pl.BlockSpec((cols, width), lambda g, *_: (0, 0)),
            pl.BlockSpec((cols, width), lambda g, *_: (1 + g, 0)), vec_spec, vec_spec, vec_spec,
        ],
        out_specs=head_outs
        + [
            whole_block((rows, width)), whole_block((rows, width)), whole_block((rows, 1)),
            whole_block((width, rows)),
        ],
        out_shape=head_shapes(groups - 1) + [low, wide, sds((rows, 1), F32), sds((width, rows), BF)],
        scratch=[pltpu.VMEM((rows, width), F32), pltpu.VMEM((rows, width), BF)],
        prefetch=1,
    )(*head_args, context0, w_out, w_out, out_bias, norm1_gain, norm1_bias)
    linv_rest = rest_heads[5]

    blk = ff // 4
    hid, slope, normed2, inv2, mixed_out, first_turned = call(
        chain,
        ffn_kernel,
        "ffn",
        grid=(4,),
        in_specs=[
            whole_block((rows, width)),
            pl.BlockSpec((width, blk), lambda j, *_: (0, j)),
            whole_block((ff,)),
            pl.BlockSpec((blk, width), lambda j, *_: (j, 0)),
            vec_spec, vec_spec, vec_spec, whole_block((1, rows)),
        ],
        out_specs=[
            pl.BlockSpec((rows, blk), lambda j, *_: (0, j)),
            pl.BlockSpec((rows, blk), lambda j, *_: (0, j)),
            whole_block((rows, width)), whole_block((rows, 1)), whole_block((slots, width)),
            whole_block((width, rows)),
        ],
        out_shape=[
            sds((rows, ff), BF), sds((rows, ff), BF), wide, sds((rows, 1), F32),
            sds((slots, width), BF), sds((width, rows), BF),
        ],
        scratch=[pltpu.VMEM((rows, width), F32)],
        prefetch=1,
    )(ids, first_low, w_in, in_bias, w_down, down_bias, norm2_gain, norm2_bias, slot_row)
    mixed_in = lax.all_to_all(mixed_out, ("seq", "batch"), split_axis=0, concat_axis=0, tiled=True)

    def quarter(first):
        def at(j, ids_ref):
            rel = jnp.where(j == 0, 3, 1) if first else jnp.where(j == 0, 2, 0)
            return jnp.bitwise_xor(ids_ref[0], rel)

        return at

    far, near = quarter(True), quarter(False)
    wd_spec = lambda at: pl.BlockSpec((blk, width), lambda j, i: (at(j, i), 0))
    act_spec = lambda at: pl.BlockSpec((rows, blk), lambda j, i: (0, at(j, i)))
    bias_spec = lambda at: pl.BlockSpec((1, blk), lambda j, i: (0, at(j, i)))
    gw_spec = pl.BlockSpec((1, blk, width), lambda j, *_: (j, 0, 0))
    g_pre2, g_branch, vec2, act_half, bias_a, gwd_far = call(
        chain,
        down_back_kernel,
        "down_back",
        grid=(2,),
        in_specs=[
            whole_block((1, rows)), whole_block((slots, width)), whole_block((rows, width)),
            whole_block((rows, 1)), vec_spec, wd_spec(far), act_spec(far), act_spec(far),
        ],
        out_specs=[
            whole_block((rows, width)), whole_block((rows, width)), whole_block((8, width)),
            act_spec(far), bias_spec(far), gw_spec,
        ],
        out_shape=[
            wide, low, sds((8, width), F32), sds((rows, ff), BF), sds((1, ff), F32),
            sds((2, blk, width), BF),
        ],
        prefetch=1,
    )(ids, slot_row, cot_in, normed2, inv2, norm2_gain, w_down, slope, hid)
    gwd_mate = exchange(gwd_far, "seq", 1)
    any_spec = pl.BlockSpec(memory_space=pl.ANY)
    g_act, bias_b = call(
        chain,
        act_back_kernel,
        "act_back",
        grid=(2,),
        in_specs=[whole_block((rows, width)), wd_spec(near), act_spec(near), any_spec],
        out_specs=[act_spec(near), bias_spec(near)],
        out_shape=[sds((rows, ff), BF), sds((1, ff), F32)],
        prefetch=1,
        aliases={4: 0},
    )(ids, g_branch, w_down, slope, act_half)
    share_spec = pl.BlockSpec((blk, width), lambda j, *_: (0, 0))
    send, keep = call(
        chain,
        down_grad_kernel,
        "down_grad",
        grid=(2,),
        in_specs=[act_spec(near), whole_block((rows, width)), gw_spec],
        out_specs=[share_spec, share_spec],
        out_shape=[sds((blk, width), BF)] * 2,
        prefetch=1,
    )(ids, hid, g_branch, gwd_mate)
    down_share = Share(chain, ids, "w_down", send, keep)

    part = width // 4
    xt_half = lambda at: pl.BlockSpec((2 * part, rows), lambda j: (at, 0))
    act_col = pl.BlockSpec((rows, blk), lambda j: (0, j))
    gwi_spec = pl.BlockSpec((2 * part, blk), lambda j: (0, j))
    gwi_far = call(
        chain,
        in_grad_kernel,
        "in_grad_far",
        grid=(4,),
        in_specs=[xt_half(0), act_col],
        out_specs=gwi_spec,
        out_shape=sds((2 * part, ff), BF),
    )(first_turned, g_act)
    gwi_mate = exchange(gwi_far, "seq", 1)

    g_pre1, g_ctx, vec1, gwo_far, gwo_near = call(
        chain,
        first_back_kernel,
        "first_back",
        grid=(4,),
        in_specs=[
            whole_block((rows, width)), act_col, pl.BlockSpec((width, blk), lambda j: (0, j)),
            whole_block((rows, width)), whole_block((rows, 1)), vec_spec,
            whole_block((width, width)), whole_block((width, rows)), whole_block(linv0.shape),
            whole_block(linv_rest.shape),
        ],
        out_specs=[
            whole_block((rows, width)), whole_block((rows, width)), whole_block((8, width)),
            whole_block((2 * part, width)), whole_block((2 * part, width)),
        ],
        out_shape=[
            wide, low, sds((8, width), F32), sds((2 * part, width), BF), sds((2 * part, width), BF),
        ],
        scratch=[pltpu.VMEM((rows, width), F32)],
    )(g_pre2, g_act, w_in, normed1, inv1, norm1_gain, w_out, ctx_turned, linv0, linv_rest)

    one_share = pl.BlockSpec((part, blk), lambda j: (0, j))
    send, keep = call(
        chain,
        in_grad_add_kernel,
        "in_grad_near",
        grid=(4,),
        in_specs=[xt_half(1), act_col, gwi_spec],
        out_specs=[one_share, one_share],
        out_shape=[sds((part, ff), BF)] * 2,
    )(first_turned, g_act, gwi_mate)
    in_share = Share(chain, ids, "w_in", send, keep)

    projs, vecs, fars, nears = [], [], [gwo_far], [gwo_near]
    steps = heads // pair

    def group_back(g):
        arrays, base = (first_heads, 0) if g == 0 else (rest_heads, g - 1)
        own_col = pl.BlockSpec((rows, 128), lambda p: (0, base * steps + p))
        all_col = pl.BlockSpec((rows, 128), lambda p: (0, g * steps + p))
        proj, vec, gw_far, gw_near = call(
            chain,
            functools.partial(attend_back_kernel, g * heads, pair),
            "attend_back",
            grid=(steps,),
            in_specs=[
                smem(), smem(), own_col, own_col, own_col,
                pl.BlockSpec((pair, 2, half, half), lambda p: (base * steps + p, 0, 0, 0)),
                all_col, own_col, whole_block((width, rows)),
            ],
            out_specs=[
                whole_block((rows, 3 * cols)), whole_block((1, 3 * cols)),
                whole_block((2 * part, 3 * cols)), whole_block((2 * part, 3 * cols)),
            ],
            out_shape=[
                sds((rows, 3 * cols), BF), sds((1, 3 * cols), F32),
                sds((2 * part, 3 * cols), BF), sds((2 * part, 3 * cols), BF),
            ],
            scratch=[pltpu.VMEM((rows, 128), F32)] * 3,
        )(
            seq_lengths, head_swap, *arrays[:3], arrays[4], g_ctx, arrays[3], x_turned
        )
        projs.append(proj)
        vecs.append(vec)
        fars.append(gw_far)
        nears.append(gw_near)

    def attention_share(first, last, name):
        own = nears[first:last]
        sizes = tuple(a.shape[0] // 2 for a in own)
        mates = [exchange(a, "seq", 1) for a in fars[first:last]]
        send, keep = simple(
            chain,
            functools.partial(first_add_kernel, sizes),
            name + "_x",
            (*own, *mates),
            [sds((sum(sizes), width), BF)] * 2,
        )
        return Share(chain, ids, name, send, keep)

    group_back(0)
    down_share.step_y()
    share_a = attention_share(0, 2, "attn_a")
    group_back(1)
    down_share.step_z()
    group_back(2)
    down_share.step_far()
    vec_far, vec_near = simple(
        chain,
        functools.partial(vector_kernel, groups),
        "vectors",
        (ids, vec2, bias_a, bias_b, vec1, *vecs),
        [sds((64, width), BF)] * 2,
        1,
    )
    fars.append(vec_far)
    nears.append(vec_near)
    in_share.step_y()
    share_b = attention_share(2, 5, "attn_b")
    down_share.step_back()
    in_share.step_z()
    share_a.step_y()
    (mixed,) = simple(
        chain, place_kernel, "mixed_place", (in_row, mixed_in), [sds((ffn_rows, width), BF)]
    )
    in_share.step_far()
    share_a.step_z()
    share_b.step_y()
    share_a.step_far()
    in_share.step_back()
    input_grad = call(
        chain,
        functools.partial(input_grad_kernel, groups),
        "input_grad",
        grid=(groups,),
        in_specs=[whole_block((rows, 3 * cols))] * groups
        + [
            pl.BlockSpec((width, cols), lambda g: (0, g)),
            pl.BlockSpec((width, cols), lambda g: (0, groups + g)),
            pl.BlockSpec((width, cols), lambda g: (0, 2 * groups + g)),
            whole_block((rows, width)),
        ],
        out_specs=whole_block((rows, width)),
        out_shape=low,
        scratch=[pltpu.VMEM((rows, width), F32)],
    )(*projs, w_qkv, w_qkv, w_qkv, g_pre1)
    share_b.step_z()
    share_a.step_back()
    share_b.step_far()
    g_w_down = down_share.join()
    g_w_in = in_share.join()
    share_b.step_back()
    one = lambda size: sds((size,), F32)
    g_w_qkv, g_w_out, g_qv, g_in_bias, g_n2g, g_n2b, g_down_bias, g_n1g, g_n1b, g_out_bias = simple(
        chain,
        functools.partial(attend_join_kernel, groups),
        "attn_join",
        (ids, *share_a.pieces, *share_b.pieces),
        [sds((part, 3 * width), F32), sds((part, width), F32), one(width // 2), one(width)]
        + [one(part)] * 6,
        1,
        scratch=[pltpu.VMEM(share_a.shape, F32), pltpu.VMEM(share_b.shape, F32)],
    )
    return (
        mixed, input_grad, g_w_qkv, g_qv, g_w_out, g_out_bias, g_n1g, g_n1b, g_w_in, g_in_bias,
        g_w_down, g_down_bias, g_n2g, g_n2b,
    )


def solution(mesh):
    rows_spec = P(("seq", "batch"), None)
    in_specs = (
        rows_spec, rows_spec, P(), P(("seq", "batch")), P(), P(), P(), P(), P(), P(), P(), P(),
        P(), P(), P(), P(), rows_spec,
    )
    out_specs = (
        rows_spec, rows_spec, P("seq", None), P("seq"), P("seq", None), P("seq"), P("seq"),
        P("seq"), P("seq", None), P("seq"), P("seq", None), P("seq"), P("seq"), P("seq"),
    )
    return jax.shard_map(body, mesh=mesh, in_specs=in_specs, out_specs=out_specs, check_vma=False)
```

time: 763 us -> 351 us (0.46)
  waiting for transfers between devices: 280 us -> 36.5 us
  Pallas kernels: 0 us -> 233 us
  matrix products: 174 us -> 0 us
  local copies, waits for them, and re-layouts: 133 us -> 20.8 us
  other arithmetic: 96.9 us -> 0.59 us
  starting transfers between devices: 16.9 us -> 51.7 us
  blocking collectives: 34.2 us -> 0 us
  between operations: 17.7 us -> 1.41 us
    pallas_call x0 -> x38, Pallas kernels: none -> 233 us  [run(): outs = kernel(*args, *before)]
    dot_general x19 -> x0, matrix products: 174 us -> none  [the longest x1 30.5 us: body(): pre_act = jnp.dot(moved, w_in, preferred_element_type=jnp.float32) + in_bias]
    reduce_scatter x3 -> x0, waiting for transfers between devices: 127 us -> none  [the longest x1 50.5 us: body(): lax.psum_scatter(g_w_in.astype(jnp.bfloat16), 'seq', scatter_dimension=0,...]
    psum x1 -> x0, waiting for transfers between devices: 71.6 us -> none  [body(): lax.psum(shares[0].astype(jnp.bfloat16), 'batch').astype(jnp.float32)]
    all_to_all x2, waiting for transfers between devices: 66.7 us -> 0.01 us  [the longest x1 0.01 us: body(): lax.all_to_all(cot_out, ('seq', 'batch'), split_axis=0, concat_axis=0, ti...]
    convert_element_type x14 -> x0, other arithmetic: 41.7 us -> none  [the longest x1 17.2 us: body(): g_scores = (soft_again * (g_soft - jnp.sum(soft_again * g_soft, axis=-1,...]
    ppermute x0 -> x35, waiting for transfers between devices: none -> 36.5 us  [exchange(): return lax.ppermute(values, axis, [(i, i ^ mask) for i in range(count)])]
    ppermute x0 -> x35, starting transfers between devices: none -> 32.4 us  [exchange(): return lax.ppermute(values, axis, [(i, i ^ mask) for i in range(count)])]
  transfers between devices with their start and end apart: 8 -> 38, of which waited for: 7 -> 9; matrix products, arithmetic and copies ran while one was open for 23% -> 0% of each run, Pallas kernels for 0% -> 56%
where the time goes in v1:
time: 351 us; the launch traced here: 344 us
  Pallas kernels  233 us (66%)
  starting transfers between devices  51.7 us (15%)
  waiting for transfers between devices  36.5 us (10%)
  local copies, waits for them, and re-layouts  20.8 us (6%)
    pallas_call x38, Pallas kernels, run(): outs = kernel(*args, *before)  233 us
    ppermute x35, waiting for transfers between devices, exchange(): return lax.ppermute(values, axis, [(i, i ^ mask) for i in range(count)])  36.5 us
    ppermute x35, starting transfers between devices, exchange(): return lax.ppermute(values, axis, [(i, i ^ mask) for i in range(count)])  32.4 us
    unnamed x92, local copies, waits for them, and re-layouts  20.8 us
    all_to_all x1, starting transfers between devices, body(): lax.all_to_all(out_target, ('seq', 'batch'), split_axis=0, concat_axis=0,...  7.3 us
  transfers between devices with their start and end apart: 38, of which 9 were waited for; matrix products, arithmetic and copies ran while one was open for 0% of the time, Pallas kernels for 56%

profile of v1, /device:TPU:0, one launch (start us, length us, event | category | flops | bytes accessed | tf_op | source)
XLA Modules:
  0.0 344.2 jit_solution(14311360474419026573)
XLA Ops:
  2.5 7.3 %all-to-all-start = ((s32[32,1,32]{2,1,0:T(1,128)}), s32[32,1,32]{2,1,0:T(1,128)S(1)}, u32[]{:S(2)}, u32[]{:S(2)}) async-start(s32[32,1,32]{2,1,0:T(1,128)} %bitcast.15), calls=%async_computation | async-start | bytes 32768 | tf_op jit(solution)/shard_map/all_to_all | solution.py:730
  10.4 10.4 %attend_first.1 = (bf16[1024,256]{1,0:T(8,128)(2,1)}, bf16[1024,256]{1,0:T(8,128)(2,1)}, bf16[1024,256]{1,0:T(8,128)(2,1)}, bf16[1024,256]{1,0:T(8,128)(2,1)}, b...) custom-call(s32[2]{0:T(128)} %pad_add_fusion.refs_0_, s32[1,2]{1,0:T(1,128)} %refs_0_.5, ...), custom_call_target="tpu_custom_call" | custom-call | flops 1 | bytes 1 | tf_op jit(solution)/shard_map/attend_first/pallas_call | solution.py:75
  21.4 4.8 %cot_gather.1 = (bf16[1024,768]{1,0:T(8,128)(2,1)}, s32[1,1024]{1,0:T(1,128)}) custom-call(s32[32,32]{1,0:T(8,128)} %bitcast.14, bf16[896,768]{1,0:T(8,128)(2,1)} %refs_1_.7, bf16[1024,256]{1,0:T(8,128)(2,1)} %get-tuple-element.104.refs_2_), custom_call_target="tpu_custom_call" | custom-call | flops 1 | bytes 1 | tf_op jit(solution)/shard_map/cot_gather/pallas_call | solution.py:75
  26.3 6.0 %all-to-all-start.2 = ((bf16[32,32,768]{2,1,0:T(8,128)(2,1)}), bf16[32,32,768]{2,1,0:T(8,128)(2,1)S(1)}, u32[]{:S(2)}, u32[]{:S(2)}) async-start(bf16[32,32,768]{2,1,0:T(8,128)(2,1)} %bitcast.13), calls=%async_computation.2 | async-start | bytes 3145728 | tf_op jit(solution)/shard_map/all_to_all | solution.py:765
  32.3 21.9 %attend_rest.1 = (bf16[1024,512]{1,0:T(8,128)(2,1)}, bf16[1024,512]{1,0:T(8,128)(2,1)}, bf16[1024,512]{1,0:T(8,128)(2,1)}, bf16[1024,512]{1,0:T(8,128)(2,1)}, bf...) custom-call(s32[2]{0:T(128)} %pad_add_fusion.refs_0_, ...), custom_call_target="tpu_custom_call" | custom-call | flops 1 | bytes 1 | tf_op jit(solution)/shard_map/attend_rest/pallas_call | solution.py:75
  54.3 24.9 %ffn.1 = (bf16[1024,3072]{1,0:T(8,128)(2,1)}, bf16[1024,3072]{1,0:T(8,128)(2,1)}, f32[1024,768]{1,0:T(8,128)}, f32[1024,1]{1,0:T(8,128)}, bf16[1024,768]{1,0:T(8,128)(2,1)}, /*index=5*/bf16[768,1024]{1,0:T(8,128)(2,1)}) custom-call(s32[2]{0:T(128)} %pad_add_fusion.refs_0_, bf16[1024,768]{1,0:T(8,128)(2,1)} %get-tuple-element.107.refs_1_, ...), custom_call_target="tpu_custom_call" | custom-call | flops 1 | bytes 1 | tf_op jit(solution)/shard_map/ffn/pallas_call | solution.py:75
  80.3 15.7 %down_back.1 = (f32[1024,768]{1,0:T(8,128)}, bf16[1024,768]{1,0:T(8,128)(2,1)}, f32[8,768]{1,0:T(8,128)}, bf16[1024,3072]{1,0:T(8,128)(2,1)}, f32[1,3072]{1,0:T(1,128)}, /*index=5*/bf16[2,768,768]{2,1,0:T(8,128)(2,1)}) custom-call(s32[2]{0:T(128)} %pad_add_fusion.refs_0_, s32[1,1024]{1,0:T(1,128)} %get-tuple-element.103.refs_8_.refs_1_, ...), custom_call_target="tpu_custom_call" | custom-call | flops 1 | bytes 1 | tf_op jit(solution)/shard_map/down_back/pallas_call | solution.py:75
  96.4 7.4 %act_back.1 = (bf16[1024,3072]{1,0:T(8,128)(2,1)}, f32[1,3072]{1,0:T(1,128)}) custom-call(s32[2]{0:T(128)} %pad_add_fusion.refs_0_, bf16[1024,768]{1,0:T(8,128)(2,1)} %get-tuple-element.116.refs_1_.refs_2_, bf16[3072,768]{1,0:T(8,128)(2,1)} %refs_2_.8, bf16[1024,3072]{1,0:T(8,128)(2,1)} %get-tuple-element.113.refs_7_.refs_3_, ...), custom_call_target="tpu_custom_call", output_to_operand_aliasing={{0}: (4, {})} | custom-call | flops 1 | bytes 1 | tf_op jit(solution)/shard_map/act_back/pallas_call | solution.py:75
  105.2 7.5 %down_grad.1 = (bf16[768,768]{1,0:T(8,128)(2,1)}, bf16[768,768]{1,0:T(8,128)(2,1)}) custom-call(s32[2]{0:T(128)} %pad_add_fusion.refs_0_, bf16[1024,3072]{1,0:T(8,128)(2,1)} %get-tuple-element.114.refs_8_.refs_1_, bf16[1024,768]{1,0:T(8,128)(2,1)} %get-tuple-element.116.refs_1_.refs_2_, bf16[2,768,768]{2,1,0:T(8,128)(2,1)} %copy-done.5, ...), custom_call_target="tpu_custom_call" | custom-call | flops 1 | bytes 1 | tf_op jit(solution)/shard_map/down_grad/pallas_call | solution.py:75
  112.7 6.5 %in_grad_far.1.refs_10_ = bf16[384,3072]{1,0:T(8,128)(2,1)} custom-call(bf16[768,1024]{1,0:T(8,128)(2,1)} %get-tuple-element.124.refs_0_, bf16[1024,3072]{1,0:T(8,128)(2,1)} %get-tuple-element.119.refs_1_, bf16[768,768]{1,0:T(8,128)(2,1)} %get-tuple-element.127.refs_2_), custom_call_target="tpu_custom_call" | custom-call | flops 1 | bytes 1 | tf_op jit(solution)/shard_map/in_grad_far/pallas_call | solution.py:75
  119.4 5.9 %all-to-all-start.1 = ((bf16[32,32,768]{2,1,0:T(8,128)(2,1)}), bf16[32,32,768]{2,1,0:T(8,128)(2,1)S(1)}, u32[]{:S(2)}, u32[]{:S(2)}) async-start(bf16[32,32,768]{2,1,0:T(8,128)(2,1)} %bitcast.6), calls=%async_computation.1 | async-start | bytes 3145728 | tf_op jit(solution)/shard_map/all_to_all | solution.py:813
  127.2 19.3 %first_back.1 = (f32[1024,768]{1,0:T(8,128)}, bf16[1024,768]{1,0:T(8,128)(2,1)}, f32[8,768]{1,0:T(8,128)}, bf16[384,768]{1,0:T(8,128)(2,1)}, bf16[384,768]{1,0:T(8,128)(2,1)}) custom-call(f32[1024,768]{1,0:T(8,128)} %get-tuple-element.115.refs_0_, bf16[1024,3072]{1,0:T(8,128)(2,1)} %get-tuple-element.119.refs_1_, bf16[768,3072]{1,0:T(8,128)(2,1)} %refs_2_.9, ...), custom_call_target="tpu_custom_call" | custom-call | flops 1 | bytes 1 | tf_op jit(solution)/shard_map/first_back/pallas_call | solution.py:75
  146.5 6.9 %in_grad_near.1 = (bf16[192,3072]{1,0:T(8,128)(2,1)}, bf16[192,3072]{1,0:T(8,128)(2,1)}) custom-call(bf16[768,1024]{1,0:T(8,128)(2,1)} %get-tuple-element.124.refs_0_, bf16[1024,3072]{1,0:T(8,128)(2,1)} %get-tuple-element.119.refs_1_, bf16[384,3072]{1,0:T(8,128)(2,1)} %collective-permute-done.1.refs_2_, f32[8,768]{1,0:T(8,128)} %get-tuple-element.134.refs_3_.refs_4_), custom_call_target="tpu_custom_call" | custom-call | flops 1 | bytes 1 | tf_op jit(solution)/shard_map/in_grad_near/pallas_call | solution.py:75
  153.7 11.7 %attend_back.3 = (bf16[1024,768]{1,0:T(8,128)(2,1)}, f32[1,768]{1,0:T(1,128)}, bf16[384,768]{1,0:T(8,128)(2,1)}, bf16[384,768]{1,0:T(8,128)(2,1)}) custom-call(s32[1,2]{1,0:T(1,128)} %refs_0_.5, s32[12]{0:T(128)} %refs_1_.11, bf16[1024,256]{1,0:T(8,128)(2,1)} %get-tuple-element.104.refs_2_, bf16[1024,256]{1,0:T(8,128)(2,1)} %get-tuple-element.129.refs_3_, ...), custom_call_target="tpu_custom_call" | custom-call | flops 1 | bytes 1 | tf_op jit(solution)/shard_map/attend_back/pallas_call | solution.py:75
  165.9 4.9 %collective-permute-done.4.refs_2_ = bf16[768,768]{1,0:T(8,128)(2,1)S(1)} collective-permute-done((bf16[768,768]{1,0:T(8,128)(2,1)S(1)}, bf16[768,768]{1,0:T(8,128)(2,1)S(1)}, u32[]{:S(2)}, u32[]{:S(2)}) %collective-permute-start.4) | collective-permute-done | bytes 1179680 | tf_op jit(solution)/shard_map/ppermute | solution.py:636
  180.8 12.0 %attend_back.4 = (bf16[1024,768]{1,0:T(8,128)(2,1)}, f32[1,768]{1,0:T(1,128)}, bf16[384,768]{1,0:T(8,128)(2,1)}, bf16[384,768]{1,0:T(8,128)(2,1)}) custom-call(s32[1,2]{1,0:T(1,128)} %refs_0_.5, s32[12]{0:T(128)} %refs_1_.11, bf16[1024,512]{1,0:T(8,128)(2,1)} %get-tuple-element.146.refs_2_, bf16[1024,512]{1,0:T(8,128)(2,1)} %get-tuple-element.147.refs_3_, ...), custom_call_target="tpu_custom_call" | custom-call | flops 1 | bytes 1 | tf_op jit(solution)/shard_map/attend_back/pallas_call | solution.py:75
  197.9 11.9 %attend_back.5 = (bf16[1024,768]{1,0:T(8,128)(2,1)}, f32[1,768]{1,0:T(1,128)}, bf16[384,768]{1,0:T(8,128)(2,1)}, bf16[384,768]{1,0:T(8,128)(2,1)}) custom-call(s32[1,2]{1,0:T(1,128)} %refs_0_.5, s32[12]{0:T(128)} %refs_1_.11, bf16[1024,512]{1,0:T(8,128)(2,1)} %get-tuple-element.146.refs_2_, bf16[1024,512]{1,0:T(8,128)(2,1)} %get-tuple-element.147.refs_3_, ...), custom_call_target="tpu_custom_call" | custom-call | flops 1 | bytes 1 | tf_op jit(solution)/shard_map/attend_back/pallas_call | solution.py:75
  230.4 8.4 %collective-permute-done.10.refs_1_ = bf16[384,384]{1,0:T(8,128)(2,1)S(1)} collective-permute-done((bf16[384,384]{1,0:T(8,128)(2,1)S(1)}, bf16[384,384]{1,0:T(8,128)(2,1)S(1)}, u32[]{:S(2)}, u32[]{:S(2)}) %collective-permute-start.10) | collective-permute-done | bytes 294944 | tf_op jit(solution)/shard_map/ppermute | solution.py:636
  251.6 4.1 %mixed_place.1.refs_2_ = bf16[896,768]{1,0:T(8,128)(2,1)} custom-call(s32[1,1024]{1,0:T(1,128)} %get-tuple-element.105.refs_14_.refs_0_, bf16[1024,768]{1,0:T(8,128)(2,1)} %bitcast.11, bf16[384,384]{1,0:T(8,128)(2,1)} %get-tuple-element.166.refs_2_.refs_1_), custom_call_target="tpu_custom_call" | custom-call | flops 1 | bytes 1 | tf_op jit(solution)/shard_map/mixed_place/pallas_call | solution.py:75
  270.5 5.2 %collective-permute-done.17.refs_1_ = bf16[192,384]{1,0:T(8,128)(2,1)S(1)} collective-permute-done((bf16[192,384]{1,0:T(8,128)(2,1)}, bf16[192,384]{1,0:T(8,128)(2,1)S(1)}, u32[]{:S(2)}, u32[]{:S(2)}) %collective-permute-start.17) | collective-permute-done | bytes 147488 | tf_op jit(solution)/shard_map/ppermute | solution.py:636
  282.1 9.4 %input_grad.1.refs_3_ = bf16[1024,768]{1,0:T(8,128)(2,1)} custom-call(bf16[1024,768]{1,0:T(8,128)(2,1)} %get-tuple-element.167.refs_0_, bf16[1024,768]{1,0:T(8,128)(2,1)} %get-tuple-element.168.refs_1_, bf16[1024,768]{1,0:T(8,128)(2,1)} %get-tuple-element.169.refs_2_, bf16[768,2304]{1,0:T(8,128)(2,1)} %refs_5_.11, bf16[768,2304]{1,0:T(8,128)(2,1)} %refs_5_.11, ...), custom_call_target="tpu_custom_call" | custom-call | flops 1 | bytes 1 | tf_op jit(solution)/shard_map/input_grad/pallas_call | solution.py:75
  306.3 5.2 %collective-permute-done.31.refs_4_ = bf16[384,384]{1,0:T(8,128)(2,1)S(1)} collective-permute-done((bf16[384,384]{1,0:T(8,128)(2,1)S(1)}, bf16[384,384]{1,0:T(8,128)(2,1)S(1)}, u32[]{:S(2)}, u32[]{:S(2)}) %collective-permute-start.31) | collective-permute-done | bytes 294944 | tf_op jit(solution)/shard_map/ppermute | solution.py:636
  332.7 4.5 %collective-permute-done.22.refs_3_ = bf16[192,384]{1,0:T(8,128)(2,1)S(1)} collective-permute-done((bf16[192,384]{1,0:T(8,128)(2,1)S(1)}, bf16[192,384]{1,0:T(8,128)(2,1)S(1)}, u32[]{:S(2)}, u32[]{:S(2)}) %collective-permute-start.22) | collective-permute-done | bytes 147488 | tf_op jit(solution)/shard_map/ppermute | solution.py:636
  340.1 3.7 %attn_join.1 = (f32[192,2304]{1,0:T(8,128)}, f32[192,768]{1,0:T(8,128)}, f32[384]{0:T(512)}, f32[768]{0:T(1024)}, f32[192]{0:T(256)}, /*index=5*/f32[192]{0:T(25...) custom-call(s32[2]{0:T(128)} %pad_add_fusion.refs_0_, bf16[192,384]{1,0:T(8,128)(2,1)} %attn_a_f.1.refs_2_.refs_1_, ...), custom_call_target="tpu_custom_call" | custom-call | flops 1 | bytes 1 | tf_op jit(solution)/shard_map/attn_join/pallas_call | solution.py:75
  (183 shorter events, 117.2 us)
Async XLA Ops:
  2.5 18.3 %all-to-all-start = ((s32[32,1,32]{2,1,0:T(1,128)}), s32[32,1,32]{2,1,0:T(1,128)S(1)}, u32[]{:S(2)}, u32[]{:S(2)}) async-start(s32[32,1,32]{2,1,0:T(1,128)} %bitcast.15), calls=%async_computation | async-start | bytes 32768 | tf_op jit(solution)/shard_map/all_to_all | solution.py:730
  26.3 52.9 %all-to-all-start.2 = ((bf16[32,32,768]{2,1,0:T(8,128)(2,1)}), bf16[32,32,768]{2,1,0:T(8,128)(2,1)S(1)}, u32[]{:S(2)}, u32[]{:S(2)}) async-start(bf16[32,32,768]{2,1,0:T(8,128)(2,1)} %bitcast.13), calls=%async_computation.2 | async-start | bytes 3145728 | tf_op jit(solution)/shard_map/all_to_all | solution.py:765
  119.2 27.2 %collective-permute-start.1 = (bf16[384,3072]{1,0:T(8,128)(2,1)}, bf16[384,3072]{1,0:T(8,128)(2,1)}, u32[]{:S(2)}, u32[]{:S(2)}) collective-permute-start(bf16[384,3072]{1,0:T(8,128)(2,1)} %in_grad_far.1.refs_10_), channel_id=1, source_target_pairs={{0,8},{8,0},{16,24},{24,16},{1,9},{9,1},{17,25},{25,17},{2,10},{10... | collective-permute-start | bytes 7077896 | tf_op jit(solution)/shard_map/ppermute | solution.py:636
  119.4 131.0 %all-to-all-start.1 = ((bf16[32,32,768]{2,1,0:T(8,128)(2,1)}), bf16[32,32,768]{2,1,0:T(8,128)(2,1)S(1)}, u32[]{:S(2)}, u32[]{:S(2)}) async-start(bf16[32,32,768]{2,1,0:T(8,128)(2,1)} %bitcast.6), calls=%async_computation.1 | async-start | bytes 3145728 | tf_op jit(solution)/shard_map/all_to_all | solution.py:813
  125.4 45.5 %collective-permute-start.4 = (bf16[768,768]{1,0:T(8,128)(2,1)S(1)}, bf16[768,768]{1,0:T(8,128)(2,1)S(1)}, u32[]{:S(2)}, u32[]{:S(2)}) collective-permute-start(bf16[768,768]{1,0:T(8,128)(2,1)S(1)} %copy-done.9), channel_id=1, source_target_pairs={{0,16},{8,24},{16,0},{24,8},{1,17},{9,25},{17,1},{25,9},{2,18},{10... | collective-permute-start | bytes 3538952 | tf_op jit(solution)/shard_map/ppermute | solution.py:636
  153.4 62.2 %collective-permute-start.6 = (bf16[192,3072]{1,0:T(8,128)(2,1)}, bf16[192,3072]{1,0:T(8,128)(2,1)S(1)}, u32[]{:S(2)}, u32[]{:S(2)}) collective-permute-start(bf16[192,3072]{1,0:T(8,128)(2,1)} %get-tuple-element.135.refs_9_), channel_id=1, source_target_pairs={{0,16},{8,24},{16,0},{24,8},{1,17},{9,25},{17,1},{25,9},{2,18},{10... | collective-permute-start | bytes 3538952 | tf_op jit(solution)/shard_map/ppermute | solution.py:636
  153.7 23.2 %collective-permute-start.2 = (bf16[384,768]{1,0:T(8,128)(2,1)S(1)}, bf16[384,768]{1,0:T(8,128)(2,1)S(1)}, u32[]{:S(2)}, u32[]{:S(2)}) collective-permute-start(bf16[384,768]{1,0:T(8,128)(2,1)S(1)} %copy-done.45), channel_id=1, source_target_pairs={{0,8},{8,0},{16,24},{24,16},{1,9},{9,1},{17,25},{25,17},{2,10},{10... | collective-permute-start | bytes 1769480 | tf_op jit(solution)/shard_map/ppermute | solution.py:636
  175.5 17.3 %collective-permute-start.7 = (bf16[768,384]{1,0:T(8,128)(2,1)}, bf16[768,384]{1,0:T(8,128)(2,1)S(1)}, u32[]{:S(2)}, u32[]{:S(2)}) collective-permute-start(bf16[768,384]{1,0:T(8,128)(2,1)} %get-tuple-element.152), channel_id=1, source_target_pairs={{0,1},{1,0},{2,3},{3,2},{4,5},{5,4},{6,7},{7,6},{8,9},{9,8},{10,11... | collective-permute-start | bytes 1769480 | tf_op jit(solution)/shard_map/ppermute | solution.py:636
  196.4 13.9 %collective-permute-start.8 = (bf16[384,384]{1,0:T(8,128)(2,1)}, bf16[384,384]{1,0:T(8,128)(2,1)S(1)}, u32[]{:S(2)}, u32[]{:S(2)}) collective-permute-start(bf16[384,384]{1,0:T(8,128)(2,1)} %get-tuple-element.155), channel_id=1, source_target_pairs={{0,2},{1,3},{2,0},{3,1},{4,6},{5,7},{6,4},{7,5},{8,10},{9,11},{10,... | collective-permute-start | bytes 884744 | tf_op jit(solution)/shard_map/ppermute | solution.py:636
  209.8 15.4 %collective-permute-start.11 = (bf16[384,768]{1,0:T(8,128)(2,1)S(1)}, bf16[384,768]{1,0:T(8,128)(2,1)S(1)}, u32[]{:S(2)}, u32[]{:S(2)}) collective-permute-start(bf16[384,768]{1,0:T(8,128)(2,1)S(1)} %copy-done.44), channel_id=1, source_target_pairs={{0,8},{8,0},{16,24},{24,16},{1,9},{9,1},{17,25},{25,17},{2,10},{10... | collective-permute-start | bytes 1769480 | tf_op jit(solution)/shard_map/ppermute | solution.py:636
  209.9 15.3 %collective-permute-start.12 = (bf16[384,768]{1,0:T(8,128)(2,1)}, bf16[384,768]{1,0:T(8,128)(2,1)S(1)}, u32[]{:S(2)}, u32[]{:S(2)}) collective-permute-start(bf16[384,768]{1,0:T(8,128)(2,1)} %get-tuple-element.163), channel_id=1, source_target_pairs={{0,8},{8,0},{16,24},{24,16},{1,9},{9,1},{17,25},{25,17},{2,10},{10... | collective-permute-start | bytes 1769480 | tf_op jit(solution)/shard_map/ppermute | solution.py:636
  220.3 21.0 %collective-permute-start.9 = (bf16[192,1536]{1,0:T(8,128)(2,1)}, bf16[192,1536]{1,0:T(8,128)(2,1)S(1)}, u32[]{:S(2)}, u32[]{:S(2)}) collective-permute-start(bf16[192,1536]{1,0:T(8,128)(2,1)} %get-tuple-element.158), channel_id=1, source_target_pairs={{0,1},{1,0},{2,3},{3,2},{4,5},{5,4},{6,7},{7,6},{8,9},{9,8},{10,11... | collective-permute-start | bytes 1769480 | tf_op jit(solution)/shard_map/ppermute | solution.py:636
  221.2 23.7 %collective-permute-start.5 = (bf16[384,768]{1,0:T(8,128)(2,1)S(1)}, bf16[384,768]{1,0:T(8,128)(2,1)S(1)}, u32[]{:S(2)}, u32[]{:S(2)}) collective-permute-start(bf16[384,768]{1,0:T(8,128)(2,1)S(1)} %copy-done.11), channel_id=1, source_target_pairs={{0,16},{8,24},{16,0},{24,8},{1,17},{9,25},{17,1},{25,9},{2,18},{10... | collective-permute-start | bytes 1769480 | tf_op jit(solution)/shard_map/ppermute | solution.py:636
  223.0 15.7 %collective-permute-start.10 = (bf16[384,384]{1,0:T(8,128)(2,1)S(1)}, bf16[384,384]{1,0:T(8,128)(2,1)S(1)}, u32[]{:S(2)}, u32[]{:S(2)}) collective-permute-start(bf16[384,384]{1,0:T(8,128)(2,1)S(1)} %copy-done.3), channel_id=1, source_target_pairs={{0,4},{1,5},{2,6},{3,7},{4,0},{5,1},{6,2},{7,3},{8,12},{9,13},{10,... | collective-permute-start | bytes 884744 | tf_op jit(solution)/shard_map/ppermute | solution.py:636
  229.1 35.4 %collective-permute-start.18 = (bf16[416,768]{1,0:T(8,128)(2,1)}, bf16[416,768]{1,0:T(8,128)(2,1)S(1)}, u32[]{:S(2)}, u32[]{:S(2)}) collective-permute-start(bf16[416,768]{1,0:T(8,128)(2,1)} %get-tuple-element.164.refs_2_), channel_id=1, source_target_pairs={{0,16},{8,24},{16,0},{24,8},{1,17},{9,25},{17,1},{25,9},{2,18},{10... | collective-permute-start | bytes 1916936 | tf_op jit(solution)/shard_map/ppermute | solution.py:636
  258.2 19.9 %collective-permute-start.15 = (bf16[96,1536]{1,0:T(8,128)(2,1)}, bf16[96,1536]{1,0:T(8,128)(2,1)S(1)}, u32[]{:S(2)}, u32[]{:S(2)}) collective-permute-start(bf16[96,1536]{1,0:T(8,128)(2,1)} %w_in_a.1.refs_3_.refs_0_), channel_id=1, source_target_pairs={{0,4},{1,5},{2,6},{3,7},{4,0},{5,1},{6,2},{7,3},{8,12},{9,13},{10,... | collective-permute-start | bytes 884744 | tf_op jit(solution)/shard_map/ppermute | solution.py:636
  268.3 23.2 %collective-permute-start.20 = (bf16[416,384]{1,0:T(8,128)(2,1)}, bf16[416,384]{1,0:T(8,128)(2,1)S(1)}, u32[]{:S(2)}, u32[]{:S(2)}) collective-permute-start(bf16[416,384]{1,0:T(8,128)(2,1)} %get-tuple-element.177), channel_id=1, source_target_pairs={{0,1},{1,0},{2,3},{3,2},{4,5},{5,4},{6,7},{7,6},{8,9},{9,8},{10,11... | collective-permute-start | bytes 958472 | tf_op jit(solution)/shard_map/ppermute | solution.py:636
  268.5 26.8 %collective-permute-start.29 = (bf16[384,384]{1,0:T(8,128)(2,1)S(1)}, bf16[384,384]{1,0:T(8,128)(2,1)S(1)}, u32[]{:S(2)}, u32[]{:S(2)}) collective-permute-start(bf16[384,384]{1,0:T(8,128)(2,1)S(1)} %copy-done.2), channel_id=1, source_target_pairs={{0,2},{1,3},{2,0},{3,1},{4,6},{5,7},{6,4},{7,5},{8,10},{9,11},{10,... | collective-permute-start | bytes 884744 | tf_op jit(solution)/shard_map/ppermute | solution.py:636
  280.6 16.8 %collective-permute-start.26 = (bf16[96,1536]{1,0:T(8,128)(2,1)}, bf16[96,1536]{1,0:T(8,128)(2,1)S(1)}, u32[]{:S(2)}, u32[]{:S(2)}) collective-permute-start(bf16[96,1536]{1,0:T(8,128)(2,1)} %w_in_f.1.refs_7_.refs_1_), channel_id=1, source_target_pairs={{0,2},{1,3},{2,0},{3,1},{4,6},{5,7},{6,4},{7,5},{8,10},{9,11},{10,... | collective-permute-start | bytes 884744 | tf_op jit(solution)/shard_map/ppermute | solution.py:636
  280.6 16.7 %collective-permute-start.19 = (bf16[192,384]{1,0:T(8,128)(2,1)}, bf16[192,384]{1,0:T(8,128)(2,1)S(1)}, u32[]{:S(2)}, u32[]{:S(2)}) collective-permute-start(bf16[192,384]{1,0:T(8,128)(2,1)} %attn_a_a.1.refs_2_.refs_0_), channel_id=1, source_target_pairs={{0,4},{1,5},{2,6},{3,7},{4,0},{5,1},{6,2},{7,3},{8,12},{9,13},{10,... | collective-permute-start | bytes 442376 | tf_op jit(solution)/shard_map/ppermute | solution.py:636
  295.3 16.3 %collective-permute-start.31 = (bf16[384,384]{1,0:T(8,128)(2,1)S(1)}, bf16[384,384]{1,0:T(8,128)(2,1)S(1)}, u32[]{:S(2)}, u32[]{:S(2)}) collective-permute-start(bf16[384,384]{1,0:T(8,128)(2,1)S(1)} %collective-permute-done.29.refs_2_), channel_id=1, source_target_pairs={{0,1},{1,0},{2,3},{3,2},{4,5},{5,4},{6,7},{7,6},{8,9},{9,8},{10,11... | collective-permute-start | bytes 884744 | tf_op jit(solution)/shard_map/ppermute | solution.py:636
  297.3 18.6 %collective-permute-start.27 = (bf16[96,1536]{1,0:T(8,128)(2,1)S(1)}, bf16[96,1536]{1,0:T(8,128)(2,1)S(1)}, u32[]{:S(2)}, u32[]{:S(2)}) collective-permute-start(bf16[96,1536]{1,0:T(8,128)(2,1)S(1)} %copy-done.4), channel_id=1, source_target_pairs={{0,1},{1,0},{2,3},{3,2},{4,5},{5,4},{6,7},{7,6},{8,9},{9,8},{10,11... | collective-permute-start | bytes 884744 | tf_op jit(solution)/shard_map/ppermute | solution.py:636
  297.4 20.7 %collective-permute-start.28 = (bf16[96,1536]{1,0:T(8,128)(2,1)S(1)}, bf16[96,1536]{1,0:T(8,128)(2,1)S(1)}, u32[]{:S(2)}, u32[]{:S(2)}) collective-permute-start(bf16[96,1536]{1,0:T(8,128)(2,1)S(1)} %collective-permute-done.26.refs_2_), channel_id=1, source_target_pairs={{0,1},{1,0},{2,3},{3,2},{4,5},{5,4},{6,7},{7,6},{8,9},{9,8},{10,11... | collective-permute-start | bytes 884744 | tf_op jit(solution)/shard_map/ppermute | solution.py:636
  303.4 19.0 %collective-permute-start.25 = (bf16[208,384]{1,0:T(8,128)(2,1)}, bf16[208,384]{1,0:T(8,128)(2,1)S(1)}, u32[]{:S(2)}, u32[]{:S(2)}) collective-permute-start(bf16[208,384]{1,0:T(8,128)(2,1)} %attn_b_a.1.refs_5_.refs_0_), channel_id=1, source_target_pairs={{0,4},{1,5},{2,6},{3,7},{4,0},{5,1},{6,2},{7,3},{8,12},{9,13},{10,... | collective-permute-start | bytes 479240 | tf_op jit(solution)/shard_map/ppermute | solution.py:636
  (60 other events, 272.8 us)

commit v2 on v1

v2 whole, which is shorter than its diff:
```python
import functools

import jax
import jax.numpy as jnp
from jax import lax
from jax.experimental import pallas as pl
from jax.experimental.pallas import tpu as pltpu
from jax.sharding import PartitionSpec as P

EPS = 1e-05
BIG = 1e30
BF = jnp.bfloat16
F32 = jnp.float32
I32 = jnp.int32
MIB = 1 << 20
COST = 5e10
COST_SMALL = 1e10

NN = (((1,), (0,)), ((), ()))
NT = (((1,), (1,)), ((), ()))
TN = (((0,), (0,)), ((), ()))


def mm(left_op, right_op, dims):
    return lax.dot_general(left_op, right_op, dims, preferred_element_type=F32)


def sds(shape, dtype):
    return jax.ShapeDtypeStruct(shape, dtype)


def hbm(shape, dtype):
    return pltpu.HBM(shape, dtype)


def vmem(shape, dtype):
    return pltpu.VMEM(shape, dtype)


def whole_block(shape):
    zeros = (0,) * len(shape)
    return pl.BlockSpec(shape, lambda *_: zeros)


def smem():
    return pl.BlockSpec(memory_space=pltpu.SMEM)


class Chain:
    def __init__(self):
        self.last = None
        self.spaces = {}

    def link(self, outs, shapes):
        flat = jax.tree.leaves(outs)
        self.last = min(flat, key=lambda a: a.size * a.dtype.itemsize)
        for out, shape in zip(flat, shapes if isinstance(shapes, (list, tuple)) else [shapes]):
            if getattr(shape, "memory_space", None) in (pltpu.HBM, pltpu.VMEM):
                self.keep(shape.memory_space, out)

    def keep(self, space, *arrays):
        for array in arrays:
            self.spaces[id(array)] = (space, array)

    def place(self, array):
        if id(array) in self.spaces:
            return pltpu.with_memory_space_constraint(array, self.spaces[id(array)][0])
        return array


def call(chain, body, name, *, grid, in_specs, out_specs, out_shape, scratch=(), prefetch=0,
         aliases=None, vmem=56, cost=COST, free=()):
    count = prefetch + len(in_specs)
    before = [] if chain.last is None else [chain.last]

    def ordered(*refs):
        body(*refs[:count], *refs[count + len(before) :])

    kernel = pl.pallas_call(
        ordered,
        name=name,
        grid_spec=pltpu.PrefetchScalarGridSpec(
            num_scalar_prefetch=prefetch,
            grid=grid,
            in_specs=list(in_specs) + [pl.BlockSpec(memory_space=pl.ANY)] * len(before),
            out_specs=out_specs,
            scratch_shapes=list(scratch),
        ),
        out_shape=out_shape,
        input_output_aliases=aliases or {},
        compiler_params=pltpu.CompilerParams(
            vmem_limit_bytes=vmem * MIB, dimension_semantics=("arbitrary",) * len(grid)
        ),
        cost_estimate=pl.CostEstimate(flops=int(cost), bytes_accessed=1, transcendentals=0),
    )

    def run(*args):
        placed = [a if at in free else chain.place(a) for at, a in enumerate(args)]
        outs = kernel(*placed, *[chain.place(a) for a in before])
        chain.link(outs, out_shape)
        return outs

    return run


def slot_of(rel):
    return jnp.where(rel == 0, 3, jnp.where(rel == 3, 0, rel))


def floor_div(values, divisor):
    return jnp.floor((values.astype(F32) + 0.5) * (1.0 / divisor)).astype(I32)


def route_kernel(ffn_rows, capacity, place_ref, slot_ref, target_ref):
    devices = target_ref.shape[0]
    rows = place_ref.shape[1]
    place = place_ref[...]
    live = place >= 0
    dev = jnp.where(live, floor_div(place, ffn_rows), -1)
    local = place - dev * ffn_rows
    hit = lax.broadcasted_iota(I32, (devices, rows), 0) == dev
    onehot = hit.astype(F32)
    upper = (
        lax.broadcasted_iota(I32, (rows, rows), 0) <= lax.broadcasted_iota(I32, (rows, rows), 1)
    ).astype(F32).astype(BF)
    running = mm(onehot.astype(BF), upper, NN)
    rank = (jnp.sum(running * onehot, axis=0, keepdims=True) - 1.0).astype(I32)
    slot_ref[...] = jnp.where(live, dev * capacity + rank, devices * capacity)
    ranked = (lax.broadcasted_iota(I32, (capacity, rows), 0) == rank).astype(F32).astype(BF)
    high = (local >> 5).astype(F32)
    low = (local & 31).astype(F32)
    filled = mm(onehot.astype(BF), ranked, NT)
    high_at = mm((onehot * high).astype(BF), ranked, NT)
    low_at = mm((onehot * low).astype(BF), ranked, NT)
    target = (high_at * 32.0 + low_at).astype(I32)
    target_ref[...] = jnp.where(filled > 0.5, target, ffn_rows)


def expand_targets(target, capacity):
    devices = target.shape[0]
    slots = devices * capacity
    lane = lax.broadcasted_iota(I32, (capacity, slots), 1)
    lane_dev = floor_div(lane, capacity)
    spread = ((lane - lane_dev * capacity) == lax.broadcasted_iota(I32, (capacity, slots), 0)).astype(
        F32
    ).astype(BF)
    high = mm((target >> 5).astype(F32).astype(BF), spread, NN)
    low = mm((target & 31).astype(F32).astype(BF), spread, NN)
    wide = high * 32.0 + low
    own_dev = floor_div(lax.broadcasted_iota(I32, (devices, slots), 1), capacity)
    own = own_dev == lax.broadcasted_iota(I32, (devices, slots), 0)
    return jnp.sum(jnp.where(own, wide, 0.0), axis=0, keepdims=True).astype(I32)


def onehot_rows(row_index, row_count):
    lanes = row_index.shape[1]
    return (lax.broadcasted_iota(I32, (row_count, lanes), 0) == row_index).astype(F32).astype(BF)


def onehot_cols(row_index, col_count):
    rows = row_index.shape[1]
    column = jnp.broadcast_to(row_index.astype(F32), (128, rows)).T[:, :1].astype(I32)
    return (lax.broadcasted_iota(I32, (rows, col_count), 1) == column).astype(F32).astype(BF)


def gather_kernel(capacity, target_ref, cot_ref, out_ref, row_ref):
    row = expand_targets(target_ref[...], capacity)
    row_ref[...] = row
    chosen = onehot_cols(row, cot_ref.shape[0])
    out_ref[...] = mm(chosen, cot_ref[...], NN).astype(BF)


def place_kernel(row_ref, in_ref, out_ref):
    chosen = onehot_rows(row_ref[...], out_ref.shape[0])
    out_ref[...] = mm(chosen, in_ref[...], NN).astype(BF)


def norm_rows(values):
    center = values - jnp.mean(values, axis=-1, keepdims=True)
    inverse = lax.rsqrt(jnp.mean(center * center, axis=-1, keepdims=True) + EPS)
    return center * inverse, inverse


def project(x_ref, w_refs, bq, bv, outs):
    x = x_ref[...]
    wq_ref, wk_ref, wv_ref = w_refs
    q_ref, k_ref, v_ref = outs
    q_ref[...] = (mm(x, wq_ref[...], NN) + bq).astype(BF)
    k_ref[...] = mm(x, wk_ref[...], NN).astype(BF)
    v_ref[...] = (mm(x, wv_ref[...], NN) + bv).astype(BF)


def attend_pair(
    head_base, heads, len_ref, swap_ref, q_ref, k_ref, v_ref, cut, ctx_ref, soft_ref, linv_ref
):
    rows = q_ref.shape[0]
    half = rows // 2
    quarter = rows // 4
    head_size = 128 // heads
    scale = head_size ** (-0.5)
    len0, len1 = len_ref[0, 0], len_ref[0, 1]
    is_long = len1 == 0
    lane = lax.broadcasted_iota(I32, (1, 128), 1)
    row = lax.broadcasted_iota(I32, (half, 1), 0)
    row_quarter = (row >= quarter).astype(I32)
    for b in range(2):
        q_rows = slice(b * half, (b + 1) * half)
        q_blk = q_ref[q_rows, cut].astype(F32) * scale
        out_blk = linv_blk = None
        for sub in range(heads):
            swapped = swap_ref[head_base + sub] == 1
            cross = jnp.logical_and(is_long, swapped)
            kb = jnp.where(cross, 1 - b, b)
            limit = jnp.where(is_long, len0 - kb * half, jnp.where(kb == 0, len0, len1))
            mine = jnp.logical_and(lane >= sub * head_size, lane < (sub + 1) * head_size)
            spare = ((sub + 1) % heads) * head_size
            key_rows = pl.ds(pl.multiple_of(kb * half, half), half)
            k_one = jnp.where(mine, k_ref[key_rows, cut].astype(F32), 0.0)
            q_one = jnp.where(mine, q_blk, 0.0)
            for part in range(2):
                other = jnp.where(swapped, 1 - part, part)
                band_ok = jnp.logical_or(is_long, row_quarter == other)
                bias = jnp.where(jnp.logical_and(band_ok, row < limit), 0.0, -BIG)
                at = lane == spare + part
                k_one = jnp.where(at, bias, k_one)
                q_one = jnp.where(at, jnp.where(row_quarter == part, 1.0, 0.0), q_one)
            scores = mm(q_one.astype(BF), k_one.astype(BF), NT)
            top = jnp.max(scores, axis=1, keepdims=True)
            weights = jnp.exp(scores - top)
            linv = 1.0 / jnp.sum(weights, axis=1, keepdims=True)
            soft = weights.astype(BF)
            soft_ref[sub, b] = soft
            mixed = mm(soft, v_ref[key_rows, cut], NN) * linv
            out_blk = mixed if out_blk is None else jnp.where(mine, mixed, out_blk)
            linv_blk = (
                jnp.broadcast_to(linv, mixed.shape)
                if linv_blk is None
                else jnp.where(mine, linv, linv_blk)
            )
        ctx_ref[q_rows, :] = out_blk.astype(BF)
        linv_ref[q_rows, :] = linv_blk


def attend_kernel(
    first, pairs, heads, ids_ref, len_ref, swap_ref, x_ref, wq_ref, wk_ref, wv_ref, b_ref, *refs
):
    if first == 0:
        q_ref, k_ref, v_ref, ctx_ref, soft_ref, linv_ref, xt_ref = refs
    else:
        (
            ctx0_ref, wo0_ref, wo_ref, ob_ref, gain_ref, shift_ref,
            q_ref, k_ref, v_ref, ctx_ref, soft_ref, linv_ref, first_ref, normed_ref, inv_ref,
            ctxt_ref, acc_ref, ctx_all,
        ) = refs
    cols = q_ref.shape[1]
    width = x_ref.shape[1]
    group = first + pl.program_id(0)
    pair = pl.program_id(1)

    @pl.when(pair == 0)
    def _():
        bq = b_ref[pl.ds(pl.multiple_of(group * cols, cols), cols)].reshape(1, -1)
        bv = b_ref[pl.ds(pl.multiple_of(width + group * cols, cols), cols)].reshape(1, -1)
        project(x_ref, (wq_ref, wk_ref, wv_ref), bq, bv, (q_ref, k_ref, v_ref))

    cut = pl.ds(pl.multiple_of(pair * 128, 128), 128)
    attend_pair(
        group * (pairs * heads) + pair * heads, heads, len_ref, swap_ref, q_ref, k_ref, v_ref, cut,
        ctx_ref, soft_ref, linv_ref,
    )
    if first == 0:

        @pl.when(pair == pairs - 1)
        def _():
            write_turned(x_ref[...], ids_ref[0], xt_ref)

        return
    ctx_all[:, pl.ds(pl.multiple_of(group * cols + pair * 128, 128), 128)] = ctx_ref[...]

    @pl.when(pair == pairs - 1)
    def _():
        own = pl.ds(pl.multiple_of(group * cols, cols), cols)
        part_sum = mm(ctx_all[:, own], wo_ref[...], NN)

        @pl.when(group == first)
        def _():
            ctx_all[:, :cols] = ctx0_ref[...]
            acc_ref[...] = part_sum + mm(ctx0_ref[...], wo0_ref[...], NN)

        @pl.when(group > first)
        def _():
            acc_ref[...] += part_sum

        @pl.when(pl.program_id(0) == pl.num_programs(0) - 1)
        def _():
            attn = acc_ref[...] + ob_ref[...].reshape(1, -1)
            normed, inverse = norm_rows(x_ref[...].astype(F32) + attn)
            normed_ref[...] = normed.astype(BF)
            inv_ref[...] = inverse
            out = normed * gain_ref[...].reshape(1, -1) + shift_ref[...].reshape(1, -1)
            first_ref[...] = out.astype(BF)
            write_turned(ctx_all[...], ids_ref[0], ctxt_ref)


def write_turned(values, seq_id, out_ref):
    turned = values.T
    quarter = turned.shape[0] // 4
    for q in range(4):
        at = slot_of(jnp.bitwise_xor(seq_id, q))
        out_ref[pl.ds(pl.multiple_of(at * quarter, quarter), quarter), :] = turned[
            q * quarter : (q + 1) * quarter
        ]


def block_cols(index, size):
    return pl.ds(pl.multiple_of(index * size, size), size)


def ffn_kernel(
    ids_ref, x_ref, wi_ref, bi_ref, wd_ref, bd_ref, gain_ref, shift_ref,
    hid_ref, slope_ref, normed_ref, inv_ref, out_ref, xt_ref, acc_ref,
):
    step = pl.program_id(0)
    steps = pl.num_programs(0)
    x = x_ref[...]
    own = block_cols(step, wi_ref.shape[1])
    pre = mm(x, wi_ref[...], NN) + bi_ref[own].reshape(1, -1)
    phi = 0.5 * (1.0 + lax.erf(pre * 0.7071067811865476))
    hid = (pre * phi).astype(BF)
    hid_ref[...] = hid
    slope_ref[...] = (phi + pre * jnp.exp(-0.5 * pre * pre) * 0.3989422804014327).astype(BF)
    part_sum = mm(hid, wd_ref[...], NN)

    @pl.when(step == 0)
    def _():
        acc_ref[...] = part_sum
        write_turned(x, ids_ref[0], xt_ref)

    @pl.when(step > 0)
    def _():
        acc_ref[...] += part_sum

    @pl.when(step == steps - 1)
    def _():
        branch = acc_ref[...] + bd_ref[...].reshape(1, -1)
        normed, inverse = norm_rows(x_ref[...].astype(F32) + branch)
        normed_ref[...] = normed.astype(BF)
        inv_ref[...] = inverse
        out = normed * gain_ref[...].reshape(1, -1) + shift_ref[...].reshape(1, -1)
        out_ref[...] = out.astype(BF)


def norm_back(upstream, normed, inverse, gain):
    scaled = upstream * gain
    inner = (
        scaled
        - jnp.mean(scaled, axis=-1, keepdims=True)
        - normed * jnp.mean(scaled * normed, axis=-1, keepdims=True)
    )
    return inner * inverse


def put_rows(ref, *rows):
    for at, row in enumerate(rows):
        ref[at : at + 1, :] = row


def store_halves(ids_ref, total, mine_ref, other_ref):
    half = mine_ref.shape[1]
    second = (ids_ref[1] & 1) == 1
    left, right = total[:, :half], total[:, half:]
    mine_ref[...] = jnp.where(second, right, left)
    other_ref[...] = jnp.where(second, left, right)


def quarter_at(step, ids_ref, near):
    rel = jnp.where(step == 0, 2, 0) if near else jnp.where(step == 0, 3, 1)
    return jnp.bitwise_xor(ids_ref[0], rel)


def act_back(ids_ref, near, branch, wd_ref, slope_ref, act_ref, bias_ref):
    own = block_cols(quarter_at(pl.program_id(0), ids_ref, near), wd_ref.shape[0])
    g_act = (mm(branch, wd_ref[...], NT) * slope_ref[:, own].astype(F32)).astype(BF)
    act_ref[:, own] = g_act
    bias_ref[:, own] = jnp.sum(g_act.astype(F32), axis=0, keepdims=True)


def cot_back_kernel(
    slot_ref, in_ref, normed_ref, inv_ref, gain_ref, pre_ref, branch_ref, vec_ref
):
    chosen = onehot_cols(slot_ref[...], in_ref.shape[0])
    cot = mm(chosen, in_ref[...], NN)
    normed = normed_ref[...].astype(F32)
    g_pre = norm_back(cot, normed, inv_ref[...], gain_ref[...].reshape(1, -1))
    pre_ref[...] = g_pre
    branch = g_pre.astype(BF)
    branch_ref[...] = branch
    put_rows(
        vec_ref,
        jnp.sum(cot * normed, axis=0, keepdims=True),
        jnp.sum(cot, axis=0, keepdims=True),
        jnp.sum(branch.astype(F32), axis=0, keepdims=True),
    )


def down_back_kernel(ids_ref, branch_ref, wd_ref, slope_ref, hid_ref, act_ref, bias_ref, gw_ref):
    branch = branch_ref[...]
    act_back(ids_ref, False, branch, wd_ref, slope_ref, act_ref, bias_ref)
    own = block_cols(quarter_at(pl.program_id(0), ids_ref, False), wd_ref.shape[0])
    gw_ref[pl.program_id(0)] = mm(hid_ref[:, own], branch, TN).astype(BF)


def act_back_kernel(ids_ref, branch_ref, wd_ref, slope_ref, old_act, act_ref, bias_ref):
    act_back(ids_ref, True, branch_ref[...], wd_ref, slope_ref, act_ref, bias_ref)


def down_grad_kernel(ids_ref, hid_ref, branch_ref, mate_ref, send_ref, keep_ref):
    step = pl.program_id(0)
    own = block_cols(quarter_at(step, ids_ref, True), send_ref.shape[0])
    grad = mm(hid_ref[:, own], branch_ref[...], TN).astype(BF).astype(F32)
    total = (grad + mate_ref[step].astype(F32)).astype(BF)

    @pl.when(step == 0)
    def _():
        send_ref[...] = total

    @pl.when(step == 1)
    def _():
        keep_ref[...] = total


def in_grad_kernel(near, ids_ref, xt_ref, act_ref, *refs):
    half = xt_ref.shape[0] // 2
    turned = xt_ref[half:, :] if near else xt_ref[:half, :]
    grad = mm(turned, act_ref[...], NN).astype(BF)
    if not near:
        refs[0][...] = grad
        return
    mate_ref, mine_ref, other_ref = refs
    total = (grad.astype(F32) + mate_ref[...].astype(F32)).astype(BF)
    store_halves(ids_ref, total, mine_ref, other_ref)


def first_back_kernel(
    pre2_ref, act_ref, wi_ref, normed_ref, inv_ref, gain_ref, wo_ref, linv0_ref, linv_ref,
    pre1_ref, gattn_ref, gctx_ref, vec_ref, acc_ref,
):
    step = pl.program_id(0)
    part_sum = mm(act_ref[:, block_cols(step, wi_ref.shape[1])], wi_ref[...], NT)

    @pl.when(step == 0)
    def _():
        acc_ref[...] = part_sum

    @pl.when(step > 0)
    def _():
        acc_ref[...] += part_sum

    @pl.when(step == pl.num_programs(0) - 1)
    def _():
        g_first = (pre2_ref[...] + acc_ref[...]).astype(BF).astype(F32)
        normed = normed_ref[...].astype(F32)
        g_pre = norm_back(g_first, normed, inv_ref[...], gain_ref[...].reshape(1, -1))
        pre1_ref[...] = g_pre
        g_attn = g_pre.astype(BF)
        put_rows(
            vec_ref,
            jnp.sum(g_first * normed, axis=0, keepdims=True),
            jnp.sum(g_first, axis=0, keepdims=True),
            jnp.sum(g_attn.astype(F32), axis=0, keepdims=True),
        )
        g_ctx = mm(g_attn, wo_ref[...], NT)
        cols = linv0_ref.shape[1]
        gctx_ref[:, :cols] = (g_ctx[:, :cols] * linv0_ref[...]).astype(BF)
        gctx_ref[:, cols:] = (g_ctx[:, cols:] * linv_ref[...]).astype(BF)
        gattn_ref[...] = g_attn


def attend_back_kernel(
    head_base, heads, len_ref, swap_ref, q_ref, k_ref, v_ref, soft_ref, gctx_ref, ctx_ref,
    proj_ref, vec_ref, gq_s, gk_s, gv_s,
):
    step = pl.program_id(0)
    rows = q_ref.shape[0]
    half = rows // 2
    head_size = 128 // heads
    scale = head_size ** (-0.5)
    is_long = len_ref[0, 1] == 0
    lane = lax.broadcasted_iota(I32, (1, 128), 1)
    for sub in range(heads):
        swapped = swap_ref[head_base + step * heads + sub] == 1
        cross = jnp.logical_and(is_long, swapped)
        mine = jnp.logical_and(lane >= sub * head_size, lane < (sub + 1) * head_size)
        for b in range(2):
            q_rows = slice(b * half, (b + 1) * half)
            kb = jnp.where(cross, 1 - b, b)
            key_rows = pl.ds(pl.multiple_of(kb * half, half), half)
            soft = soft_ref[sub, b]
            up = gctx_ref[q_rows, :]
            up_one = jnp.where(mine, up, jnp.zeros_like(up))
            inner = jnp.sum(
                up_one.astype(F32) * ctx_ref[q_rows, :].astype(F32), axis=1, keepdims=True
            )
            g_soft = mm(up_one, v_ref[key_rows, :], NT)
            g_scores = (soft.astype(F32) * (g_soft - inner)).astype(BF)
            g_q = mm(g_scores, k_ref[key_rows, :], NN) * scale
            g_k = mm(g_scores, q_ref[q_rows, :], TN) * scale
            g_v = mm(soft, up, TN)
            if sub == 0:
                gq_s[q_rows, :] = g_q
                gk_s[key_rows, :] = g_k
                gv_s[key_rows, :] = g_v
            else:
                gq_s[q_rows, :] = jnp.where(mine, g_q, gq_s[q_rows, :])
                gk_s[key_rows, :] = jnp.where(mine, g_k, gk_s[key_rows, :])
                gv_s[key_rows, :] = jnp.where(mine, g_v, gv_s[key_rows, :])
    cols = proj_ref.shape[1] // 3
    for at, ref in enumerate((gq_s, gk_s, gv_s)):
        low = ref[...].astype(BF)
        out_cols = pl.ds(pl.multiple_of(at * cols + step * 128, 128), 128)
        proj_ref[:, out_cols] = low
        vec_ref[:, out_cols] = jnp.sum(low.astype(F32), axis=0, keepdims=True)


def input_grad_kernel(groups, *refs):
    proj_refs, (wq_ref, wk_ref, wv_ref, pre_ref, out_ref, acc_ref) = refs[:groups], refs[groups:]
    step = pl.program_id(0)
    cols = wq_ref.shape[1]

    @pl.when(step == 0)
    def _():
        acc_ref[...] = pre_ref[...]

    for at, proj_ref in enumerate(proj_refs):

        @pl.when(step == at)
        def _():
            acc_ref[...] += (
                mm(proj_ref[:, :cols], wq_ref[...], NT)
                + mm(proj_ref[:, cols : 2 * cols], wk_ref[...], NT)
                + mm(proj_ref[:, 2 * cols :], wv_ref[...], NT)
            )

    @pl.when(step == groups - 1)
    def _():
        out_ref[...] = acc_ref[...].astype(BF)


def vector_rows(ids_ref, rel_of, rows_ref, base_of, vec_refs):
    vec2_ref, bias_a, bias_b, vec1_ref, *qkv_refs = vec_refs
    width = vec1_ref.shape[1]
    cols = width // len(qkv_refs)
    wide = jnp.concatenate(
        [ref[:, :cols] for ref in qkv_refs] + [ref[:, 2 * cols :] for ref in qkv_refs], axis=1
    )
    for q in range(4):
        rel = jnp.bitwise_xor(ids_ref[0], q)
        odd = (rel & 1) == 1
        hid_q = slice(q * (bias_a.shape[1] // 4), (q + 1) * (bias_a.shape[1] // 4))
        rows = [jnp.where(odd, bias_a[:, hid_q], bias_b[:, hid_q])]
        qv = width // 2
        rows.append(wide[:, q * qv : (q + 1) * qv])
        own = slice(q * (width // 4), (q + 1) * (width // 4))
        for ref in (vec2_ref, vec1_ref):
            for at in range(3):
                rows.append(ref[at : at + 1, own])

        def store(base):
            for r, row in enumerate(rows):
                rows_ref[base + r : base + r + 1, : row.shape[1]] = row

        for want, base in zip(rel_of, base_of):
            pl.when(rel == want)(functools.partial(store, base))


def share_grad_kernel(near, y_first, count, extra, ids_ref, *refs):
    pairs = [(refs[2 * at], refs[2 * at + 1]) for at in range(count)]
    refs = refs[2 * count :]
    part = pairs[0][0].shape[0] // 4
    size = count * part + extra
    if extra:
        *refs, rows_ref = refs
    if near:
        *vec_refs, mate_ref, left_ref, right_ref = refs
    else:
        *vec_refs, out_ref = refs

    def put(base, value):
        rows = slice(base, base + value.shape[0])
        if near:
            value = value.astype(F32) + mate_ref[rows, :].astype(F32)
        value = value.astype(BF)
        if not near:
            out_ref[rows, :] = value
        elif y_first:
            store_halves(ids_ref, value, left_ref.at[rows], right_ref.at[rows])
        else:
            out = left_ref if base < size else right_ref
            base -= 0 if base < size else size
            out[base : base + value.shape[0], :] = value

    for at, (turned_ref, product_ref) in enumerate(pairs):
        cut = 2 * part
        turned = turned_ref[cut:, :] if near else turned_ref[:cut, :]
        grad = mm(turned, product_ref[...], NN).astype(BF)
        put(at * part, grad[:part])
        put(size + at * part, grad[part:])
    if extra:
        rows_ref[...] = jnp.zeros_like(rows_ref)
        vector_rows(ids_ref, (2, 0) if near else (3, 1), rows_ref, (0, extra), vec_refs)
        for half in range(2):
            vectors = rows_ref[half * extra : (half + 1) * extra, :].astype(BF)
            put(half * size + count * part, vectors)


def split_cols_kernel(ids_ref, keep_ref, got_ref, mine_ref, other_ref):
    total = (keep_ref[...].astype(F32) + got_ref[...].astype(F32)).astype(BF)
    store_halves(ids_ref, total, mine_ref, other_ref)


def split_shares_kernel(mine_ref, got_ref, send_ref, keep_ref):
    total = (mine_ref[...].astype(F32) + got_ref[...].astype(F32)).astype(BF)
    rows = send_ref.shape[0]
    send_ref[...] = total[:rows]
    keep_ref[...] = total[rows:]


def split_rows_kernel(ids_ref, keep_ref, got_ref, mine_ref, other_ref):
    half = mine_ref.shape[0]
    bit = (ids_ref[1] >> 1) & 1

    def part(at):
        rows = pl.ds(pl.multiple_of(at * half, half), half)
        return (keep_ref[rows, :].astype(F32) + got_ref[rows, :].astype(F32)).astype(BF)

    mine_ref[...] = part(bit)
    other_ref[...] = part(1 - bit)


def add_kernel(left_ref, right_ref, out_ref):
    out_ref[...] = (left_ref[...].astype(F32) + right_ref[...].astype(F32)).astype(BF)


def join_kernel(ids_ref, own_ref, near_ref, far_own_ref, far_near_ref, out_ref):
    half_rows, half_cols = own_ref.shape
    second = (ids_ref[1] & 1) == 1
    bit = (ids_ref[1] >> 1) & 1
    for rel, (mine, other) in enumerate(((own_ref, far_own_ref), (near_ref, far_near_ref))):
        at = jnp.bitwise_xor(bit, rel)
        rows = pl.ds(pl.multiple_of(at * half_rows, half_rows), half_rows)
        a, b = mine[...].astype(F32), other[...].astype(F32)
        out_ref[rows, :half_cols] = jnp.where(second, b, a)
        out_ref[rows, half_cols:] = jnp.where(second, a, b)


def stack_kernel(ids_ref, own_ref, near_ref, out_ref):
    half = own_ref.shape[0]
    bit = (ids_ref[1] >> 1) & 1
    for rel, ref in enumerate((own_ref, near_ref)):
        at = jnp.bitwise_xor(bit, rel)
        out_ref[pl.ds(pl.multiple_of(at * half, half), half), :] = ref[...]


def join_into(ids_ref, mine_ref, other_ref, out_ref):
    half = mine_ref.shape[1]
    second = (ids_ref[1] & 1) == 1
    a, b = mine_ref[...].astype(F32), other_ref[...].astype(F32)
    out_ref[:, :half] = jnp.where(second, b, a)
    out_ref[:, half:] = jnp.where(second, a, b)


def join_kernel(ids_ref, mine_ref, other_ref, out_ref):
    join_into(ids_ref, mine_ref, other_ref, out_ref)


def attend_join_kernel(groups, ids_ref, *refs):
    a_refs, b_refs = refs[:2], refs[2:4]
    gwq_ref, gwo_ref, qv_ref, hid_ref = refs[4:8]
    vec_refs, (a_all, b_all) = refs[8:14], refs[14:]
    join_into(ids_ref, *a_refs, a_all)
    join_into(ids_ref, *b_refs, b_all)
    part, width = gwo_ref.shape
    cols = width // groups
    gwo_ref[...] = a_all[:part, :]
    places = [(a_all, part)] + [(b_all, part * at) for at in range(groups - 1)]
    for g, (ref, base) in enumerate(places):
        for at in range(3):
            gwq_ref[:, at * width + g * cols : at * width + (g + 1) * cols] = ref[
                base : base + part, at * cols : (at + 1) * cols
            ]
    base = part * (groups - 1)
    hid_ref[...] = b_all[base, :]
    qv_ref[...] = b_all[base + 1, : qv_ref.shape[0]]
    for at, ref in enumerate(vec_refs):
        ref[...] = b_all[base + 2 + at, : ref.shape[0]]


def exchange(values, axis, mask):
    count = lax.axis_size(axis)
    return lax.ppermute(values, axis, [(i, i ^ mask) for i in range(count)])


def simple(chain, body, name, args, out_shape, prefetch=0, vmem=12, scratch=(), cost=COST_SMALL):
    tensors = args[prefetch:]
    return call(
        chain,
        body,
        name,
        grid=(1,),
        in_specs=[whole_block(a.shape) for a in tensors],
        out_specs=[whole_block(o.shape) for o in out_shape],
        out_shape=out_shape,
        prefetch=prefetch,
        vmem=vmem,
        cost=cost,
        scratch=scratch,
    )(*args)


class Share:
    def __init__(self, chain, ids, name, left, right, y_first=False):
        self.chain, self.ids, self.name = chain, ids, name
        if y_first:
            self.keep, self.got = left, exchange(right, "batch", 1)
            self.shape = (left.shape[0] // 2, left.shape[1] * 2)
        else:
            self.keep, self.got = right, exchange(left, "seq", 2)
            self.shape = right.shape

    def step_x(self):
        rows, cols = self.shape
        send, self.keep = simple(
            self.chain, split_shares_kernel, self.name + "_x", (self.keep, self.got),
            [vmem((rows, cols // 2), BF)] * 2,
        )
        self.got = exchange(send, "seq", 2)

    def halve(self, kernel, shape, label, mask):
        self.keep, other = simple(
            self.chain, kernel, self.name + label, (self.ids, self.keep, self.got),
            [vmem(shape, BF)] * 2, 1,
        )
        self.got = exchange(other, "batch", mask)

    def step_y(self):
        rows, cols = self.shape
        self.halve(split_cols_kernel, (rows, cols // 2), "_y", 1)

    def step_z(self):
        rows, cols = self.shape
        self.halve(split_rows_kernel, (rows // 2, cols // 2), "_z", 2)

    def add(self, label):
        (self.keep,) = simple(
            self.chain, add_kernel, self.name + label, (self.keep, self.got),
            [vmem(self.keep.shape, BF)],
        )

    def step_far(self):
        mask = 4
        while mask <= lax.axis_size("batch") // 2:
            self.add("_a")
            self.got = exchange(self.keep, "batch", mask)
            mask *= 2

    def step_back(self):
        self.add("_f")
        self.got = exchange(self.keep, "batch", 2)

    def step_wide(self):
        rows, cols = self.shape
        (self.keep,) = simple(
            self.chain, stack_kernel, self.name + "_g", (self.ids, self.keep, self.got),
            [vmem((rows, cols // 2), BF)], 1,
        )
        self.pieces = (self.keep, exchange(self.keep, "batch", 1))

    def join(self):
        (whole,) = simple(
            self.chain, join_kernel, self.name + "_j", (self.ids, *self.pieces),
            [hbm(self.shape, F32)], 1,
        )
        return whole


def body(
    hidden_in, seq_lengths, head_swap, place, w_qkv, qv_bias, w_out, out_bias, norm1_gain,
    norm1_bias, w_in, in_bias, w_down, down_bias, norm2_gain, norm2_bias, cotangent,
):
    rows, width = hidden_in.shape
    ff = w_in.shape[1]
    ffn_rows = cotangent.shape[0]
    devices = lax.axis_size(("seq", "batch"))
    capacity = (rows + devices - 1) // devices
    slots = devices * capacity
    head_count = head_swap.shape[0]
    head_size = width // head_count
    half = rows // 2
    cols = 256
    groups = width // cols
    heads = cols // head_size
    pair = 128 // head_size
    ids = jnp.stack([lax.axis_index("seq"), lax.axis_index("batch")]).astype(I32)
    chain = Chain()
    chain.keep(pltpu.HBM, hidden_in, w_qkv, w_out, w_in, w_down, cotangent)

    slot_row, out_target = simple(
        chain,
        functools.partial(route_kernel, ffn_rows, capacity),
        "route",
        (place.reshape(1, -1),),
        [sds((1, rows), I32), sds((devices, capacity), I32)],
    )
    in_target = lax.all_to_all(out_target, ("seq", "batch"), split_axis=0, concat_axis=0, tiled=True)

    bf_rows = (rows, width)
    turned_shape = (width, rows)
    vec_spec = whole_block((width,))
    steps = heads // pair
    some = lambda count, dtype: hbm((rows, count * cols), dtype)
    col = lambda base: pl.BlockSpec((width, cols), lambda g, p, *_: (0, base + g))
    out_col = pl.BlockSpec((rows, cols), lambda g, p, *_: (0, g))
    pair_out = pl.BlockSpec((rows, 128), lambda g, p, *_: (0, g * steps + p))
    soft_spec = pl.BlockSpec((pair, 2, half, half), lambda g, p, *_: (g * steps + p, 0, 0, 0))
    head_outs = [out_col] * 3 + [pair_out, soft_spec, pair_out]
    head_shapes = lambda count: [some(count, BF)] * 4 + [
        hbm((count * heads, 2, half, half), BF), some(count, F32)
    ]
    head_args = (ids, seq_lengths, head_swap, hidden_in, w_qkv, w_qkv, w_qkv, qv_bias)
    head_specs = lambda first: [
        smem(), smem(), whole_block(bf_rows), col(first), col(groups + first),
        col(2 * groups + first), whole_block((2 * width,)),
    ]
    *first_heads, x_turned = call(
        chain,
        functools.partial(attend_kernel, 0, steps, pair),
        "attend_first",
        vmem=32,
        grid=(1, steps),
        in_specs=head_specs(0),
        out_specs=head_outs + [whole_block(turned_shape)],
        out_shape=head_shapes(1) + [hbm(turned_shape, BF)],
        prefetch=1,
    )(*head_args)
    context0, linv0 = first_heads[3], first_heads[5]
    cot_out, in_row = simple(
        chain,
        functools.partial(gather_kernel, capacity),
        "cot_gather",
        (in_target, cotangent),
        [sds((slots, width), BF), sds((1, slots), I32)],
    )
    cot_in = lax.all_to_all(cot_out, ("seq", "batch"), split_axis=0, concat_axis=0, tiled=True)
    *rest_heads, first_low, normed1, inv1, ctx_turned = call(
        chain,
        functools.partial(attend_kernel, 1, steps, pair),
        "attend_rest",
        vmem=40,
        grid=(groups - 1, steps),
        in_specs=head_specs(1)
        + [
            whole_block((rows, cols)), pl.BlockSpec((cols, width), lambda g, p, *_: (0, 0)),
            pl.BlockSpec((cols, width), lambda g, p, *_: (1 + g, 0)), vec_spec, vec_spec, vec_spec,
        ],
        out_specs=head_outs
        + [
            whole_block(bf_rows), whole_block(bf_rows), whole_block((rows, 1)),
            whole_block(turned_shape),
        ],
        out_shape=head_shapes(groups - 1)
        + [hbm(bf_rows, BF), hbm(bf_rows, BF), hbm((rows, 1), F32), hbm(turned_shape, BF)],
        scratch=[pltpu.VMEM(bf_rows, F32), pltpu.VMEM(bf_rows, BF)],
        prefetch=1,
    )(*head_args, context0, w_out, w_out, out_bias, norm1_gain, norm1_bias)
    linv_rest = rest_heads[5]

    blk = ff // 4
    act_shape = (rows, ff)
    act_col = pl.BlockSpec((rows, blk), lambda j, *_: (0, j))
    hid, slope, normed2, inv2, mixed_home, first_turned = call(
        chain,
        ffn_kernel,
        "ffn",
        vmem=36,
        grid=(4,),
        in_specs=[
            whole_block(bf_rows),
            pl.BlockSpec((width, blk), lambda j, *_: (0, j)),
            whole_block((ff,)),
            pl.BlockSpec((blk, width), lambda j, *_: (j, 0)),
            vec_spec, vec_spec, vec_spec,
        ],
        out_specs=[
            act_col, act_col, whole_block(bf_rows), whole_block((rows, 1)), whole_block(bf_rows),
            whole_block(turned_shape),
        ],
        out_shape=[
            hbm(act_shape, BF), hbm(act_shape, BF), hbm(bf_rows, BF), hbm((rows, 1), F32),
            hbm(bf_rows, BF), hbm(turned_shape, BF),
        ],
        scratch=[pltpu.VMEM(bf_rows, F32)],
        prefetch=1,
    )(ids, first_low, w_in, in_bias, w_down, down_bias, norm2_gain, norm2_bias)

    (mixed_out,) = simple(
        chain, place_kernel, "mixed_slots", (slot_row, mixed_home), [sds((slots, width), BF)],
        cost=COST,
    )
    mixed_in = lax.all_to_all(mixed_out, ("seq", "batch"), split_axis=0, concat_axis=0, tiled=True)

    def wd_spec(near):
        return pl.BlockSpec((blk, width), lambda j, ids_ref: (quarter_at(j, ids_ref, near), 0))

    g_pre2, g_branch, vec2 = simple(
        chain,
        cot_back_kernel,
        "cot_back",
        (slot_row, cot_in, normed2, inv2, norm2_gain),
        [hbm(bf_rows, F32), vmem(bf_rows, BF), sds((8, width), F32)],
        vmem=24,
        cost=COST,
    )
    act_half, bias_a, gwd_far = call(
        chain,
        down_back_kernel,
        "down_back",
        vmem=16,
        grid=(2,),
        in_specs=[
            whole_block(bf_rows), wd_spec(False), whole_block(act_shape), whole_block(act_shape),
        ],
        out_specs=[whole_block(act_shape), whole_block((1, ff)), whole_block((2, blk, width))],
        out_shape=[vmem(act_shape, BF), sds((1, ff), F32), vmem((2, blk, width), BF)],
        prefetch=1,
        free=(3, 4),
    )(ids, g_branch, w_down, slope, hid)
    gwd_mate = exchange(gwd_far, "seq", 1)
    g_act, bias_b = call(
        chain,
        act_back_kernel,
        "act_back",
        vmem=10,
        grid=(2,),
        in_specs=[
            whole_block(bf_rows), wd_spec(True), whole_block(act_shape), whole_block(act_shape),
        ],
        out_specs=[whole_block(act_shape), whole_block((1, ff))],
        out_shape=[vmem(act_shape, BF), sds((1, ff), F32)],
        prefetch=1,
        aliases={4: 0},
        free=(3,),
    )(ids, g_branch, w_down, slope, act_half)
    part = width // 4
    gwi_shape = (2 * part, ff)
    gwi_far = call(
        chain,
        functools.partial(in_grad_kernel, False),
        "in_grad_far",
        vmem=8,
        grid=(1,),
        in_specs=[whole_block(turned_shape), whole_block(act_shape)],
        out_specs=whole_block(gwi_shape),
        out_shape=vmem(gwi_shape, BF),
        prefetch=1,
        free=(1,),
    )(ids, first_turned, g_act)
    gwi_mate = exchange(gwi_far, "seq", 1)
    share_shape = (blk, width)
    send, keep = call(
        chain,
        down_grad_kernel,
        "down_grad",
        vmem=10,
        grid=(2,),
        in_specs=[whole_block(act_shape), whole_block(bf_rows), whole_block((2, blk, width))],
        out_specs=[whole_block(share_shape)] * 2,
        out_shape=[vmem(share_shape, BF)] * 2,
        prefetch=1,
        free=(1,),
    )(ids, hid, g_branch, gwd_mate)
    down_share = Share(chain, ids, "w_down", send, keep)


    in_share_shape = (2 * part, ff // 2)
    send, keep = call(
        chain,
        functools.partial(in_grad_kernel, True),
        "in_grad_near",
        vmem=8,
        grid=(1,),
        in_specs=[whole_block(turned_shape), whole_block(act_shape), whole_block(gwi_shape)],
        out_specs=[whole_block(in_share_shape)] * 2,
        out_shape=[vmem(in_share_shape, BF)] * 2,
        prefetch=1,
        free=(1,),
    )(ids, first_turned, g_act, gwi_mate)
    in_share = Share(chain, ids, "w_in", send, keep, y_first=True)

    g_pre1, g_attn, g_ctx, vec1 = call(
        chain,
        first_back_kernel,
        "first_back",
        vmem=32,
        grid=(4,),
        in_specs=[
            whole_block(bf_rows), whole_block(act_shape),
            pl.BlockSpec((width, blk), lambda j: (0, j)),
            whole_block(bf_rows), whole_block((rows, 1)), vec_spec,
            whole_block((width, width)), whole_block(linv0.shape), whole_block(linv_rest.shape),
        ],
        out_specs=[
            whole_block(bf_rows), whole_block(bf_rows), whole_block(bf_rows),
            whole_block((8, width)),
        ],
        out_shape=[hbm(bf_rows, F32), vmem(bf_rows, BF), vmem(bf_rows, BF), sds((8, width), F32)],
        scratch=[pltpu.VMEM(bf_rows, F32)],
        free=(0, 3, 6, 7, 8),
    )(g_pre2, g_act, w_in, normed1, inv1, norm1_gain, w_out, linv0, linv_rest)

    projs, vecs = [], []
    low = hbm(bf_rows, BF)

    def group_back(g):
        own_col = pl.BlockSpec((rows, 128), lambda p: (0, g * steps + p))
        arrays, base = (first_heads, 0) if g == 0 else (rest_heads, g - 1)
        head_col = pl.BlockSpec((rows, 128), lambda p: (0, base * steps + p))
        proj, vec = call(
            chain,
            functools.partial(attend_back_kernel, g * heads, pair),
            "attend_back",
            vmem=20,
            grid=(steps,),
            in_specs=[
                smem(), smem(), head_col, head_col, head_col,
                pl.BlockSpec((pair, 2, half, half), lambda p: (base * steps + p, 0, 0, 0)),
                own_col, head_col,
            ],
            out_specs=[whole_block((rows, 3 * cols)), whole_block((1, 3 * cols))],
            out_shape=[vmem((rows, 3 * cols), BF), sds((1, 3 * cols), F32)],
            scratch=[pltpu.VMEM((rows, 128), F32)] * 3,
        )(seq_lengths, head_swap, *arrays[:3], arrays[4], g_ctx, arrays[3])
        projs.append(proj)
        vecs.append(vec)

    def attention_share(pairs, vec_ins, name, y_first):
        extra = 32 if vec_ins else 0
        size = len(pairs) * part + extra
        flat = [a for both in pairs for a in both]
        scratch = [pltpu.VMEM((2 * extra, width), F32)] if extra else []
        (far_grad,) = simple(
            chain,
            functools.partial(share_grad_kernel, False, y_first, len(pairs), extra),
            name + "_far",
            (ids, *flat, *vec_ins),
            [vmem((2 * size, width), BF)],
            1,
            scratch=scratch,
        )
        mate = exchange(far_grad, "seq", 1)

        def near_part():
            shape = (2 * size, width // 2) if y_first else (size, width)
            left, right = simple(
                chain,
                functools.partial(share_grad_kernel, True, y_first, len(pairs), extra),
                name + "_near",
                (ids, *flat, *vec_ins, mate),
                [vmem(shape, BF)] * 2,
                1,
                scratch=scratch,
            )
            return Share(chain, ids, name, left, right, y_first)

        return near_part

    group_back(0)
    down_share.step_y()
    start_a = attention_share([(ctx_turned, g_attn), (x_turned, projs[0])], [], "attn_a", False)
    group_back(1)
    share_a = start_a()
    in_share.step_x()
    down_share.step_z()
    group_back(2)
    vec_ins = [vec2, bias_a, bias_b, vec1, *vecs]
    start_b = attention_share(
        [(x_turned, projs[1]), (x_turned, projs[2])], vec_ins, "attn_b", True
    )
    share_a.step_y()
    down_share.step_far()
    share_b = start_b()
    in_share.step_z()
    input_grad = call(
        chain,
        functools.partial(input_grad_kernel, groups),
        "input_grad",
        vmem=24,
        grid=(groups,),
        in_specs=[whole_block((rows, 3 * cols))] * groups
        + [
            pl.BlockSpec((width, cols), lambda g: (0, g)),
            pl.BlockSpec((width, cols), lambda g: (0, groups + g)),
            pl.BlockSpec((width, cols), lambda g: (0, 2 * groups + g)),
            whole_block((rows, width)),
        ],
        out_specs=whole_block((rows, width)),
        out_shape=low,
        scratch=[pltpu.VMEM((rows, width), F32)],
    )(*projs, w_qkv, w_qkv, w_qkv, g_pre1)
    (mixed,) = simple(
        chain, place_kernel, "mixed_place", (in_row, mixed_in), [hbm((ffn_rows, width), BF)]
    )
    share_b.step_x()
    share_a.step_z()
    in_share.step_far()
    down_share.step_back()
    share_b.step_z()
    share_a.step_far()
    in_share.step_back()
    share_b.step_far()
    down_share.step_wide()
    share_a.step_back()
    in_share.step_wide()
    share_b.step_back()
    share_a.step_wide()
    g_w_down = down_share.join()
    share_b.step_wide()
    g_w_in = in_share.join()
    one = lambda size: sds((size,), F32)
    g_w_qkv, g_w_out, g_qv, g_in_bias, g_n2g, g_n2b, g_down_bias, g_n1g, g_n1b, g_out_bias = simple(
        chain,
        functools.partial(attend_join_kernel, groups),
        "attn_join",
        (ids, *share_a.pieces, *share_b.pieces),
        [hbm((part, 3 * width), F32), hbm((part, width), F32), one(width // 2), one(width)]
        + [one(part)] * 6,
        1,
        scratch=[pltpu.VMEM(share_a.shape, F32), pltpu.VMEM(share_b.shape, F32)],
    )
    return (
        mixed, input_grad, g_w_qkv, g_qv, g_w_out, g_out_bias, g_n1g, g_n1b, g_w_in, g_in_bias,
        g_w_down, g_down_bias, g_n2g, g_n2b,
    )


def solution(mesh):
    rows_spec = P(("seq", "batch"), None)
    in_specs = (
        rows_spec, rows_spec, P(), P(("seq", "batch")), P(), P(), P(), P(), P(), P(), P(), P(),
        P(), P(), P(), P(), rows_spec,
    )
    out_specs = (
        rows_spec, rows_spec, P("seq", None), P("seq"), P("seq", None), P("seq"), P("seq"),
        P("seq"), P("seq", None), P("seq"), P("seq", None), P("seq"), P("seq"), P("seq"),
    )
    return jax.shard_map(body, mesh=mesh, in_specs=in_specs, out_specs=out_specs, check_vma=False)
```

time: 351 us -> 284 us (0.81)
  Pallas kernels: 233 us -> 177 us
  local copies, waits for them, and re-layouts: 20.8 us -> 1.53 us
  waiting for transfers between devices: 36.5 us -> 49.5 us
    pallas_call x38 -> x45, Pallas kernels: 233 us -> 177 us  [run(): outs = kernel(*placed, *[chain.place(a) for a in before])]
    unnamed x92 -> x66, local copies, waits for them, and re-layouts: 20.8 us -> 1.53 us
    ppermute x35 -> x28, waiting for transfers between devices: 36.5 us -> 49.5 us  [exchange(): return lax.ppermute(values, axis, [(i, i ^ mask) for i in range(count)])]
    ppermute x35 -> x28, starting transfers between devices: 32.4 us -> 29.3 us  [exchange(): return lax.ppermute(values, axis, [(i, i ^ mask) for i in range(count)])]
  transfers between devices with their start and end apart: 38 -> 31, of which waited for: 9 -> 14; matrix products, arithmetic and copies ran while one was open for 0% -> 0% of each run, Pallas kernels for 56% -> 61%
where the time goes in v2:
time: 284 us; the launch traced here: 279 us
  Pallas kernels  177 us (62%)
  waiting for transfers between devices  49.5 us (17%)
  starting transfers between devices  49.2 us (17%)
    pallas_call x45, Pallas kernels, run(): outs = kernel(*placed, *[chain.place(a) for a in before])  177 us
    ppermute x28, waiting for transfers between devices, exchange(): return lax.ppermute(values, axis, [(i, i ^ mask) for i in range(count)])  49.5 us
    ppermute x28, starting transfers between devices, exchange(): return lax.ppermute(values, axis, [(i, i ^ mask) for i in range(count)])  29.3 us
    all_to_all x1, starting transfers between devices, body(): lax.all_to_all(out_target, ('seq', 'batch'), split_axis=0, concat_axis=0,...  7.3 us
    all_to_all x1, starting transfers between devices, body(): lax.all_to_all(mixed_out, ('seq', 'batch'), split_axis=0, concat_axis=0,...  6.47 us
    all_to_all x1, starting transfers between devices, body(): lax.all_to_all(cot_out, ('seq', 'batch'), split_axis=0, concat_axis=0, ti...  6.13 us
  transfers between devices with their start and end apart: 31, of which 14 were waited for; matrix products, arithmetic and copies ran while one was open for 0% of the time, Pallas kernels for 61%

profile of v2, /device:TPU:0, one launch (start us, length us, event | category | flops | bytes accessed | tf_op | source)
XLA Modules:
  0.0 278.9 jit_solution(3912996957916676866)
XLA Ops:
  2.5 7.3 %all-to-all-start = ((s32[32,1,32]{2,1,0:T(1,128)}), s32[32,1,32]{2,1,0:T(1,128)S(1)}, u32[]{:S(2)}, u32[]{:S(2)}) async-start(s32[32,1,32]{2,1,0:T(1,128)} %bitcast.2), calls=%async_computation | async-start | bytes 32768 | tf_op jit(solution)/shard_map/all_to_all | solution.py:814
  9.9 10.5 %attend_first.1 = (bf16[1024,256]{1,0:T(8,128)(2,1)}, bf16[1024,256]{1,0:T(8,128)(2,1)}, bf16[1024,256]{1,0:T(8,128)(2,1)}, bf16[1024,256]{1,0:T(8,128)(2,1)}, b...) custom-call(s32[2]{0:T(128)S(1)} %pad_add_fusion.refs_0_, s32[1,2]{1,0:T(1,128)S(1)} %copy-done.10, ...), custom_call_target="tpu_custom_call" | custom-call | flops 49999998976 | bytes 1 | tf_op jit(solution)/shard_map/attend_first/pallas_call | solution.py:99
  20.4 4.8 %cot_gather.1 = (bf16[1024,768]{1,0:T(8,128)(2,1)}, s32[1,1024]{1,0:T(1,128)S(1)}) custom-call(s32[32,32]{1,0:T(8,128)S(1)} %bitcast.11, bf16[896,768]{1,0:T(8,128)(2,1)} %refs_1_.7, bf16[1024,256]{1,0:T(8,128)(2,1)} %get-tuple-element.95.refs_2_), custom_call_target="tpu_custom_call" | custom-call | flops 10000000000 | bytes 1 | tf_op jit(solution)/shard_map/cot_gather/pallas_call | solution.py:99
  25.3 6.1 %all-to-all-start.2 = ((bf16[32,32,768]{2,1,0:T(8,128)(2,1)}), bf16[32,32,768]{2,1,0:T(8,128)(2,1)}, u32[]{:S(2)}, u32[]{:S(2)}) async-start(bf16[32,32,768]{2,1,0:T(8,128)(2,1)} %bitcast.8), calls=%async_computation.2 | async-start | bytes 3145728 | tf_op jit(solution)/shard_map/all_to_all | solution.py:853
  31.5 21.1 %attend_rest.1 = (bf16[1024,512]{1,0:T(8,128)(2,1)}, bf16[1024,512]{1,0:T(8,128)(2,1)}, bf16[1024,512]{1,0:T(8,128)(2,1)}, bf16[1024,512]{1,0:T(8,128)(2,1)}, bf...) custom-call(s32[2]{0:T(128)S(1)} %pad_add_fusion.refs_0_, ...), custom_call_target="tpu_custom_call" | custom-call | flops 49999998976 | bytes 1 | tf_op jit(solution)/shard_map/attend_rest/pallas_call | solution.py:99
  52.6 22.2 %ffn.1 = (bf16[1024,3072]{1,0:T(8,128)(2,1)}, bf16[1024,3072]{1,0:T(8,128)(2,1)}, bf16[1024,768]{1,0:T(8,128)(2,1)}, f32[1024,1]{1,0:T(8,128)}, bf16[1024,768]{1,0:T(8,128)(2,1)}, /*index=5*/bf16[768,1024]{1,0:T(8,128)(2,1)}) custom-call(s32[2]{0:T(128)S(1)} %pad_add_fusion.refs_0_, bf16[1024,768]{1,0:T(8,128)(2,1)} %get-tuple-element.98.refs_1_, ...), custom_call_target="tpu_custom_call" | custom-call | flops 49999998976 | bytes 1 | tf_op jit(solution)/shard_map/ffn/pallas_call | solution.py:99
  74.8 4.3 %mixed_slots.1.refs_5_ = bf16[1024,768]{1,0:T(8,128)(2,1)} custom-call(s32[1,1024]{1,0:T(1,128)S(1)} %get-tuple-element.94.refs_8_.refs_0_, bf16[1024,768]{1,0:T(8,128)(2,1)} %get-tuple-element.100.refs_1_, f32[1024,1]{1,0:T(8,128)} %get-tuple-element.101.refs_2_.refs_3_), custom_call_target="tpu_custom_call" | custom-call | flops 49999998976 | bytes 1 | tf_op jit(solution)/shard_map/mixed_slots/pallas_call | solution.py:99
  79.2 6.5 %all-to-all-start.1 = ((bf16[32,32,768]{2,1,0:T(8,128)(2,1)}), bf16[32,32,768]{2,1,0:T(8,128)(2,1)}, u32[]{:S(2)}, u32[]{:S(2)}) async-start(bf16[32,32,768]{2,1,0:T(8,128)(2,1)} %bitcast.6), calls=%async_computation.1 | async-start | bytes 3145728 | tf_op jit(solution)/shard_map/all_to_all | solution.py:909
  85.7 7.2 %cot_back.1 = (f32[1024,768]{1,0:T(8,128)}, bf16[1024,768]{1,0:T(8,128)(2,1)S(1)}, f32[8,768]{1,0:T(8,128)S(1)}) custom-call(s32[1,1024]{1,0:T(1,128)S(1)} %get-tuple-element.94.refs_8_.refs_0_, bf16[1024,768]{1,0:T(8,128)(2,1)} %bitcast.9.refs_1_, bf16[1024,768]{1,0:T(8,128)(2,1)} %get-tuple-element.106.refs_2_, ...), custom_call_target="tpu_custom_call" | custom-call | flops 49999998976 | bytes 1 | tf_op jit(solution)/shard_map/cot_back/pallas_call | solution.py:99
  92.8 7.4 %down_back.1 = (bf16[1024,3072]{1,0:T(8,128)(2,1)S(1)}, f32[1,3072]{1,0:T(1,128)S(1)}, bf16[2,768,768]{2,1,0:T(8,128)(2,1)S(1)}) custom-call(s32[2]{0:T(128)S(1)} %pad_add_fusion.refs_0_, bf16[1024,768]{1,0:T(8,128)(2,1)S(1)} %get-tuple-element.108.refs_1_.refs_2_, bf16[3072,768]{1,0:T(8,128)(2,1)} %refs_2_.10, bf16[1024,3072]{1,0:T(8,128)(2,1)S(1)} %copy-done.17, ...), custom_call_target="tpu_custom_call" | custom-call | flops 49999998976 | bytes 1 | tf_op jit(solution)/shard_map/down_back/pallas_call | solution.py:99
  100.7 4.9 %act_back.1 = (bf16[1024,3072]{1,0:T(8,128)(2,1)S(1)}, f32[1,3072]{1,0:T(1,128)S(1)}) custom-call(s32[2]{0:T(128)S(1)} %pad_add_fusion.refs_0_, bf16[1024,768]{1,0:T(8,128)(2,1)S(1)} %get-tuple-element.108.refs_1_.refs_2_, bf16[3072,768]{1,0:T(8,128)(2,1)} %refs_2_.10, bf16[1024,3072]{1,0:T(8,128)(2,1)S(1)} %copy-done.17, ...), custom_call_target="tpu_custom_call", output_to_operand_aliasing={{0}: (4, {})} | custom-call | flops 49999998976 | bytes 1 | tf_op jit(solution)/shard_map/act_back/pallas_call | solution.py:99
  109.0 4.8 %down_grad.1 = (bf16[768,768]{1,0:T(8,128)(2,1)}, bf16[768,768]{1,0:T(8,128)(2,1)S(1)}) custom-call(s32[2]{0:T(128)S(1)} %pad_add_fusion.refs_0_, bf16[1024,3072]{1,0:T(8,128)(2,1)S(1)} %copy-done.16, bf16[1024,768]{1,0:T(8,128)(2,1)S(1)} %get-tuple-element.108.refs_1_.refs_2_, bf16[2,768,768]{2,1,0:T(8,128)(2,1)S(1)} %collective-permute-done.1.refs_3_, ...), custom_call_target="tpu_custom_call" | custom-call | flops 49999998976 | bytes 1 | tf_op jit(solution)/shard_map/down_grad/pallas_call | solution.py:99
  115.8 4.5 %in_grad_near.1 = (bf16[384,1536]{1,0:T(8,128)(2,1)S(1)}, bf16[384,1536]{1,0:T(8,128)(2,1)}) custom-call(s32[2]{0:T(128)S(1)} %pad_add_fusion.refs_0_, bf16[768,1024]{1,0:T(8,128)(2,1)S(1)} %copy-done.21, bf16[1024,3072]{1,0:T(8,128)(2,1)S(1)} %get-tuple-element.114.refs_2_.refs_1_, bf16[384,3072]{1,0:T(8,128)(2,1)S(1)} %collective-permute-done.refs_3_, ...), custom_call_target="tpu_custom_call" | custom-call | flops 49999998976 | bytes 1 | tf_op jit(solution)/shard_map/in_grad_near/pallas_call | solution.py:99
  121.8 13.5 %first_back.1 = (f32[1024,768]{1,0:T(8,128)}, bf16[1024,768]{1,0:T(8,128)(2,1)S(1)}, bf16[1024,768]{1,0:T(8,128)(2,1)S(1)}, f32[8,768]{1,0:T(8,128)S(1)}) custom-call(f32[1024,768]{1,0:T(8,128)S(1)} %copy-done.18, bf16[1024,3072]{1,0:T(8,128)(2,1)S(1)} %get-tuple-element.114.refs_2_.refs_1_, bf16[768,3072]{1,0:T(8,128)(2,1)} %refs_2_.11, ...), custom_call_target="tpu_custom_call" | custom-call | flops 49999998976 | bytes 1 | tf_op jit(solution)/shard_map/first_back/pallas_call | solution.py:99
  135.3 7.5 %attend_back.3 = (bf16[1024,768]{1,0:T(8,128)(2,1)S(1)}, f32[1,768]{1,0:T(1,128)S(1)}) custom-call(s32[1,2]{1,0:T(1,128)S(1)} %copy-done.10, s32[12]{0:T(128)S(1)} %copy-done.11, bf16[1024,256]{1,0:T(8,128)(2,1)} %get-tuple-element.95.refs_2_, bf16[1024,256]{1,0:T(8,128)(2,1)} %get-tuple-element.102.refs_3_, bf16[1024,256]{1,0:T(8,128)(2,1)} %get-tuple-element.103.refs_4_, ...), custom_call_target="tpu_custom_call" | custom-call | flops 49999998976 | bytes 1 | tf_op jit(solution)/shard_map/attend_back/pallas_call | solution.py:99
  151.7 7.8 %attend_back.4 = (bf16[1024,768]{1,0:T(8,128)(2,1)S(1)}, f32[1,768]{1,0:T(1,128)S(1)}) custom-call(s32[1,2]{1,0:T(1,128)S(1)} %copy-done.10, s32[12]{0:T(128)S(1)} %copy-done.11, bf16[1024,512]{1,0:T(8,128)(2,1)} %get-tuple-element.126.refs_2_, bf16[1024,512]{1,0:T(8,128)(2,1)} %get-tuple-element.127.refs_3_, bf16[1024,512]{1,0:T(8,128)(2,1)} %get-tuple-element.128.refs_4_, ...), custom_call_target="tpu_custom_call" | custom-call | flops 49999998976 | bytes 1 | tf_op jit(solution)/shard_map/attend_back/pallas_call | solution.py:99
  167.8 7.6 %attend_back.5 = (bf16[1024,768]{1,0:T(8,128)(2,1)S(1)}, f32[1,768]{1,0:T(1,128)S(1)}) custom-call(s32[1,2]{1,0:T(1,128)S(1)} %copy-done.10, s32[12]{0:T(128)S(1)} %copy-done.11, bf16[1024,512]{1,0:T(8,128)(2,1)} %get-tuple-element.126.refs_2_, bf16[1024,512]{1,0:T(8,128)(2,1)} %get-tuple-element.127.refs_3_, bf16[1024,512]{1,0:T(8,128)(2,1)} %get-tuple-element.128.refs_4_, ...), custom_call_target="tpu_custom_call" | custom-call | flops 49999998976 | bytes 1 | tf_op jit(solution)/shard_map/attend_back/pallas_call | solution.py:99
  194.7 8.3 %input_grad.1.refs_2_ = bf16[1024,768]{1,0:T(8,128)(2,1)} custom-call(bf16[1024,768]{1,0:T(8,128)(2,1)S(1)} %get-tuple-element.125.refs_4_.refs_0_, bf16[1024,768]{1,0:T(8,128)(2,1)S(1)} %get-tuple-element.137.refs_2_.refs_1_, bf16[1024,768]{1,0:T(8,128)(2,1)S(1)} %get-tuple-element.144.refs_4_.refs_2_, bf16[768,2304]{1,0:T(8,128)(2,1)} %refs_5_.9, ...), custom_call_target="tpu_custom_call" | custom-call | flops 49999998976 | bytes 1 | tf_op jit(solution)/shard_map/input_grad/pallas_call | solution.py:99
  203.7 4.1 %mixed_place.1.refs_2_ = bf16[896,768]{1,0:T(8,128)(2,1)} custom-call(s32[1,1024]{1,0:T(1,128)S(1)} %copy-done.32, bf16[1024,768]{1,0:T(8,128)(2,1)} %bitcast.7.refs_1_, bf16[1024,768]{1,0:T(8,128)(2,1)} %input_grad.1.refs_2_), custom_call_target="tpu_custom_call" | custom-call | flops 10000000000 | bytes 1 | tf_op jit(solution)/shard_map/mixed_place/pallas_call | solution.py:99
  223.9 6.7 %collective-permute-done.19.refs_1_ = bf16[96,1536]{1,0:T(8,128)(2,1)S(1)} collective-permute-done((bf16[96,1536]{1,0:T(8,128)(2,1)S(1)}, bf16[96,1536]{1,0:T(8,128)(2,1)S(1)}, u32[]{:S(2)}, u32[]{:S(2)}) %collective-permute-start.19) | collective-permute-done | bytes 294944 | tf_op jit(solution)/shard_map/ppermute | solution.py:700
  230.7 7.0 %collective-permute-done.18.refs_1_ = bf16[208,384]{1,0:T(8,128)(2,1)S(1)} collective-permute-done((bf16[208,384]{1,0:T(8,128)(2,1)S(1)}, bf16[208,384]{1,0:T(8,128)(2,1)S(1)}, u32[]{:S(2)}, u32[]{:S(2)}) %collective-permute-start.18) | collective-permute-done | bytes 159776 | tf_op jit(solution)/shard_map/ppermute | solution.py:700
  243.3 4.2 %collective-permute-done.22.refs_2_ = bf16[96,1536]{1,0:T(8,128)(2,1)S(1)} collective-permute-done((bf16[96,1536]{1,0:T(8,128)(2,1)S(1)}, bf16[96,1536]{1,0:T(8,128)(2,1)S(1)}, u32[]{:S(2)}, u32[]{:S(2)}) %collective-permute-start.22) | collective-permute-done | bytes 294944 | tf_op jit(solution)/shard_map/ppermute | solution.py:700
  251.6 4.3 %collective-permute-done.25.refs_2_ = bf16[768,384]{1,0:T(8,128)(2,1)S(1)} collective-permute-done((bf16[768,384]{1,0:T(8,128)(2,1)S(1)}, bf16[768,384]{1,0:T(8,128)(2,1)S(1)}, u32[]{:S(2)}, u32[]{:S(2)}) %collective-permute-start.25) | collective-permute-done | bytes 589856 | tf_op jit(solution)/shard_map/ppermute | solution.py:700
  259.1 9.3 %collective-permute-done.27.refs_2_ = bf16[192,1536]{1,0:T(8,128)(2,1)S(1)} collective-permute-done((bf16[192,1536]{1,0:T(8,128)(2,1)S(1)}, bf16[192,1536]{1,0:T(8,128)(2,1)S(1)}, u32[]{:S(2)}, u32[]{:S(2)}) %collective-permute-start.27) | collective-permute-done | bytes 589856 | tf_op jit(solution)/shard_map/ppermute | solution.py:700
  (150 shorter events, 85.6 us)
Async XLA Ops:
  2.5 17.9 %all-to-all-start = ((s32[32,1,32]{2,1,0:T(1,128)}), s32[32,1,32]{2,1,0:T(1,128)S(1)}, u32[]{:S(2)}, u32[]{:S(2)}) async-start(s32[32,1,32]{2,1,0:T(1,128)} %bitcast.2), calls=%async_computation | async-start | bytes 32768 | tf_op jit(solution)/shard_map/all_to_all | solution.py:814
  25.3 53.9 %all-to-all-start.2 = ((bf16[32,32,768]{2,1,0:T(8,128)(2,1)}), bf16[32,32,768]{2,1,0:T(8,128)(2,1)}, u32[]{:S(2)}, u32[]{:S(2)}) async-start(bf16[32,32,768]{2,1,0:T(8,128)(2,1)} %bitcast.8), calls=%async_computation.2 | async-start | bytes 3145728 | tf_op jit(solution)/shard_map/all_to_all | solution.py:853
  79.2 124.5 %all-to-all-start.1 = ((bf16[32,32,768]{2,1,0:T(8,128)(2,1)}), bf16[32,32,768]{2,1,0:T(8,128)(2,1)}, u32[]{:S(2)}, u32[]{:S(2)}) async-start(bf16[32,32,768]{2,1,0:T(8,128)(2,1)} %bitcast.6), calls=%async_computation.1 | async-start | bytes 3145728 | tf_op jit(solution)/shard_map/all_to_all | solution.py:909
  113.9 30.7 %collective-permute-start.2 = (bf16[768,768]{1,0:T(8,128)(2,1)}, bf16[768,768]{1,0:T(8,128)(2,1)}, u32[]{:S(2)}, u32[]{:S(2)}) collective-permute-start(bf16[768,768]{1,0:T(8,128)(2,1)} %get-tuple-element.121.refs_4_), channel_id=1, source_target_pairs={{0,16},{8,24},{16,0},{24,8},{1,17},{9,25},{17,1},{25,9},{2,18},{10... | collective-permute-start | bytes 3538952 | tf_op jit(solution)/shard_map/ppermute | solution.py:700
  120.3 44.2 %collective-permute-start.4 = (bf16[384,1536]{1,0:T(8,128)(2,1)}, bf16[384,1536]{1,0:T(8,128)(2,1)}, u32[]{:S(2)}, u32[]{:S(2)}) collective-permute-start(bf16[384,1536]{1,0:T(8,128)(2,1)} %get-tuple-element.139), channel_id=1, source_target_pairs={{0,1},{1,0},{2,3},{3,2},{4,5},{5,4},{6,7},{7,6},{8,9},{9,8},{10,11... | collective-permute-start | bytes 3538952 | tf_op jit(solution)/shard_map/ppermute | solution.py:700
  146.7 20.4 %collective-permute-start.3 = (bf16[768,384]{1,0:T(8,128)(2,1)S(1)}, bf16[768,384]{1,0:T(8,128)(2,1)S(1)}, u32[]{:S(2)}, u32[]{:S(2)}) collective-permute-start(bf16[768,384]{1,0:T(8,128)(2,1)S(1)} %get-tuple-element.138), channel_id=1, source_target_pairs={{0,1},{1,0},{2,3},{3,2},{4,5},{5,4},{6,7},{7,6},{8,9},{9,8},{10,11... | collective-permute-start | bytes 1769480 | tf_op jit(solution)/shard_map/ppermute | solution.py:700
  163.4 18.3 %collective-permute-start.9 = (bf16[384,768]{1,0:T(8,128)(2,1)S(1)}, bf16[384,768]{1,0:T(8,128)(2,1)S(1)}, u32[]{:S(2)}, u32[]{:S(2)}) collective-permute-start(bf16[384,768]{1,0:T(8,128)(2,1)S(1)} %get-tuple-element.141.refs_2_), channel_id=1, source_target_pairs={{0,16},{8,24},{16,0},{24,8},{1,17},{9,25},{17,1},{25,9},{2,18},{10... | collective-permute-start | bytes 1769480 | tf_op jit(solution)/shard_map/ppermute | solution.py:700
  166.0 25.8 %collective-permute-start.6 = (bf16[192,1536]{1,0:T(8,128)(2,1)S(1)}, bf16[192,1536]{1,0:T(8,128)(2,1)S(1)}, u32[]{:S(2)}, u32[]{:S(2)}) collective-permute-start(bf16[192,1536]{1,0:T(8,128)(2,1)S(1)} %get-tuple-element.142.refs_3_), channel_id=1, source_target_pairs={{0,16},{8,24},{16,0},{24,8},{1,17},{9,25},{17,1},{25,9},{2,18},{10... | collective-permute-start | bytes 1769480 | tf_op jit(solution)/shard_map/ppermute | solution.py:700
  175.4 9.3 %collective-permute-start.8 = (bf16[384,384]{1,0:T(8,128)(2,1)S(1)}, bf16[384,384]{1,0:T(8,128)(2,1)S(1)}, u32[]{:S(2)}, u32[]{:S(2)}) collective-permute-start(bf16[384,384]{1,0:T(8,128)(2,1)S(1)} %get-tuple-element.148), channel_id=1, source_target_pairs={{0,2},{1,3},{2,0},{3,1},{4,6},{5,7},{6,4},{7,5},{8,10},{9,11},{10,... | collective-permute-start | bytes 884744 | tf_op jit(solution)/shard_map/ppermute | solution.py:700
  182.4 29.6 %collective-permute-start.10 = (bf16[384,384]{1,0:T(8,128)(2,1)S(1)}, bf16[384,384]{1,0:T(8,128)(2,1)S(1)}, u32[]{:S(2)}, u32[]{:S(2)}) collective-permute-start(bf16[384,384]{1,0:T(8,128)(2,1)S(1)} %get-tuple-element.153), channel_id=1, source_target_pairs={{0,1},{1,0},{2,3},{3,2},{4,5},{5,4},{6,7},{7,6},{8,9},{9,8},{10,11... | collective-permute-start | bytes 884744 | tf_op jit(solution)/shard_map/ppermute | solution.py:700
  184.7 31.0 %collective-permute-start.14 = (bf16[384,384]{1,0:T(8,128)(2,1)S(1)}, bf16[384,384]{1,0:T(8,128)(2,1)S(1)}, u32[]{:S(2)}, u32[]{:S(2)}) collective-permute-start(bf16[384,384]{1,0:T(8,128)(2,1)S(1)} %w_down_a.1.refs_13_.refs_0_), channel_id=1, source_target_pairs={{0,4},{1,5},{2,6},{3,7},{4,0},{5,1},{6,2},{7,3},{8,12},{9,13},{10,... | collective-permute-start | bytes 884744 | tf_op jit(solution)/shard_map/ppermute | solution.py:700
  192.5 20.6 %collective-permute-start.15 = (bf16[96,1536]{1,0:T(8,128)(2,1)S(1)}, bf16[96,1536]{1,0:T(8,128)(2,1)S(1)}, u32[]{:S(2)}, u32[]{:S(2)}) collective-permute-start(bf16[96,1536]{1,0:T(8,128)(2,1)S(1)} %get-tuple-element.159), channel_id=1, source_target_pairs={{0,2},{1,3},{2,0},{3,1},{4,6},{5,7},{6,4},{7,5},{8,10},{9,11},{10,... | collective-permute-start | bytes 884744 | tf_op jit(solution)/shard_map/ppermute | solution.py:700
  194.7 15.7 %collective-permute-start.11 = (bf16[832,384]{1,0:T(8,128)(2,1)S(1)}, bf16[832,384]{1,0:T(8,128)(2,1)S(1)}, u32[]{:S(2)}, u32[]{:S(2)}) collective-permute-start(bf16[832,384]{1,0:T(8,128)(2,1)S(1)} %get-tuple-element.154), channel_id=1, source_target_pairs={{0,1},{1,0},{2,3},{3,2},{4,5},{5,4},{6,7},{7,6},{8,9},{9,8},{10,11... | collective-permute-start | bytes 1916936 | tf_op jit(solution)/shard_map/ppermute | solution.py:700
  213.2 17.4 %collective-permute-start.19 = (bf16[96,1536]{1,0:T(8,128)(2,1)S(1)}, bf16[96,1536]{1,0:T(8,128)(2,1)S(1)}, u32[]{:S(2)}, u32[]{:S(2)}) collective-permute-start(bf16[96,1536]{1,0:T(8,128)(2,1)S(1)} %w_in_a.1.refs_2_.refs_0_), channel_id=1, source_target_pairs={{0,4},{1,5},{2,6},{3,7},{4,0},{5,1},{6,2},{7,3},{8,12},{9,13},{10,... | collective-permute-start | bytes 884744 | tf_op jit(solution)/shard_map/ppermute | solution.py:700
  215.8 24.2 %collective-permute-start.17 = (bf16[384,384]{1,0:T(8,128)(2,1)S(1)}, bf16[384,384]{1,0:T(8,128)(2,1)S(1)}, u32[]{:S(2)}, u32[]{:S(2)}) collective-permute-start(bf16[384,384]{1,0:T(8,128)(2,1)S(1)} %w_down_f.1.refs_3_.refs_1_), channel_id=1, source_target_pairs={{0,2},{1,3},{2,0},{3,1},{4,6},{5,7},{6,4},{7,5},{8,10},{9,11},{10,... | collective-permute-start | bytes 884744 | tf_op jit(solution)/shard_map/ppermute | solution.py:700
  221.1 20.6 %collective-permute-start.16 = (bf16[192,384]{1,0:T(8,128)(2,1)S(1)}, bf16[192,384]{1,0:T(8,128)(2,1)S(1)}, u32[]{:S(2)}, u32[]{:S(2)}) collective-permute-start(bf16[192,384]{1,0:T(8,128)(2,1)S(1)} %attn_a_a.1.refs_2_.refs_0_), channel_id=1, source_target_pairs={{0,4},{1,5},{2,6},{3,7},{4,0},{5,1},{6,2},{7,3},{8,12},{9,13},{10,... | collective-permute-start | bytes 442376 | tf_op jit(solution)/shard_map/ppermute | solution.py:700
  221.4 16.3 %collective-permute-start.18 = (bf16[208,384]{1,0:T(8,128)(2,1)S(1)}, bf16[208,384]{1,0:T(8,128)(2,1)S(1)}, u32[]{:S(2)}, u32[]{:S(2)}) collective-permute-start(bf16[208,384]{1,0:T(8,128)(2,1)S(1)} %get-tuple-element.161), channel_id=1, source_target_pairs={{0,2},{1,3},{2,0},{3,1},{4,6},{5,7},{6,4},{7,5},{8,10},{9,11},{10,... | collective-permute-start | bytes 479240 | tf_op jit(solution)/shard_map/ppermute | solution.py:700
  230.7 16.8 %collective-permute-start.22 = (bf16[96,1536]{1,0:T(8,128)(2,1)S(1)}, bf16[96,1536]{1,0:T(8,128)(2,1)S(1)}, u32[]{:S(2)}, u32[]{:S(2)}) collective-permute-start(bf16[96,1536]{1,0:T(8,128)(2,1)S(1)} %w_in_f.1.refs_2_.refs_1_), channel_id=1, source_target_pairs={{0,2},{1,3},{2,0},{3,1},{4,6},{5,7},{6,4},{7,5},{8,10},{9,11},{10,... | collective-permute-start | bytes 884744 | tf_op jit(solution)/shard_map/ppermute | solution.py:700
  237.8 10.6 %collective-permute-start.21 = (bf16[208,384]{1,0:T(8,128)(2,1)S(1)}, bf16[208,384]{1,0:T(8,128)(2,1)S(1)}, u32[]{:S(2)}, u32[]{:S(2)}) collective-permute-start(bf16[208,384]{1,0:T(8,128)(2,1)S(1)} %attn_b_a.1.refs_3_.refs_0_), channel_id=1, source_target_pairs={{0,4},{1,5},{2,6},{3,7},{4,0},{5,1},{6,2},{7,3},{8,12},{9,13},{10,... | collective-permute-start | bytes 479240 | tf_op jit(solution)/shard_map/ppermute | solution.py:700
  240.6 15.2 %collective-permute-start.25 = (bf16[768,384]{1,0:T(8,128)(2,1)S(1)}, bf16[768,384]{1,0:T(8,128)(2,1)S(1)}, u32[]{:S(2)}, u32[]{:S(2)}) collective-permute-start(bf16[768,384]{1,0:T(8,128)(2,1)S(1)} %w_down_g.1.refs_2_.refs_1_), channel_id=1, source_target_pairs={{0,1},{1,0},{2,3},{3,2},{4,5},{5,4},{6,7},{7,6},{8,9},{9,8},{10,11... | collective-permute-start | bytes 1769480 | tf_op jit(solution)/shard_map/ppermute | solution.py:700
  248.1 20.4 %collective-permute-start.27 = (bf16[192,1536]{1,0:T(8,128)(2,1)S(1)}, bf16[192,1536]{1,0:T(8,128)(2,1)S(1)}, u32[]{:S(2)}, u32[]{:S(2)}) collective-permute-start(bf16[192,1536]{1,0:T(8,128)(2,1)S(1)} %w_in_g.1.refs_2_.refs_1_), channel_id=1, source_target_pairs={{0,1},{1,0},{2,3},{3,2},{4,5},{5,4},{6,7},{7,6},{8,9},{9,8},{10,11... | collective-permute-start | bytes 1769480 | tf_op jit(solution)/shard_map/ppermute | solution.py:700
  248.5 9.6 %collective-permute-start.24 = (bf16[208,384]{1,0:T(8,128)(2,1)S(1)}, bf16[208,384]{1,0:T(8,128)(2,1)S(1)}, u32[]{:S(2)}, u32[]{:S(2)}) collective-permute-start(bf16[208,384]{1,0:T(8,128)(2,1)S(1)} %attn_b_f.1.refs_3_.refs_1_), channel_id=1, source_target_pairs={{0,2},{1,3},{2,0},{3,1},{4,6},{5,7},{6,4},{7,5},{8,10},{9,11},{10,... | collective-permute-start | bytes 479240 | tf_op jit(solution)/shard_map/ppermute | solution.py:700
  251.2 22.0 %collective-permute-start.23 = (bf16[384,384]{1,0:T(8,128)(2,1)S(1)}, bf16[384,384]{1,0:T(8,128)(2,1)S(1)}, u32[]{:S(2)}, u32[]{:S(2)}) collective-permute-start(bf16[384,384]{1,0:T(8,128)(2,1)S(1)} %attn_a_g.1.refs_3_.refs_1_), channel_id=1, source_target_pairs={{0,1},{1,0},{2,3},{3,2},{4,5},{5,4},{6,7},{7,6},{8,9},{9,8},{10,11... | collective-permute-start | bytes 884744 | tf_op jit(solution)/shard_map/ppermute | solution.py:700
  258.6 17.9 %collective-permute-start.26 = (bf16[416,384]{1,0:T(8,128)(2,1)S(1)}, bf16[416,384]{1,0:T(8,128)(2,1)S(1)}, u32[]{:S(2)}, u32[]{:S(2)}) collective-permute-start(bf16[416,384]{1,0:T(8,128)(2,1)S(1)} %attn_b_g.1.refs_3_), channel_id=1, source_target_pairs={{0,1},{1,0},{2,3},{3,2},{4,5},{5,4},{6,7},{7,6},{8,9},{9,8},{10,11... | collective-permute-start | bytes 958472 | tf_op jit(solution)/shard_map/ppermute | solution.py:700
  (40 other events, 331.6 us)

commit v3 on v2

--- a/solution.py
+++ b/solution.py
@@ -14,7 +14,9 @@
 I32 = jnp.int32
 MIB = 1 << 20
 COST = 5e10
+COST_MID = 2e10
 COST_SMALL = 1e10
+COST_TINY = 1e9
 
 NN = (((1,), (0,)), ((), ()))
 NT = (((1,), (1,)), ((), ()))
@@ -101,10 +103,6 @@
         return outs
 
     return run
-
-
-def slot_of(rel):
-    return jnp.where(rel == 0, 3, jnp.where(rel == 3, 0, rel))
 
 
 def floor_div(values, divisor):
@@ -242,15 +240,15 @@
 
 
 def attend_kernel(
-    first, pairs, heads, ids_ref, len_ref, swap_ref, x_ref, wq_ref, wk_ref, wv_ref, b_ref, *refs
+    first, pairs, heads, len_ref, swap_ref, x_ref, wq_ref, wk_ref, wv_ref, b_ref, *refs
 ):
     if first == 0:
-        q_ref, k_ref, v_ref, ctx_ref, soft_ref, linv_ref, xt_ref = refs
+        q_ref, k_ref, v_ref, ctx_ref, soft_ref, linv_ref = refs
     else:
         (
             ctx0_ref, wo0_ref, wo_ref, ob_ref, gain_ref, shift_ref,
-            q_ref, k_ref, v_ref, ctx_ref, soft_ref, linv_ref, first_ref, normed_ref, inv_ref,
-            ctxt_ref, acc_ref, ctx_all,
+            q_ref, k_ref, v_ref, soft_ref, linv_ref, first_ref, normed_ref, inv_ref, ctx_all,
+            acc_ref,
         ) = refs
     cols = q_ref.shape[1]
     width = x_ref.shape[1]
@@ -264,18 +262,14 @@
         project(x_ref, (wq_ref, wk_ref, wv_ref), bq, bv, (q_ref, k_ref, v_ref))
 
     cut = pl.ds(pl.multiple_of(pair * 128, 128), 128)
+    if first > 0:
+        ctx_ref = ctx_all.at[:, pl.ds(pl.multiple_of(group * cols + pair * 128, 128), 128)]
     attend_pair(
         group * (pairs * heads) + pair * heads, heads, len_ref, swap_ref, q_ref, k_ref, v_ref, cut,
         ctx_ref, soft_ref, linv_ref,
     )
     if first == 0:
-
-        @pl.when(pair == pairs - 1)
-        def _():
-            write_turned(x_ref[...], ids_ref[0], xt_ref)
-
         return
-    ctx_all[:, pl.ds(pl.multiple_of(group * cols + pair * 128, 128), 128)] = ctx_ref[...]
 
     @pl.when(pair == pairs - 1)
     def _():
@@ -299,17 +293,6 @@
             inv_ref[...] = inverse
             out = normed * gain_ref[...].reshape(1, -1) + shift_ref[...].reshape(1, -1)
             first_ref[...] = out.astype(BF)
-            write_turned(ctx_all[...], ids_ref[0], ctxt_ref)
-
-
-def write_turned(values, seq_id, out_ref):
-    turned = values.T
-    quarter = turned.shape[0] // 4
-    for q in range(4):
-        at = slot_of(jnp.bitwise_xor(seq_id, q))
-        out_ref[pl.ds(pl.multiple_of(at * quarter, quarter), quarter), :] = turned[
-            q * quarter : (q + 1) * quarter
-        ]
 
 
 def block_cols(index, size):
@@ -317,8 +300,8 @@
 
 
 def ffn_kernel(
-    ids_ref, x_ref, wi_ref, bi_ref, wd_ref, bd_ref, gain_ref, shift_ref,
-    hid_ref, slope_ref, normed_ref, inv_ref, out_ref, xt_ref, acc_ref,
+    x_ref, wi_ref, bi_ref, wd_ref, bd_ref, gain_ref, shift_ref,
+    hid_ref, slope_ref, normed_ref, inv_ref, out_ref, acc_ref,
 ):
     step = pl.program_id(0)
     steps = pl.num_programs(0)
@@ -334,7 +317,6 @@
     @pl.when(step == 0)
     def _():
         acc_ref[...] = part_sum
-        write_turned(x, ids_ref[0], xt_ref)
 
     @pl.when(step > 0)
     def _():
@@ -373,16 +355,25 @@
     other_ref[...] = jnp.where(second, left, right)
 
 
-def quarter_at(step, ids_ref, near):
-    rel = jnp.where(step == 0, 2, 0) if near else jnp.where(step == 0, 3, 1)
+def quarter_at(step, ids_ref):
+    rel = jnp.where(step == 0, 3, jnp.where(step == 3, 0, step))
     return jnp.bitwise_xor(ids_ref[0], rel)
 
 
-def act_back(ids_ref, near, branch, wd_ref, slope_ref, act_ref, bias_ref):
-    own = block_cols(quarter_at(pl.program_id(0), ids_ref, near), wd_ref.shape[0])
-    g_act = (mm(branch, wd_ref[...], NT) * slope_ref[:, own].astype(F32)).astype(BF)
-    act_ref[:, own] = g_act
-    bias_ref[:, own] = jnp.sum(g_act.astype(F32), axis=0, keepdims=True)
+def store_quarters(ids_ref, grad, far_ref, near_ref, base, size, cols=slice(None)):
+    part = grad.shape[0] // 4
+    for q in range(4):
+        rel = jnp.bitwise_xor(ids_ref[0], q)
+        value = grad[q * part : (q + 1) * part]
+        rows = pl.ds(pl.multiple_of(jnp.where(rel < 2, size, 0) + base, 16), part)
+
+        @pl.when((rel & 1) == 1)
+        def _():
+            far_ref[rows, cols] = value
+
+        @pl.when((rel & 1) == 0)
+        def _():
+            near_ref[rows, cols] = value
 
 
 def cot_back_kernel(
@@ -403,41 +394,40 @@
     )
 
 
-def down_back_kernel(ids_ref, branch_ref, wd_ref, slope_ref, hid_ref, act_ref, bias_ref, gw_ref):
+def down_back_kernel(
+    ids_ref, branch_ref, wd_ref, slope_ref, hid_ref, act_ref, bias_ref, far_ref, near_ref
+):
+    step = pl.program_id(0)
     branch = branch_ref[...]
-    act_back(ids_ref, False, branch, wd_ref, slope_ref, act_ref, bias_ref)
-    own = block_cols(quarter_at(pl.program_id(0), ids_ref, False), wd_ref.shape[0])
-    gw_ref[pl.program_id(0)] = mm(hid_ref[:, own], branch, TN).astype(BF)
-
-
-def act_back_kernel(ids_ref, branch_ref, wd_ref, slope_ref, old_act, act_ref, bias_ref):
-    act_back(ids_ref, True, branch_ref[...], wd_ref, slope_ref, act_ref, bias_ref)
-
-
-def down_grad_kernel(ids_ref, hid_ref, branch_ref, mate_ref, send_ref, keep_ref):
-    step = pl.program_id(0)
-    own = block_cols(quarter_at(step, ids_ref, True), send_ref.shape[0])
-    grad = mm(hid_ref[:, own], branch_ref[...], TN).astype(BF).astype(F32)
-    total = (grad + mate_ref[step].astype(F32)).astype(BF)
-
-    @pl.when(step == 0)
-    def _():
-        send_ref[...] = total
-
-    @pl.when(step == 1)
-    def _():
-        keep_ref[...] = total
-
-
-def in_grad_kernel(near, ids_ref, xt_ref, act_ref, *refs):
-    half = xt_ref.shape[0] // 2
-    turned = xt_ref[half:, :] if near else xt_ref[:half, :]
-    grad = mm(turned, act_ref[...], NN).astype(BF)
-    if not near:
-        refs[0][...] = grad
-        return
-    mate_ref, mine_ref, other_ref = refs
-    total = (grad.astype(F32) + mate_ref[...].astype(F32)).astype(BF)
+    own = block_cols(quarter_at(step, ids_ref), wd_ref.shape[0])
+    g_act = (mm(branch, wd_ref[...], NT) * slope_ref[...].astype(F32)).astype(BF)
+    act_ref[:, own] = g_act
+    bias_ref[:, own] = jnp.sum(g_act.astype(F32), axis=0, keepdims=True)
+    grad = mm(hid_ref[...], branch, TN).astype(BF)
+
+    @pl.when(step < 2)
+    def _():
+        far_ref[step] = grad
+
+    @pl.when(step >= 2)
+    def _():
+        near_ref[step - 2] = grad
+
+
+def down_add_kernel(near_ref, mate_ref, send_ref, keep_ref):
+    for at, out_ref in enumerate((send_ref, keep_ref)):
+        out_ref[...] = (near_ref[at].astype(F32) + mate_ref[at].astype(F32)).astype(BF)
+
+
+def in_back_kernel(ids_ref, x_ref, act_ref, far_ref, near_ref):
+    blk = x_ref.shape[1]
+    own = block_cols(pl.program_id(0), blk)
+    grad = mm(x_ref[...], act_ref[:, own], TN).astype(BF)
+    store_quarters(ids_ref, grad, far_ref, near_ref, 0, blk // 4, own)
+
+
+def in_add_kernel(ids_ref, near_ref, mate_ref, mine_ref, other_ref):
+    total = (near_ref[...].astype(F32) + mate_ref[...].astype(F32)).astype(BF)
     store_halves(ids_ref, total, mine_ref, other_ref)
 
 
@@ -546,71 +536,52 @@
         out_ref[...] = acc_ref[...].astype(BF)
 
 
-def vector_rows(ids_ref, rel_of, rows_ref, base_of, vec_refs):
-    vec2_ref, bias_a, bias_b, vec1_ref, *qkv_refs = vec_refs
+def store_vectors(ids_ref, vec_refs, far_ref, near_ref, base, size):
+    vec2_ref, bias_ref, vec1_ref, *qkv_refs = vec_refs
     width = vec1_ref.shape[1]
     cols = width // len(qkv_refs)
+    part = width // 4
     wide = jnp.concatenate(
         [ref[:, :cols] for ref in qkv_refs] + [ref[:, 2 * cols :] for ref in qkv_refs], axis=1
     )
+    extra = size - base
     for q in range(4):
         rel = jnp.bitwise_xor(ids_ref[0], q)
-        odd = (rel & 1) == 1
-        hid_q = slice(q * (bias_a.shape[1] // 4), (q + 1) * (bias_a.shape[1] // 4))
-        rows = [jnp.where(odd, bias_a[:, hid_q], bias_b[:, hid_q])]
-        qv = width // 2
-        rows.append(wide[:, q * qv : (q + 1) * qv])
-        own = slice(q * (width // 4), (q + 1) * (width // 4))
+        rows = [bias_ref[:, q * width : (q + 1) * width]]
+        rows.append(wide[:, q * (width // 2) : (q + 1) * (width // 2)])
         for ref in (vec2_ref, vec1_ref):
-            for at in range(3):
-                rows.append(ref[at : at + 1, own])
-
-        def store(base):
-            for r, row in enumerate(rows):
-                rows_ref[base + r : base + r + 1, : row.shape[1]] = row
-
-        for want, base in zip(rel_of, base_of):
-            pl.when(rel == want)(functools.partial(store, base))
-
-
-def share_grad_kernel(near, y_first, count, extra, ids_ref, *refs):
+            rows += [ref[at : at + 1, q * part : (q + 1) * part] for at in range(3)]
+        rows = [jnp.pad(row, ((0, 0), (0, width - row.shape[1]))) for row in rows]
+        rows.append(jnp.zeros((extra - len(rows), width), F32))
+        block = jnp.concatenate(rows, axis=0).astype(BF)
+        at = pl.ds(pl.multiple_of(jnp.where(rel < 2, size, 0) + base, 16), extra)
+
+        @pl.when((rel & 1) == 1)
+        def _():
+            far_ref[at, :] = block
+
+        @pl.when((rel & 1) == 0)
+        def _():
+            near_ref[at, :] = block
+
+
+def share_grad_kernel(count, extra, ids_ref, *refs):
     pairs = [(refs[2 * at], refs[2 * at + 1]) for at in range(count)]
-    refs = refs[2 * count :]
-    part = pairs[0][0].shape[0] // 4
+    *vec_refs, far_ref, near_ref = refs[2 * count :]
+    part = pairs[0][0].shape[1] // 4
     size = count * part + extra
+    for at, (left_ref, right_ref) in enumerate(pairs):
+        grad = mm(left_ref[...], right_ref[...], TN).astype(BF)
+        store_quarters(ids_ref, grad, far_ref, near_ref, at * part, size)
     if extra:
-        *refs, rows_ref = refs
-    if near:
-        *vec_refs, mate_ref, left_ref, right_ref = refs
-    else:
-        *vec_refs, out_ref = refs
-
-    def put(base, value):
-        rows = slice(base, base + value.shape[0])
-        if near:
-            value = value.astype(F32) + mate_ref[rows, :].astype(F32)
-        value = value.astype(BF)
-        if not near:
-            out_ref[rows, :] = value
-        elif y_first:
-            store_halves(ids_ref, value, left_ref.at[rows], right_ref.at[rows])
-        else:
-            out = left_ref if base < size else right_ref
-            base -= 0 if base < size else size
-            out[base : base + value.shape[0], :] = value
-
-    for at, (turned_ref, product_ref) in enumerate(pairs):
-        cut = 2 * part
-        turned = turned_ref[cut:, :] if near else turned_ref[:cut, :]
-        grad = mm(turned, product_ref[...], NN).astype(BF)
-        put(at * part, grad[:part])
-        put(size + at * part, grad[part:])
-    if extra:
-        rows_ref[...] = jnp.zeros_like(rows_ref)
-        vector_rows(ids_ref, (2, 0) if near else (3, 1), rows_ref, (0, extra), vec_refs)
-        for half in range(2):
-            vectors = rows_ref[half * extra : (half + 1) * extra, :].astype(BF)
-            put(half * size + count * part, vectors)
+        store_vectors(ids_ref, vec_refs, far_ref, near_ref, count * part, size)
+
+
+def share_add_kernel(near_ref, mate_ref, send_ref, keep_ref):
+    size = send_ref.shape[0]
+    total = (near_ref[...].astype(F32) + mate_ref[...].astype(F32)).astype(BF)
+    send_ref[...] = total[:size]
+    keep_ref[...] = total[size:]
 
 
 def split_cols_kernel(ids_ref, keep_ref, got_ref, mine_ref, other_ref):
@@ -700,7 +671,7 @@
     return lax.ppermute(values, axis, [(i, i ^ mask) for i in range(count)])
 
 
-def simple(chain, body, name, args, out_shape, prefetch=0, vmem=12, scratch=(), cost=COST_SMALL):
+def simple(chain, body, name, args, out_shape, prefetch=0, vmem=12, scratch=(), cost=COST_SMALL, free=()):
     tensors = args[prefetch:]
     return call(
         chain,
@@ -713,6 +684,7 @@
         prefetch=prefetch,
         vmem=vmem,
         cost=cost,
+        free=free,
         scratch=scratch,
     )(*args)
 
@@ -735,10 +707,10 @@
         )
         self.got = exchange(send, "seq", 2)
 
-    def halve(self, kernel, shape, label, mask):
+    def halve(self, kernel, shape, label, mask, cost=COST_SMALL):
         self.keep, other = simple(
             self.chain, kernel, self.name + label, (self.ids, self.keep, self.got),
-            [vmem(shape, BF)] * 2, 1,
+            [vmem(shape, BF)] * 2, 1, cost=cost,
         )
         self.got = exchange(other, "batch", mask)
 
@@ -746,20 +718,20 @@
         rows, cols = self.shape
         self.halve(split_cols_kernel, (rows, cols // 2), "_y", 1)
 
-    def step_z(self):
+    def step_z(self, cost=COST_SMALL):
         rows, cols = self.shape
-        self.halve(split_rows_kernel, (rows // 2, cols // 2), "_z", 2)
-
-    def add(self, label):
+        self.halve(split_rows_kernel, (rows // 2, cols // 2), "_z", 2, cost)
+
+    def add(self, label, cost=COST_SMALL):
         (self.keep,) = simple(
             self.chain, add_kernel, self.name + label, (self.keep, self.got),
-            [vmem(self.keep.shape, BF)],
+            [vmem(self.keep.shape, BF)], cost=cost,
         )
 
-    def step_far(self):
+    def step_far(self, cost=COST_SMALL):
         mask = 4
         while mask <= lax.axis_size("batch") // 2:
-            self.add("_a")
+            self.add("_a", cost)
             self.got = exchange(self.keep, "batch", mask)
             mask *= 2
 
@@ -814,7 +786,6 @@
     in_target = lax.all_to_all(out_target, ("seq", "batch"), split_axis=0, concat_axis=0, tiled=True)
 
     bf_rows = (rows, width)
-    turned_shape = (width, rows)
     vec_spec = whole_block((width,))
     steps = heads // pair
     some = lambda count, dtype: hbm((rows, count * cols), dtype)
@@ -826,21 +797,20 @@
     head_shapes = lambda count: [some(count, BF)] * 4 + [
         hbm((count * heads, 2, half, half), BF), some(count, F32)
     ]
-    head_args = (ids, seq_lengths, head_swap, hidden_in, w_qkv, w_qkv, w_qkv, qv_bias)
+    head_args = (seq_lengths, head_swap, hidden_in, w_qkv, w_qkv, w_qkv, qv_bias)
     head_specs = lambda first: [
         smem(), smem(), whole_block(bf_rows), col(first), col(groups + first),
         col(2 * groups + first), whole_block((2 * width,)),
     ]
-    *first_heads, x_turned = call(
+    first_heads = call(
         chain,
         functools.partial(attend_kernel, 0, steps, pair),
         "attend_first",
         vmem=32,
         grid=(1, steps),
         in_specs=head_specs(0),
-        out_specs=head_outs + [whole_block(turned_shape)],
-        out_shape=head_shapes(1) + [hbm(turned_shape, BF)],
-        prefetch=1,
+        out_specs=head_outs,
+        out_shape=head_shapes(1),
     )(*head_args)
     context0, linv0 = first_heads[3], first_heads[5]
     cot_out, in_row = simple(
@@ -851,7 +821,7 @@
         [sds((slots, width), BF), sds((1, slots), I32)],
     )
     cot_in = lax.all_to_all(cot_out, ("seq", "batch"), split_axis=0, concat_axis=0, tiled=True)
-    *rest_heads, first_low, normed1, inv1, ctx_turned = call(
+    *rest_heads, first_low, normed1, inv1, context = call(
         chain,
         functools.partial(attend_kernel, 1, steps, pair),
         "attend_rest",
@@ -862,22 +832,18 @@
             whole_block((rows, cols)), pl.BlockSpec((cols, width), lambda g, p, *_: (0, 0)),
             pl.BlockSpec((cols, width), lambda g, p, *_: (1 + g, 0)), vec_spec, vec_spec, vec_spec,
         ],
-        out_specs=head_outs
-        + [
-            whole_block(bf_rows), whole_block(bf_rows), whole_block((rows, 1)),
-            whole_block(turned_shape),
-        ],
-        out_shape=head_shapes(groups - 1)
-        + [hbm(bf_rows, BF), hbm(bf_rows, BF), hbm((rows, 1), F32), hbm(turned_shape, BF)],
-        scratch=[pltpu.VMEM(bf_rows, F32), pltpu.VMEM(bf_rows, BF)],
-        prefetch=1,
+        out_specs=head_outs[:3] + head_outs[4:]
+        + [whole_block(bf_rows), whole_block(bf_rows), whole_block((rows, 1)), whole_block(bf_rows)],
+        out_shape=head_shapes(groups - 1)[:3] + head_shapes(groups - 1)[4:]
+        + [hbm(bf_rows, BF), hbm(bf_rows, BF), hbm((rows, 1), F32), hbm(bf_rows, BF)],
+        scratch=[pltpu.VMEM(bf_rows, F32)],
     )(*head_args, context0, w_out, w_out, out_bias, norm1_gain, norm1_bias)
-    linv_rest = rest_heads[5]
+    linv_rest = rest_heads[4]
 
     blk = ff // 4
     act_shape = (rows, ff)
     act_col = pl.BlockSpec((rows, blk), lambda j, *_: (0, j))
-    hid, slope, normed2, inv2, mixed_home, first_turned = call(
+    hid, slope, normed2, inv2, mixed_home = call(
         chain,
         ffn_kernel,
         "ffn",
@@ -892,24 +858,19 @@
         ],
         out_specs=[
             act_col, act_col, whole_block(bf_rows), whole_block((rows, 1)), whole_block(bf_rows),
-            whole_block(turned_shape),
         ],
         out_shape=[
             hbm(act_shape, BF), hbm(act_shape, BF), hbm(bf_rows, BF), hbm((rows, 1), F32),
-            hbm(bf_rows, BF), hbm(turned_shape, BF),
+            hbm(bf_rows, BF),
         ],
         scratch=[pltpu.VMEM(bf_rows, F32)],
-        prefetch=1,
-    )(ids, first_low, w_in, in_bias, w_down, down_bias, norm2_gain, norm2_bias)
+    )(first_low, w_in, in_bias, w_down, down_bias, norm2_gain, norm2_bias)
 
     (mixed_out,) = simple(
         chain, place_kernel, "mixed_slots", (slot_row, mixed_home), [sds((slots, width), BF)],
         cost=COST,
     )
     mixed_in = lax.all_to_all(mixed_out, ("seq", "batch"), split_axis=0, concat_axis=0, tiled=True)
-
-    def wd_spec(near):
-        return pl.BlockSpec((blk, width), lambda j, ids_ref: (quarter_at(j, ids_ref, near), 0))
 
     g_pre2, g_branch, vec2 = simple(
         chain,
@@ -920,81 +881,53 @@
         vmem=24,
         cost=COST,
     )
-    act_half, bias_a, gwd_far = call(
+    part = width // 4
+    quarter_rows = pl.BlockSpec((blk, width), lambda j, i: (quarter_at(j, i), 0))
+    quarter_cols = pl.BlockSpec((rows, blk), lambda j, i: (0, quarter_at(j, i)))
+    down_shape = (2, blk, width)
+    g_act, bias_row, gwd_far, gwd_near = call(
         chain,
         down_back_kernel,
         "down_back",
-        vmem=16,
-        grid=(2,),
-        in_specs=[
-            whole_block(bf_rows), wd_spec(False), whole_block(act_shape), whole_block(act_shape),
+        vmem=24,
+        grid=(4,),
+        in_specs=[whole_block(bf_rows), quarter_rows, quarter_cols, quarter_cols],
+        out_specs=[
+            whole_block(act_shape), whole_block((1, ff)), whole_block(down_shape),
+            whole_block(down_shape),
         ],
-        out_specs=[whole_block(act_shape), whole_block((1, ff)), whole_block((2, blk, width))],
-        out_shape=[vmem(act_shape, BF), sds((1, ff), F32), vmem((2, blk, width), BF)],
+        out_shape=[
+            vmem(act_shape, BF), sds((1, ff), F32), vmem(down_shape, BF), vmem(down_shape, BF),
+        ],
         prefetch=1,
         free=(3, 4),
     )(ids, g_branch, w_down, slope, hid)
     gwd_mate = exchange(gwd_far, "seq", 1)
-    g_act, bias_b = call(
-        chain,
-        act_back_kernel,
-        "act_back",
-        vmem=10,
-        grid=(2,),
-        in_specs=[
-            whole_block(bf_rows), wd_spec(True), whole_block(act_shape), whole_block(act_shape),
-        ],
-        out_specs=[whole_block(act_shape), whole_block((1, ff))],
-        out_shape=[vmem(act_shape, BF), sds((1, ff), F32)],
-        prefetch=1,
-        aliases={4: 0},
-        free=(3,),
-    )(ids, g_branch, w_down, slope, act_half)
-    part = width // 4
-    gwi_shape = (2 * part, ff)
-    gwi_far = call(
-        chain,
-        functools.partial(in_grad_kernel, False),
-        "in_grad_far",
-        vmem=8,
-        grid=(1,),
-        in_specs=[whole_block(turned_shape), whole_block(act_shape)],
-        out_specs=whole_block(gwi_shape),
-        out_shape=vmem(gwi_shape, BF),
+    in_shape = (2 * part, ff)
+    gwi_far, gwi_near = call(
+        chain,
+        in_back_kernel,
+        "in_back",
+        vmem=16,
+        grid=(4,),
+        in_specs=[whole_block(bf_rows), whole_block(act_shape)],
+        out_specs=[whole_block(in_shape)] * 2,
+        out_shape=[vmem(in_shape, BF)] * 2,
         prefetch=1,
         free=(1,),
-    )(ids, first_turned, g_act)
+    )(ids, first_low, g_act)
     gwi_mate = exchange(gwi_far, "seq", 1)
-    share_shape = (blk, width)
-    send, keep = call(
-        chain,
-        down_grad_kernel,
-        "down_grad",
-        vmem=10,
-        grid=(2,),
-        in_specs=[whole_block(act_shape), whole_block(bf_rows), whole_block((2, blk, width))],
-        out_specs=[whole_block(share_shape)] * 2,
-        out_shape=[vmem(share_shape, BF)] * 2,
-        prefetch=1,
-        free=(1,),
-    )(ids, hid, g_branch, gwd_mate)
+    send, keep = simple(
+        chain, down_add_kernel, "w_down_c", (gwd_near, gwd_mate), [vmem((blk, width), BF)] * 2,
+        cost=COST,
+    )
     down_share = Share(chain, ids, "w_down", send, keep)
 
-
-    in_share_shape = (2 * part, ff // 2)
-    send, keep = call(
-        chain,
-        functools.partial(in_grad_kernel, True),
-        "in_grad_near",
-        vmem=8,
-        grid=(1,),
-        in_specs=[whole_block(turned_shape), whole_block(act_shape), whole_block(gwi_shape)],
-        out_specs=[whole_block(in_share_shape)] * 2,
-        out_shape=[vmem(in_share_shape, BF)] * 2,
-        prefetch=1,
-        free=(1,),
-    )(ids, first_turned, g_act, gwi_mate)
-    in_share = Share(chain, ids, "w_in", send, keep, y_first=True)
+    mine, other = simple(
+        chain, in_add_kernel, "w_in_c", (ids, gwi_near, gwi_mate),
+        [vmem((2 * part, ff // 2), BF)] * 2, 1,
+    )
+    in_share = Share(chain, ids, "w_in", mine, other, y_first=True)
 
     g_pre1, g_attn, g_ctx, vec1 = call(
         chain,
@@ -1022,7 +955,7 @@
 
     def group_back(g):
         own_col = pl.BlockSpec((rows, 128), lambda p: (0, g * steps + p))
-        arrays, base = (first_heads, 0) if g == 0 else (rest_heads, g - 1)
+        arrays, base = (first_heads[:3] + first_heads[4:], 0) if g == 0 else (rest_heads, g - 1)
         head_col = pl.BlockSpec((rows, 128), lambda p: (0, base * steps + p))
         proj, vec = call(
             chain,
@@ -1033,12 +966,12 @@
             in_specs=[
                 smem(), smem(), head_col, head_col, head_col,
                 pl.BlockSpec((pair, 2, half, half), lambda p: (base * steps + p, 0, 0, 0)),
-                own_col, head_col,
+                own_col, own_col,
             ],
             out_specs=[whole_block((rows, 3 * cols)), whole_block((1, 3 * cols))],
             out_shape=[vmem((rows, 3 * cols), BF), sds((1, 3 * cols), F32)],
             scratch=[pltpu.VMEM((rows, 128), F32)] * 3,
-        )(seq_lengths, head_swap, *arrays[:3], arrays[4], g_ctx, arrays[3])
+        )(seq_lengths, head_swap, *arrays[:4], g_ctx, context)
         projs.append(proj)
         vecs.append(vec)
 
@@ -1046,49 +979,50 @@
         extra = 32 if vec_ins else 0
         size = len(pairs) * part + extra
         flat = [a for both in pairs for a in both]
-        scratch = [pltpu.VMEM((2 * extra, width), F32)] if extra else []
-        (far_grad,) = simple(
+        far_grad, near_grad = simple(
             chain,
-            functools.partial(share_grad_kernel, False, y_first, len(pairs), extra),
-            name + "_far",
+            functools.partial(share_grad_kernel, len(pairs), extra),
+            name + "_w",
             (ids, *flat, *vec_ins),
-            [vmem((2 * size, width), BF)],
+            [vmem((2 * size, width), BF)] * 2,
             1,
-            scratch=scratch,
+            vmem=20,
+            cost=COST,
+            free=(1, 3),
         )
         mate = exchange(far_grad, "seq", 1)
 
         def near_part():
-            shape = (2 * size, width // 2) if y_first else (size, width)
-            left, right = simple(
-                chain,
-                functools.partial(share_grad_kernel, True, y_first, len(pairs), extra),
-                name + "_near",
-                (ids, *flat, *vec_ins, mate),
-                [vmem(shape, BF)] * 2,
-                1,
-                scratch=scratch,
-            )
-            return Share(chain, ids, name, left, right, y_first)
+            if y_first:
+                outs = simple(
+                    chain, in_add_kernel, name + "_c", (ids, near_grad, mate),
+                    [vmem((2 * size, width // 2), BF)] * 2, 1,
+                )
+            else:
+                outs = simple(
+                    chain, share_add_kernel, name + "_c", (near_grad, mate),
+                    [vmem((size, width), BF)] * 2,
+                )
+            return Share(chain, ids, name, *outs, y_first)
 
         return near_part
 
     group_back(0)
     down_share.step_y()
-    start_a = attention_share([(ctx_turned, g_attn), (x_turned, projs[0])], [], "attn_a", False)
+    start_a = attention_share([(context, g_attn), (hidden_in, projs[0])], [], "attn_a", False)
     group_back(1)
+    in_share.step_x()
     share_a = start_a()
-    in_share.step_x()
     down_share.step_z()
     group_back(2)
-    vec_ins = [vec2, bias_a, bias_b, vec1, *vecs]
+    down_share.step_far()
+    in_share.step_z()
+    vec_ins = [vec2, bias_row, vec1, *vecs]
     start_b = attention_share(
-        [(x_turned, projs[1]), (x_turned, projs[2])], vec_ins, "attn_b", True
-    )
-    share_a.step_y()
-    down_share.step_far()
+        [(hidden_in, projs[1]), (hidden_in, projs[2])], vec_ins, "attn_b", True
+    )
+    in_share.step_far(COST_MID)
     share_b = start_b()
-    in_share.step_z()
     input_grad = call(
         chain,
         functools.partial(input_grad_kernel, groups),
@@ -1110,20 +1044,20 @@
         chain, place_kernel, "mixed_place", (in_row, mixed_in), [hbm((ffn_rows, width), BF)]
     )
     share_b.step_x()
+    down_share.step_back()
+    share_a.step_y()
+    in_share.step_back()
+    share_b.step_z()
+    down_share.step_wide()
     share_a.step_z()
-    in_share.step_far()
-    down_share.step_back()
-    share_b.step_z()
+    share_b.step_far()
+    in_share.step_wide()
     share_a.step_far()
-    in_share.step_back()
-    share_b.step_far()
-    down_share.step_wide()
+    share_b.step_back()
     share_a.step_back()
-    in_share.step_wide()
-    share_b.step_back()
-    share_a.step_wide()
     g_w_down = down_share.join()
     share_b.step_wide()
+    share_a.step_wide()
     g_w_in = in_share.join()
     one = lambda size: sds((size,), F32)
     g_w_qkv, g_w_out, g_qv, g_in_bias, g_n2g, g_n2b, g_down_bias, g_n1g, g_n1b, g_out_bias = simple(

time: 284 us -> 259 us (0.912)
  waiting for transfers between devices: 49.5 us -> 33.2 us
  Pallas kernels: 177 us -> 167 us
    ppermute x28, waiting for transfers between devices: 49.5 us -> 33.2 us  [exchange(): return lax.ppermute(values, axis, [(i, i ^ mask) for i in range(count)])]
    pallas_call x45 -> x44, Pallas kernels: 177 us -> 167 us  [run(): outs = kernel(*placed, *[chain.place(a) for a in before])]
  transfers between devices with their start and end apart: 31 -> 31, of which waited for: 14 -> 11; matrix products, arithmetic and copies ran while one was open for 0% -> 0% of each run, Pallas kernels for 61% -> 63%
where the time goes in v3:
time: 259 us; the launch traced here: 254 us
  Pallas kernels  167 us (64%)
  starting transfers between devices  50.6 us (20%)
  waiting for transfers between devices  33.2 us (13%)
    pallas_call x44, Pallas kernels, run(): outs = kernel(*placed, *[chain.place(a) for a in before])  167 us
    ppermute x28, waiting for transfers between devices, exchange(): return lax.ppermute(values, axis, [(i, i ^ mask) for i in range(count)])  33.2 us
    ppermute x28, starting transfers between devices, exchange(): return lax.ppermute(values, axis, [(i, i ^ mask) for i in range(count)])  30.9 us
    all_to_all x1, starting transfers between devices, body(): lax.all_to_all(out_target, ('seq', 'batch'), split_axis=0, concat_axis=0,...  7.29 us
    all_to_all x1, starting transfers between devices, body(): lax.all_to_all(mixed_out, ('seq', 'batch'), split_axis=0, concat_axis=0,...  6.26 us
    all_to_all x1, starting transfers between devices, body(): lax.all_to_all(cot_out, ('seq', 'batch'), split_axis=0, concat_axis=0, ti...  6.12 us
  transfers between devices with their start and end apart: 31, of which 11 were waited for; matrix products, arithmetic and copies ran while one was open for 0% of the time, Pallas kernels for 63%

profile of v3, /device:TPU:0, one launch (start us, length us, event | category | flops | bytes accessed | tf_op | source)
XLA Modules:
  0.0 253.8 jit_solution(9929173288723295205)
XLA Ops:
  2.5 7.3 %all-to-all-start = ((s32[32,1,32]{2,1,0:T(1,128)}), s32[32,1,32]{2,1,0:T(1,128)S(1)}, u32[]{:S(2)}, u32[]{:S(2)}) async-start(s32[32,1,32]{2,1,0:T(1,128)} %bitcast.2), calls=%async_computation | async-start | bytes 32768 | tf_op jit(solution)/shard_map/all_to_all | solution.py:786
  9.8 8.3 %attend_first.1 = (bf16[1024,256]{1,0:T(8,128)(2,1)}, bf16[1024,256]{1,0:T(8,128)(2,1)}, bf16[1024,256]{1,0:T(8,128)(2,1)}, bf16[1024,256]{1,0:T(8,128)(2,1)}, b...) custom-call(s32[1,2]{1,0:T(1,128)S(1)} %copy-done.12, s32[12]{0:T(128)S(1)} %copy-done.13, ...), custom_call_target="tpu_custom_call" | custom-call | flops 49999998976 | bytes 1 | tf_op jit(solution)/shard_map/attend_first/pallas_call | solution.py:101
  18.2 4.8 %cot_gather.1 = (bf16[1024,768]{1,0:T(8,128)(2,1)}, s32[1,1024]{1,0:T(1,128)S(1)}) custom-call(s32[32,32]{1,0:T(8,128)S(1)} %bitcast.11, bf16[896,768]{1,0:T(8,128)(2,1)} %refs_1_.9, bf16[1024,256]{1,0:T(8,128)(2,1)} %get-tuple-element.97.refs_2_), custom_call_target="tpu_custom_call" | custom-call | flops 10000000000 | bytes 1 | tf_op jit(solution)/shard_map/cot_gather/pallas_call | solution.py:101
  23.0 6.1 %all-to-all-start.2 = ((bf16[32,32,768]{2,1,0:T(8,128)(2,1)}), bf16[32,32,768]{2,1,0:T(8,128)(2,1)}, u32[]{:S(2)}, u32[]{:S(2)}) async-start(bf16[32,32,768]{2,1,0:T(8,128)(2,1)} %bitcast.6), calls=%async_computation.2 | async-start | bytes 3145728 | tf_op jit(solution)/shard_map/all_to_all | solution.py:823
  29.2 19.7 %attend_rest.1 = (bf16[1024,512]{1,0:T(8,128)(2,1)}, bf16[1024,512]{1,0:T(8,128)(2,1)}, bf16[1024,512]{1,0:T(8,128)(2,1)}, bf16[8,2,512,512]{3,2,1,0:T(8,128)(2,...) custom-call(s32[1,2]{1,0:T(1,128)S(1)} %copy-done.12, ...), custom_call_target="tpu_custom_call" | custom-call | flops 49999998976 | bytes 1 | tf_op jit(solution)/shard_map/attend_rest/pallas_call | solution.py:101
  49.0 20.6 %ffn.1 = (bf16[1024,3072]{1,0:T(8,128)(2,1)}, bf16[1024,3072]{1,0:T(8,128)(2,1)}, bf16[1024,768]{1,0:T(8,128)(2,1)}, f32[1024,1]{1,0:T(8,128)}, bf16[1024,768]{1,0:T(8,128)(2,1)}) custom-call(bf16[1024,768]{1,0:T(8,128)(2,1)} %get-tuple-element.100.refs_0_.refs_1_, bf16[768,3072]{1,0:T(8,128)(2,1)} %refs_2_.9, f32[3072]{0:T(1024)S(1)} %copy-done.3, ...), custom_call_target="tpu_custom_call" | custom-call | flops 49999998976 | bytes 1 | tf_op jit(solution)/shard_map/ffn/pallas_call | solution.py:101
  69.6 4.4 %mixed_slots.1.refs_5_ = bf16[1024,768]{1,0:T(8,128)(2,1)} custom-call(s32[1,1024]{1,0:T(1,128)S(1)} %get-tuple-element.96.refs_7_.refs_0_, bf16[1024,768]{1,0:T(8,128)(2,1)} %get-tuple-element.102.refs_1_, f32[1024,1]{1,0:T(8,128)} %get-tuple-element.103.refs_2_.refs_3_), custom_call_target="tpu_custom_call" | custom-call | flops 49999998976 | bytes 1 | tf_op jit(solution)/shard_map/mixed_slots/pallas_call | solution.py:101
  74.0 6.3 %all-to-all-start.1 = ((bf16[32,32,768]{2,1,0:T(8,128)(2,1)}), bf16[32,32,768]{2,1,0:T(8,128)(2,1)}, u32[]{:S(2)}, u32[]{:S(2)}) async-start(bf16[32,32,768]{2,1,0:T(8,128)(2,1)} %bitcast.4), calls=%async_computation.1 | async-start | bytes 3145728 | tf_op jit(solution)/shard_map/all_to_all | solution.py:873
  80.3 7.2 %cot_back.1 = (f32[1024,768]{1,0:T(8,128)}, bf16[1024,768]{1,0:T(8,128)(2,1)S(1)}, f32[8,768]{1,0:T(8,128)S(1)}) custom-call(s32[1,1024]{1,0:T(1,128)S(1)} %get-tuple-element.96.refs_7_.refs_0_, bf16[1024,768]{1,0:T(8,128)(2,1)} %bitcast.7.refs_1_, bf16[1024,768]{1,0:T(8,128)(2,1)} %get-tuple-element.108.refs_2_, ...), custom_call_target="tpu_custom_call" | custom-call | flops 49999998976 | bytes 1 | tf_op jit(solution)/shard_map/cot_back/pallas_call | solution.py:101
  87.5 13.6 %down_back.1 = (bf16[1024,3072]{1,0:T(8,128)(2,1)S(1)}, f32[1,3072]{1,0:T(1,128)S(1)}, bf16[2,768,768]{2,1,0:T(8,128)(2,1)S(1)}, bf16[2,768,768]{2,1,0:T(8,128)(2,1)S(1)}) custom-call(s32[2]{0:T(128)S(1)} %pad_add_fusion.refs_0_, bf16[1024,768]{1,0:T(8,128)(2,1)S(1)} %get-tuple-element.110.refs_1_, bf16[3072,768]{1,0:T(8,128)(2,1)} %refs_2_.8, ...), custom_call_target="tpu_custom_call" | custom-call | flops 49999998976 | bytes 1 | tf_op jit(solution)/shard_map/down_back/pallas_call | solution.py:101
  101.5 7.0 %in_back.1 = (bf16[384,3072]{1,0:T(8,128)(2,1)S(1)}, bf16[384,3072]{1,0:T(8,128)(2,1)S(1)}) custom-call(s32[2]{0:T(128)S(1)} %pad_add_fusion.refs_0_, bf16[1024,768]{1,0:T(8,128)(2,1)S(1)} %copy-done.22, bf16[1024,3072]{1,0:T(8,128)(2,1)S(1)} %get-tuple-element.114.refs_2_.refs_1_, f32[1,3072]{1,0:T(1,128)S(1)} %get-tuple-element.118.refs_3_.refs_6_), custom_call_target="tpu_custom_call" | custom-call | flops 49999998976 | bytes 1 | tf_op jit(solution)/shard_map/in_back/pallas_call | solution.py:101
  117.1 13.7 %first_back.1 = (f32[1024,768]{1,0:T(8,128)}, bf16[1024,768]{1,0:T(8,128)(2,1)S(1)}, bf16[1024,768]{1,0:T(8,128)(2,1)S(1)}, f32[8,768]{1,0:T(8,128)S(1)}) custom-call(f32[1024,768]{1,0:T(8,128)S(1)} %copy-done.16, bf16[1024,3072]{1,0:T(8,128)(2,1)S(1)} %get-tuple-element.114.refs_2_.refs_1_, bf16[768,3072]{1,0:T(8,128)(2,1)} %refs_2_.9, ...), custom_call_target="tpu_custom_call" | custom-call | flops 49999998976 | bytes 1 | tf_op jit(solution)/shard_map/first_back/pallas_call | solution.py:101
  130.8 7.5 %attend_back.3 = (bf16[1024,768]{1,0:T(8,128)(2,1)S(1)}, f32[1,768]{1,0:T(1,128)S(1)}) custom-call(s32[1,2]{1,0:T(1,128)S(1)} %copy-done.12, s32[12]{0:T(128)S(1)} %copy-done.13, bf16[1024,256]{1,0:T(8,128)(2,1)} %get-tuple-element.97.refs_2_, bf16[1024,256]{1,0:T(8,128)(2,1)} %get-tuple-element.104.refs_3_, bf16[1024,256]{1,0:T(8,128)(2,1)} %get-tuple-element.105.refs_4_, ...), custom_call_target="tpu_custom_call" | custom-call | flops 49999998976 | bytes 1 | tf_op jit(solution)/shard_map/attend_back/pallas_call | solution.py:101
  141.5 4.5 %attn_a_w.1 = (bf16[768,768]{1,0:T(8,128)(2,1)S(1)}, bf16[768,768]{1,0:T(8,128)(2,1)S(1)}) custom-call(s32[2]{0:T(128)S(1)} %pad_add_fusion.refs_0_, bf16[1024,768]{1,0:T(8,128)(2,1)S(1)} %copy-done.21, bf16[1024,768]{1,0:T(8,128)(2,1)S(1)} %get-tuple-element.133.refs_2_, bf16[1024,768]{1,0:T(8,128)(2,1)S(1)} %copy-done, ...), custom_call_target="tpu_custom_call" | custom-call | flops 49999998976 | bytes 1 | tf_op jit(solution)/shard_map/attn_a_w/pallas_call | solution.py:101
  146.1 7.7 %attend_back.4 = (bf16[1024,768]{1,0:T(8,128)(2,1)S(1)}, f32[1,768]{1,0:T(1,128)S(1)}) custom-call(s32[1,2]{1,0:T(1,128)S(1)} %copy-done.12, s32[12]{0:T(128)S(1)} %copy-done.13, bf16[1024,512]{1,0:T(8,128)(2,1)} %get-tuple-element.129.refs_2_, bf16[1024,512]{1,0:T(8,128)(2,1)} %get-tuple-element.130.refs_3_, bf16[1024,512]{1,0:T(8,128)(2,1)} %get-tuple-element.131.refs_4_, ...), custom_call_target="tpu_custom_call" | custom-call | flops 49999998976 | bytes 1 | tf_op jit(solution)/shard_map/attend_back/pallas_call | solution.py:101
  161.5 7.5 %attend_back.5 = (bf16[1024,768]{1,0:T(8,128)(2,1)S(1)}, f32[1,768]{1,0:T(1,128)S(1)}) custom-call(s32[1,2]{1,0:T(1,128)S(1)} %copy-done.12, s32[12]{0:T(128)S(1)} %copy-done.13, bf16[1024,512]{1,0:T(8,128)(2,1)} %get-tuple-element.129.refs_2_, bf16[1024,512]{1,0:T(8,128)(2,1)} %get-tuple-element.130.refs_3_, bf16[1024,512]{1,0:T(8,128)(2,1)} %get-tuple-element.131.refs_4_, ...), custom_call_target="tpu_custom_call" | custom-call | flops 49999998976 | bytes 1 | tf_op jit(solution)/shard_map/attend_back/pallas_call | solution.py:101
  174.6 4.7 %attn_b_w.1 = (bf16[832,768]{1,0:T(8,128)(2,1)S(1)}, bf16[832,768]{1,0:T(8,128)(2,1)S(1)}) custom-call(s32[2]{0:T(128)S(1)} %pad_add_fusion.refs_0_, bf16[1024,768]{1,0:T(8,128)(2,1)S(1)} %copy-done.1, bf16[1024,768]{1,0:T(8,128)(2,1)S(1)} %get-tuple-element.138.refs_2_.refs_1_, bf16[1024,768]{1,0:T(8,128)(2,1)S(1)} %copy-done.1, ...), custom_call_target="tpu_custom_call" | custom-call | flops 49999998976 | bytes 1 | tf_op jit(solution)/shard_map/attn_b_w/pallas_call | solution.py:101
  179.4 9.8 %collective-permute-done.9.refs_1_ = bf16[96,1536]{1,0:T(8,128)(2,1)S(1)} collective-permute-done((bf16[96,1536]{1,0:T(8,128)(2,1)S(1)}, bf16[96,1536]{1,0:T(8,128)(2,1)S(1)}, u32[]{:S(2)}, u32[]{:S(2)}) %collective-permute-start.9) | collective-permute-done | bytes 294944 | tf_op jit(solution)/shard_map/ppermute | solution.py:671
  191.3 8.3 %input_grad.1.refs_2_ = bf16[1024,768]{1,0:T(8,128)(2,1)} custom-call(bf16[1024,768]{1,0:T(8,128)(2,1)S(1)} %copy-done.20, bf16[1024,768]{1,0:T(8,128)(2,1)S(1)} %get-tuple-element.138.refs_2_.refs_1_, bf16[1024,768]{1,0:T(8,128)(2,1)S(1)} %get-tuple-element.146.refs_4_.refs_2_, bf16[768,2304]{1,0:T(8,128)(2,1)} %refs_5_.9, bf16[768,2304]{1,0:T(8,128)(2,1)} %refs_5_.9, ...), custom_call_target="tpu_custom_call" | custom-call | flops 49999998976 | bytes 1 | tf_op jit(solution)/shard_map/input_grad/pallas_call | solution.py:101
  199.6 4.1 %mixed_place.1.refs_2_ = bf16[896,768]{1,0:T(8,128)(2,1)} custom-call(s32[1,1024]{1,0:T(1,128)S(1)} %copy-done.25, bf16[1024,768]{1,0:T(8,128)(2,1)} %bitcast.5.refs_1_, bf16[1024,768]{1,0:T(8,128)(2,1)} %input_grad.1.refs_2_), custom_call_target="tpu_custom_call" | custom-call | flops 10000000000 | bytes 1 | tf_op jit(solution)/shard_map/mixed_place/pallas_call | solution.py:101
  221.0 4.5 %collective-permute-done.19.refs_1_ = bf16[208,384]{1,0:T(8,128)(2,1)S(1)} collective-permute-done((bf16[208,384]{1,0:T(8,128)(2,1)S(1)}, bf16[208,384]{1,0:T(8,128)(2,1)S(1)}, u32[]{:S(2)}, u32[]{:S(2)}) %collective-permute-start.19) | collective-permute-done | bytes 159776 | tf_op jit(solution)/shard_map/ppermute | solution.py:671
  225.5 3.3 %collective-permute-start.21 = (bf16[208,384]{1,0:T(8,128)(2,1)S(1)}, bf16[208,384]{1,0:T(8,128)(2,1)S(1)}, u32[]{:S(2)}, u32[]{:S(2)}) collective-permute-start(bf16[208,384]{1,0:T(8,128)(2,1)S(1)} %attn_b_a.1.refs_3_.refs_0_), channel_id=1, source_target_pairs={{0,4},{1,5},{2,6},{3,7},{4,0},{5,1},{6,2},{7,3},{8,12},{9,13},{10,... | collective-permute-start | bytes 479240 | tf_op jit(solution)/shard_map/ppermute | solution.py:671
  233.9 4.1 %collective-permute-done.20.refs_1_ = bf16[192,384]{1,0:T(8,128)(2,1)S(1)} collective-permute-done((bf16[192,384]{1,0:T(8,128)(2,1)S(1)}, bf16[192,384]{1,0:T(8,128)(2,1)S(1)}, u32[]{:S(2)}, u32[]{:S(2)}) %collective-permute-start.20) | collective-permute-done | bytes 147488 | tf_op jit(solution)/shard_map/ppermute | solution.py:671
  247.1 4.3 %collective-permute-done.25.refs_2_ = bf16[384,384]{1,0:T(8,128)(2,1)S(1)} collective-permute-done((bf16[384,384]{1,0:T(8,128)(2,1)S(1)}, bf16[384,384]{1,0:T(8,128)(2,1)S(1)}, u32[]{:S(2)}, u32[]{:S(2)}) %collective-permute-start.25) | collective-permute-done | bytes 294944 | tf_op jit(solution)/shard_map/ppermute | solution.py:671
  (147 shorter events, 63.2 us)
Async XLA Ops:
  2.5 15.7 %all-to-all-start = ((s32[32,1,32]{2,1,0:T(1,128)}), s32[32,1,32]{2,1,0:T(1,128)S(1)}, u32[]{:S(2)}, u32[]{:S(2)}) async-start(s32[32,1,32]{2,1,0:T(1,128)} %bitcast.2), calls=%async_computation | async-start | bytes 32768 | tf_op jit(solution)/shard_map/all_to_all | solution.py:786
  23.0 51.0 %all-to-all-start.2 = ((bf16[32,32,768]{2,1,0:T(8,128)(2,1)}), bf16[32,32,768]{2,1,0:T(8,128)(2,1)}, u32[]{:S(2)}, u32[]{:S(2)}) async-start(bf16[32,32,768]{2,1,0:T(8,128)(2,1)} %bitcast.6), calls=%async_computation.2 | async-start | bytes 3145728 | tf_op jit(solution)/shard_map/all_to_all | solution.py:823
  74.0 125.6 %all-to-all-start.1 = ((bf16[32,32,768]{2,1,0:T(8,128)(2,1)}), bf16[32,32,768]{2,1,0:T(8,128)(2,1)}, u32[]{:S(2)}, u32[]{:S(2)}) async-start(bf16[32,32,768]{2,1,0:T(8,128)(2,1)} %bitcast.4), calls=%async_computation.1 | async-start | bytes 3145728 | tf_op jit(solution)/shard_map/all_to_all | solution.py:873
  109.2 30.4 %collective-permute-start.2 = (bf16[768,768]{1,0:T(8,128)(2,1)S(1)}, bf16[768,768]{1,0:T(8,128)(2,1)S(1)}, u32[]{:S(2)}, u32[]{:S(2)}) collective-permute-start(bf16[768,768]{1,0:T(8,128)(2,1)S(1)} %get-tuple-element.123.refs_3_), channel_id=1, source_target_pairs={{0,16},{8,24},{16,0},{24,8},{1,17},{9,25},{17,1},{25,9},{2,18},{10... | collective-permute-start | bytes 3538952 | tf_op jit(solution)/shard_map/ppermute | solution.py:671
  115.3 38.5 %collective-permute-start.5 = (bf16[384,1536]{1,0:T(8,128)(2,1)}, bf16[384,1536]{1,0:T(8,128)(2,1)}, u32[]{:S(2)}, u32[]{:S(2)}) collective-permute-start(bf16[384,1536]{1,0:T(8,128)(2,1)} %get-tuple-element.141), channel_id=1, source_target_pairs={{0,1},{1,0},{2,3},{3,2},{4,5},{5,4},{6,7},{7,6},{8,9},{9,8},{10,11... | collective-permute-start | bytes 3538952 | tf_op jit(solution)/shard_map/ppermute | solution.py:671
  140.6 17.9 %collective-permute-start.3 = (bf16[768,384]{1,0:T(8,128)(2,1)S(1)}, bf16[768,384]{1,0:T(8,128)(2,1)S(1)}, u32[]{:S(2)}, u32[]{:S(2)}) collective-permute-start(bf16[768,384]{1,0:T(8,128)(2,1)S(1)} %get-tuple-element.139), channel_id=1, source_target_pairs={{0,1},{1,0},{2,3},{3,2},{4,5},{5,4},{6,7},{7,6},{8,9},{9,8},{10,11... | collective-permute-start | bytes 1769480 | tf_op jit(solution)/shard_map/ppermute | solution.py:671
  146.0 11.1 %collective-permute-start.4 = (bf16[768,768]{1,0:T(8,128)(2,1)S(1)}, bf16[768,768]{1,0:T(8,128)(2,1)S(1)}, u32[]{:S(2)}, u32[]{:S(2)}) collective-permute-start(bf16[768,768]{1,0:T(8,128)(2,1)S(1)} %get-tuple-element.137.refs_8_), channel_id=1, source_target_pairs={{0,8},{8,0},{16,24},{24,16},{1,9},{9,1},{17,25},{25,17},{2,10},{10... | collective-permute-start | bytes 3538952 | tf_op jit(solution)/shard_map/ppermute | solution.py:671
  155.4 16.7 %collective-permute-start.6 = (bf16[192,1536]{1,0:T(8,128)(2,1)S(1)}, bf16[192,1536]{1,0:T(8,128)(2,1)S(1)}, u32[]{:S(2)}, u32[]{:S(2)}) collective-permute-start(bf16[192,1536]{1,0:T(8,128)(2,1)S(1)} %get-tuple-element.143.refs_2_), channel_id=1, source_target_pairs={{0,16},{8,24},{16,0},{24,8},{1,17},{9,25},{17,1},{25,9},{2,18},{10... | collective-permute-start | bytes 1769480 | tf_op jit(solution)/shard_map/ppermute | solution.py:671
  158.1 49.8 %collective-permute-start.10 = (bf16[384,768]{1,0:T(8,128)(2,1)}, bf16[384,768]{1,0:T(8,128)(2,1)}, u32[]{:S(2)}, u32[]{:S(2)}) collective-permute-start(bf16[384,768]{1,0:T(8,128)(2,1)} %get-tuple-element.144.refs_3_), channel_id=1, source_target_pairs={{0,16},{8,24},{16,0},{24,8},{1,17},{9,25},{17,1},{25,9},{2,18},{10... | collective-permute-start | bytes 1769480 | tf_op jit(solution)/shard_map/ppermute | solution.py:671
  159.2 9.9 %collective-permute-start.7 = (bf16[384,384]{1,0:T(8,128)(2,1)S(1)}, bf16[384,384]{1,0:T(8,128)(2,1)S(1)}, u32[]{:S(2)}, u32[]{:S(2)}) collective-permute-start(bf16[384,384]{1,0:T(8,128)(2,1)S(1)} %get-tuple-element.150), channel_id=1, source_target_pairs={{0,2},{1,3},{2,0},{3,1},{4,6},{5,7},{6,4},{7,5},{8,10},{9,11},{10,... | collective-permute-start | bytes 884744 | tf_op jit(solution)/shard_map/ppermute | solution.py:671
  169.9 35.4 %collective-permute-start.11 = (bf16[384,384]{1,0:T(8,128)(2,1)}, bf16[384,384]{1,0:T(8,128)(2,1)}, u32[]{:S(2)}, u32[]{:S(2)}) collective-permute-start(bf16[384,384]{1,0:T(8,128)(2,1)} %w_down_a.1.refs_3_.refs_0_), channel_id=1, source_target_pairs={{0,4},{1,5},{2,6},{3,7},{4,0},{5,1},{6,2},{7,3},{8,12},{9,13},{10,... | collective-permute-start | bytes 884744 | tf_op jit(solution)/shard_map/ppermute | solution.py:671
  172.7 16.5 %collective-permute-start.9 = (bf16[96,1536]{1,0:T(8,128)(2,1)S(1)}, bf16[96,1536]{1,0:T(8,128)(2,1)S(1)}, u32[]{:S(2)}, u32[]{:S(2)}) collective-permute-start(bf16[96,1536]{1,0:T(8,128)(2,1)S(1)} %get-tuple-element.154), channel_id=1, source_target_pairs={{0,2},{1,3},{2,0},{3,1},{4,6},{5,7},{6,4},{7,5},{8,10},{9,11},{10,... | collective-permute-start | bytes 884744 | tf_op jit(solution)/shard_map/ppermute | solution.py:671
  179.3 10.1 %collective-permute-start.8 = (bf16[832,768]{1,0:T(8,128)(2,1)S(1)}, bf16[832,768]{1,0:T(8,128)(2,1)S(1)}, u32[]{:S(2)}, u32[]{:S(2)}) collective-permute-start(bf16[832,768]{1,0:T(8,128)(2,1)S(1)} %get-tuple-element.153.refs_2_), channel_id=1, source_target_pairs={{0,8},{8,0},{16,24},{24,16},{1,9},{9,1},{17,25},{25,17},{2,10},{10... | collective-permute-start | bytes 3833864 | tf_op jit(solution)/shard_map/ppermute | solution.py:671
  189.3 22.2 %collective-permute-start.16 = (bf16[96,1536]{1,0:T(8,128)(2,1)S(1)}, bf16[96,1536]{1,0:T(8,128)(2,1)S(1)}, u32[]{:S(2)}, u32[]{:S(2)}) collective-permute-start(bf16[96,1536]{1,0:T(8,128)(2,1)S(1)} %w_in_a.1.refs_3_.refs_0_), channel_id=1, source_target_pairs={{0,4},{1,5},{2,6},{3,7},{4,0},{5,1},{6,2},{7,3},{8,12},{9,13},{10,... | collective-permute-start | bytes 884744 | tf_op jit(solution)/shard_map/ppermute | solution.py:671
  190.4 13.3 %collective-permute-start.12 = (bf16[832,384]{1,0:T(8,128)(2,1)S(1)}, bf16[832,384]{1,0:T(8,128)(2,1)S(1)}, u32[]{:S(2)}, u32[]{:S(2)}) collective-permute-start(bf16[832,384]{1,0:T(8,128)(2,1)S(1)} %get-tuple-element.157), channel_id=1, source_target_pairs={{0,1},{1,0},{2,3},{3,2},{4,5},{5,4},{6,7},{7,6},{8,9},{9,8},{10,11... | collective-permute-start | bytes 1916936 | tf_op jit(solution)/shard_map/ppermute | solution.py:671
  206.4 10.0 %collective-permute-start.14 = (bf16[384,384]{1,0:T(8,128)(2,1)S(1)}, bf16[384,384]{1,0:T(8,128)(2,1)S(1)}, u32[]{:S(2)}, u32[]{:S(2)}) collective-permute-start(bf16[384,384]{1,0:T(8,128)(2,1)S(1)} %w_down_f.1.refs_3_.refs_1_), channel_id=1, source_target_pairs={{0,2},{1,3},{2,0},{3,1},{4,6},{5,7},{6,4},{7,5},{8,10},{9,11},{10,... | collective-permute-start | bytes 884744 | tf_op jit(solution)/shard_map/ppermute | solution.py:671
  209.7 10.0 %collective-permute-start.13 = (bf16[384,384]{1,0:T(8,128)(2,1)S(1)}, bf16[384,384]{1,0:T(8,128)(2,1)S(1)}, u32[]{:S(2)}, u32[]{:S(2)}) collective-permute-start(bf16[384,384]{1,0:T(8,128)(2,1)S(1)} %get-tuple-element.160), channel_id=1, source_target_pairs={{0,1},{1,0},{2,3},{3,2},{4,5},{5,4},{6,7},{7,6},{8,9},{9,8},{10,11... | collective-permute-start | bytes 884744 | tf_op jit(solution)/shard_map/ppermute | solution.py:671
  211.5 17.3 %collective-permute-start.18 = (bf16[96,1536]{1,0:T(8,128)(2,1)S(1)}, bf16[96,1536]{1,0:T(8,128)(2,1)S(1)}, u32[]{:S(2)}, u32[]{:S(2)}) collective-permute-start(bf16[96,1536]{1,0:T(8,128)(2,1)S(1)} %w_in_f.1.refs_3_.refs_1_), channel_id=1, source_target_pairs={{0,2},{1,3},{2,0},{3,1},{4,6},{5,7},{6,4},{7,5},{8,10},{9,11},{10,... | collective-permute-start | bytes 884744 | tf_op jit(solution)/shard_map/ppermute | solution.py:671
  212.2 13.3 %collective-permute-start.19 = (bf16[208,384]{1,0:T(8,128)(2,1)S(1)}, bf16[208,384]{1,0:T(8,128)(2,1)S(1)}, u32[]{:S(2)}, u32[]{:S(2)}) collective-permute-start(bf16[208,384]{1,0:T(8,128)(2,1)S(1)} %get-tuple-element.165), channel_id=1, source_target_pairs={{0,2},{1,3},{2,0},{3,1},{4,6},{5,7},{6,4},{7,5},{8,10},{9,11},{10,... | collective-permute-start | bytes 479240 | tf_op jit(solution)/shard_map/ppermute | solution.py:671
  217.0 21.1 %collective-permute-start.24 = (bf16[768,384]{1,0:T(8,128)(2,1)S(1)}, bf16[768,384]{1,0:T(8,128)(2,1)S(1)}, u32[]{:S(2)}, u32[]{:S(2)}) collective-permute-start(bf16[768,384]{1,0:T(8,128)(2,1)S(1)} %w_down_g.1.refs_3_.refs_1_), channel_id=1, source_target_pairs={{0,1},{1,0},{2,3},{3,2},{4,5},{5,4},{6,7},{7,6},{8,9},{9,8},{10,11... | collective-permute-start | bytes 1769480 | tf_op jit(solution)/shard_map/ppermute | solution.py:671
  220.4 10.4 %collective-permute-start.17 = (bf16[192,384]{1,0:T(8,128)(2,1)S(1)}, bf16[192,384]{1,0:T(8,128)(2,1)S(1)}, u32[]{:S(2)}, u32[]{:S(2)}) collective-permute-start(bf16[192,384]{1,0:T(8,128)(2,1)S(1)} %get-tuple-element.164), channel_id=1, source_target_pairs={{0,2},{1,3},{2,0},{3,1},{4,6},{5,7},{6,4},{7,5},{8,10},{9,11},{10,... | collective-permute-start | bytes 442376 | tf_op jit(solution)/shard_map/ppermute | solution.py:671
  225.5 8.2 %collective-permute-start.21 = (bf16[208,384]{1,0:T(8,128)(2,1)S(1)}, bf16[208,384]{1,0:T(8,128)(2,1)S(1)}, u32[]{:S(2)}, u32[]{:S(2)}) collective-permute-start(bf16[208,384]{1,0:T(8,128)(2,1)S(1)} %attn_b_a.1.refs_3_.refs_0_), channel_id=1, source_target_pairs={{0,4},{1,5},{2,6},{3,7},{4,0},{5,1},{6,2},{7,3},{8,12},{9,13},{10,... | collective-permute-start | bytes 479240 | tf_op jit(solution)/shard_map/ppermute | solution.py:671
  229.4 15.5 %collective-permute-start.27 = (bf16[192,1536]{1,0:T(8,128)(2,1)S(1)}, bf16[192,1536]{1,0:T(8,128)(2,1)S(1)}, u32[]{:S(2)}, u32[]{:S(2)}) collective-permute-start(bf16[192,1536]{1,0:T(8,128)(2,1)S(1)} %w_in_g.1.refs_2_.refs_1_), channel_id=1, source_target_pairs={{0,1},{1,0},{2,3},{3,2},{4,5},{5,4},{6,7},{7,6},{8,9},{9,8},{10,11... | collective-permute-start | bytes 1769480 | tf_op jit(solution)/shard_map/ppermute | solution.py:671
  240.9 10.5 %collective-permute-start.26 = (bf16[416,384]{1,0:T(8,128)(2,1)S(1)}, bf16[416,384]{1,0:T(8,128)(2,1)S(1)}, u32[]{:S(2)}, u32[]{:S(2)}) collective-permute-start(bf16[416,384]{1,0:T(8,128)(2,1)S(1)} %attn_b_g.1.refs_3_), channel_id=1, source_target_pairs={{0,1},{1,0},{2,3},{3,2},{4,5},{5,4},{6,7},{7,6},{8,9},{9,8},{10,11... | collective-permute-start | bytes 958472 | tf_op jit(solution)/shard_map/ppermute | solution.py:671
  (39 other events, 275.0 us)

commit v4 on v3

--- a/solution.py
+++ b/solution.py
@@ -16,6 +16,7 @@
 COST = 5e10
 COST_MID = 2e10
 COST_SMALL = 1e10
+COST_TINY = 1e9
 COST_TINY = 1e9
 
 NN = (((1,), (0,)), ((), ()))
@@ -347,14 +348,6 @@
         ref[at : at + 1, :] = row
 
 
-def store_halves(ids_ref, total, mine_ref, other_ref):
-    half = mine_ref.shape[1]
-    second = (ids_ref[1] & 1) == 1
-    left, right = total[:, :half], total[:, half:]
-    mine_ref[...] = jnp.where(second, right, left)
-    other_ref[...] = jnp.where(second, left, right)
-
-
 def quarter_at(step, ids_ref):
     rel = jnp.where(step == 0, 3, jnp.where(step == 3, 0, step))
     return jnp.bitwise_xor(ids_ref[0], rel)
@@ -414,21 +407,11 @@
         near_ref[step - 2] = grad
 
 
-def down_add_kernel(near_ref, mate_ref, send_ref, keep_ref):
-    for at, out_ref in enumerate((send_ref, keep_ref)):
-        out_ref[...] = (near_ref[at].astype(F32) + mate_ref[at].astype(F32)).astype(BF)
-
-
 def in_back_kernel(ids_ref, x_ref, act_ref, far_ref, near_ref):
     blk = x_ref.shape[1]
     own = block_cols(pl.program_id(0), blk)
     grad = mm(x_ref[...], act_ref[:, own], TN).astype(BF)
     store_quarters(ids_ref, grad, far_ref, near_ref, 0, blk // 4, own)
-
-
-def in_add_kernel(ids_ref, near_ref, mate_ref, mine_ref, other_ref):
-    total = (near_ref[...].astype(F32) + mate_ref[...].astype(F32)).astype(BF)
-    store_halves(ids_ref, total, mine_ref, other_ref)
 
 
 def first_back_kernel(
@@ -577,23 +560,25 @@
         store_vectors(ids_ref, vec_refs, far_ref, near_ref, count * part, size)
 
 
-def share_add_kernel(near_ref, mate_ref, send_ref, keep_ref):
-    size = send_ref.shape[0]
+def spread_kernel(ids_ref, near_ref, mate_ref, keep_ref, send_ref):
     total = (near_ref[...].astype(F32) + mate_ref[...].astype(F32)).astype(BF)
-    send_ref[...] = total[:size]
-    keep_ref[...] = total[size:]
-
-
-def split_cols_kernel(ids_ref, keep_ref, got_ref, mine_ref, other_ref):
+    rows, half = total.shape[0] // 2, total.shape[1] // 2
+    second = (ids_ref[1] & 1) == 1
+    core = (ids_ref[0] & 1) == 1
+    left, right = total[:, :half], total[:, half:]
+    mine = jnp.where(second, right, left)
+    other = jnp.where(second, left, right)
+    keep_ref[:rows, :] = mine[rows:]
+    keep_ref[rows:, :] = jnp.where(core, mine[:rows], other[rows:])
+    send_ref[:rows, :] = jnp.where(core, other[rows:], mine[:rows])
+    send_ref[rows:, :] = other[:rows]
+
+
+def split_blocks_kernel(keep_ref, got_ref, mine_ref, other_ref):
     total = (keep_ref[...].astype(F32) + got_ref[...].astype(F32)).astype(BF)
-    store_halves(ids_ref, total, mine_ref, other_ref)
-
-
-def split_shares_kernel(mine_ref, got_ref, send_ref, keep_ref):
-    total = (mine_ref[...].astype(F32) + got_ref[...].astype(F32)).astype(BF)
-    rows = send_ref.shape[0]
-    send_ref[...] = total[:rows]
-    keep_ref[...] = total[rows:]
+    rows = mine_ref.shape[0]
+    mine_ref[...] = total[:rows]
+    other_ref[...] = total[rows:]
 
 
 def split_rows_kernel(ids_ref, keep_ref, got_ref, mine_ref, other_ref):
@@ -671,6 +656,16 @@
     return lax.ppermute(values, axis, [(i, i ^ mask) for i in range(count)])
 
 
+def exchange_mixed(values, core_along_x):
+    seq, batch = lax.axis_size("seq"), lax.axis_size("batch")
+
+    def partner(s, b):
+        return (s ^ 2) * batch + b if s & 1 == core_along_x else s * batch + (b ^ 1)
+
+    pairs = [(s * batch + b, partner(s, b)) for s in range(seq) for b in range(batch)]
+    return lax.ppermute(values, ("seq", "batch"), pairs)
+
+
 def simple(chain, body, name, args, out_shape, prefetch=0, vmem=12, scratch=(), cost=COST_SMALL, free=()):
     tensors = args[prefetch:]
     return call(
@@ -690,22 +685,23 @@
 
 
 class Share:
-    def __init__(self, chain, ids, name, left, right, y_first=False):
+    def __init__(self, chain, ids, name, near, mate, cost=COST_SMALL):
         self.chain, self.ids, self.name = chain, ids, name
-        if y_first:
-            self.keep, self.got = left, exchange(right, "batch", 1)
-            self.shape = (left.shape[0] // 2, left.shape[1] * 2)
-        else:
-            self.keep, self.got = right, exchange(left, "seq", 2)
-            self.shape = right.shape
-
-    def step_x(self):
+        rows, cols = near.shape
+        self.shape = (rows // 2, cols)
+        self.keep, send = simple(
+            chain, spread_kernel, name + "_c", (ids, near, mate), [vmem((rows, cols // 2), BF)] * 2,
+            1, cost=cost,
+        )
+        self.got = exchange_mixed(send, 0)
+
+    def step_xy(self, cost=COST_SMALL):
         rows, cols = self.shape
-        send, self.keep = simple(
-            self.chain, split_shares_kernel, self.name + "_x", (self.keep, self.got),
-            [vmem((rows, cols // 2), BF)] * 2,
+        self.keep, send = simple(
+            self.chain, split_blocks_kernel, self.name + "_x", (self.keep, self.got),
+            [vmem((rows, cols // 2), BF)] * 2, cost=cost,
         )
-        self.got = exchange(send, "seq", 2)
+        self.got = exchange_mixed(send, 1)
 
     def halve(self, kernel, shape, label, mask, cost=COST_SMALL):
         self.keep, other = simple(
@@ -714,10 +710,6 @@
         )
         self.got = exchange(other, "batch", mask)
 
-    def step_y(self):
-        rows, cols = self.shape
-        self.halve(split_cols_kernel, (rows, cols // 2), "_y", 1)
-
     def step_z(self, cost=COST_SMALL):
         rows, cols = self.shape
         self.halve(split_rows_kernel, (rows // 2, cols // 2), "_z", 2, cost)
@@ -735,8 +727,8 @@
             self.got = exchange(self.keep, "batch", mask)
             mask *= 2
 
-    def step_back(self):
-        self.add("_f")
+    def step_back(self, cost=COST_SMALL):
+        self.add("_f", cost)
         self.got = exchange(self.keep, "batch", 2)
 
     def step_wide(self):
@@ -819,6 +811,7 @@
         "cot_gather",
         (in_target, cotangent),
         [sds((slots, width), BF), sds((1, slots), I32)],
+        free=(1,),
     )
     cot_in = lax.all_to_all(cot_out, ("seq", "batch"), split_axis=0, concat_axis=0, tiled=True)
     *rest_heads, first_low, normed1, inv1, context = call(
@@ -861,7 +854,7 @@
         ],
         out_shape=[
             hbm(act_shape, BF), hbm(act_shape, BF), hbm(bf_rows, BF), hbm((rows, 1), F32),
-            hbm(bf_rows, BF),
+            vmem(bf_rows, BF),
         ],
         scratch=[pltpu.VMEM(bf_rows, F32)],
     )(first_low, w_in, in_bias, w_down, down_bias, norm2_gain, norm2_bias)
@@ -877,7 +870,7 @@
         cot_back_kernel,
         "cot_back",
         (slot_row, cot_in, normed2, inv2, norm2_gain),
-        [hbm(bf_rows, F32), vmem(bf_rows, BF), sds((8, width), F32)],
+        [vmem(bf_rows, F32), vmem(bf_rows, BF), sds((8, width), F32)],
         vmem=24,
         cost=COST,
     )
@@ -900,8 +893,8 @@
             vmem(act_shape, BF), sds((1, ff), F32), vmem(down_shape, BF), vmem(down_shape, BF),
         ],
         prefetch=1,
-        free=(3, 4),
     )(ids, g_branch, w_down, slope, hid)
+    gwd_far, gwd_near = (a.reshape(2 * blk, width) for a in (gwd_far, gwd_near))
     gwd_mate = exchange(gwd_far, "seq", 1)
     in_shape = (2 * part, ff)
     gwi_far, gwi_near = call(
@@ -917,17 +910,8 @@
         free=(1,),
     )(ids, first_low, g_act)
     gwi_mate = exchange(gwi_far, "seq", 1)
-    send, keep = simple(
-        chain, down_add_kernel, "w_down_c", (gwd_near, gwd_mate), [vmem((blk, width), BF)] * 2,
-        cost=COST,
-    )
-    down_share = Share(chain, ids, "w_down", send, keep)
-
-    mine, other = simple(
-        chain, in_add_kernel, "w_in_c", (ids, gwi_near, gwi_mate),
-        [vmem((2 * part, ff // 2), BF)] * 2, 1,
-    )
-    in_share = Share(chain, ids, "w_in", mine, other, y_first=True)
+    down_share = Share(chain, ids, "w_down", gwd_near, gwd_mate, COST)
+    in_share = Share(chain, ids, "w_in", gwi_near, gwi_mate)
 
     g_pre1, g_attn, g_ctx, vec1 = call(
         chain,
@@ -975,7 +959,7 @@
         projs.append(proj)
         vecs.append(vec)
 
-    def attention_share(pairs, vec_ins, name, y_first):
+    def attention_share(pairs, vec_ins, name, cost=COST):
         extra = 32 if vec_ins else 0
         size = len(pairs) * part + extra
         flat = [a for both in pairs for a in both]
@@ -987,41 +971,29 @@
             [vmem((2 * size, width), BF)] * 2,
             1,
             vmem=20,
-            cost=COST,
+            cost=cost,
             free=(1, 3),
         )
         mate = exchange(far_grad, "seq", 1)
-
-        def near_part():
-            if y_first:
-                outs = simple(
-                    chain, in_add_kernel, name + "_c", (ids, near_grad, mate),
-                    [vmem((2 * size, width // 2), BF)] * 2, 1,
-                )
-            else:
-                outs = simple(
-                    chain, share_add_kernel, name + "_c", (near_grad, mate),
-                    [vmem((size, width), BF)] * 2,
-                )
-            return Share(chain, ids, name, *outs, y_first)
-
-        return near_part
-
+        return lambda: Share(chain, ids, name, near_grad, mate)
+
+    down_share.step_xy()
     group_back(0)
-    down_share.step_y()
-    start_a = attention_share([(context, g_attn), (hidden_in, projs[0])], [], "attn_a", False)
+    start_a = attention_share([(context, g_attn), (hidden_in, projs[0])], [], "attn_a")
+    down_share.step_z()
+    in_share.step_xy()
     group_back(1)
-    in_share.step_x()
-    share_a = start_a()
-    down_share.step_z()
-    group_back(2)
     down_share.step_far()
     in_share.step_z()
+    share_a = start_a()
+    group_back(2)
+    share_a.step_xy(COST_TINY)
     vec_ins = [vec2, bias_row, vec1, *vecs]
     start_b = attention_share(
-        [(hidden_in, projs[1]), (hidden_in, projs[2])], vec_ins, "attn_b", True
-    )
-    in_share.step_far(COST_MID)
+        [(hidden_in, projs[1]), (hidden_in, projs[2])], vec_ins, "attn_b", COST_TINY
+    )
+    in_share.step_far()
+    down_share.step_back(COST_MID)
     share_b = start_b()
     input_grad = call(
         chain,
@@ -1040,24 +1012,22 @@
         out_shape=low,
         scratch=[pltpu.VMEM((rows, width), F32)],
     )(*projs, w_qkv, w_qkv, w_qkv, g_pre1)
+    share_a.step_z()
+    share_b.step_xy()
     (mixed,) = simple(
         chain, place_kernel, "mixed_place", (in_row, mixed_in), [hbm((ffn_rows, width), BF)]
     )
-    share_b.step_x()
-    down_share.step_back()
-    share_a.step_y()
-    in_share.step_back()
     share_b.step_z()
     down_share.step_wide()
-    share_a.step_z()
+    in_share.step_back()
+    share_a.step_far()
     share_b.step_far()
     in_share.step_wide()
-    share_a.step_far()
-    share_b.step_back()
     share_a.step_back()
     g_w_down = down_share.join()
+    share_b.step_back()
+    share_a.step_wide()
     share_b.step_wide()
-    share_a.step_wide()
     g_w_in = in_share.join()
     one = lambda size: sds((size,), F32)
     g_w_qkv, g_w_out, g_qv, g_in_bias, g_n2g, g_n2b, g_down_bias, g_n1g, g_n1b, g_out_bias = simple(

time: 259 us -> 250 us (0.965)
  Pallas kernels: 167 us -> 160 us
    ppermute x0 -> x8, starting transfers between devices: none -> 10.8 us  [exchange_mixed(): return lax.ppermute(values, ('seq', 'batch'), pairs)]
    ppermute x28 -> x20, starting transfers between devices: 30.9 us -> 20.7 us  [exchange(): return lax.ppermute(values, axis, [(i, i ^ mask) for i in range(count)])]
    pallas_call x44, Pallas kernels: 167 us -> 160 us  [run(): outs = kernel(*placed, *[chain.place(a) for a in before])]
    ppermute x28 -> x20, waiting for transfers between devices: 33.2 us -> 27.4 us  [exchange(): return lax.ppermute(values, axis, [(i, i ^ mask) for i in range(count)])]
    ppermute x0 -> x8, waiting for transfers between devices: none -> 4.06 us  [exchange_mixed(): return lax.ppermute(values, ('seq', 'batch'), pairs)]
where the time goes in v4:
time: 250 us; the launch traced here: 245 us
  Pallas kernels  160 us (64%)
  starting transfers between devices  51.2 us (20%)
  waiting for transfers between devices  31.5 us (13%)
    pallas_call x44, Pallas kernels, run(): outs = kernel(*placed, *[chain.place(a) for a in before])  160 us
    ppermute x20, waiting for transfers between devices, exchange(): return lax.ppermute(values, axis, [(i, i ^ mask) for i in range(count)])  27.4 us
    ppermute x20, starting transfers between devices, exchange(): return lax.ppermute(values, axis, [(i, i ^ mask) for i in range(count)])  20.7 us
    ppermute x8, starting transfers between devices, exchange_mixed(): return lax.ppermute(values, ('seq', 'batch'), pairs)  10.8 us
    all_to_all x1, starting transfers between devices, body(): lax.all_to_all(out_target, ('seq', 'batch'), split_axis=0, concat_axis=0,...  7.29 us
    all_to_all x1, starting transfers between devices, body(): lax.all_to_all(mixed_out, ('seq', 'batch'), split_axis=0, concat_axis=0,...  6.27 us
    all_to_all x1, starting transfers between devices, body(): lax.all_to_all(cot_out, ('seq', 'batch'), split_axis=0, concat_axis=0, ti...  6.12 us
  transfers between devices with their start and end apart: 31, of which 11 were waited for; matrix products, arithmetic and copies ran while one was open for 0% of the time, Pallas kernels for 63%

profile of v4, /device:TPU:0, one launch (start us, length us, event | category | flops | bytes accessed | tf_op | source)
XLA Modules:
  0.0 244.9 jit_solution(14498724798737756737)
XLA Ops:
  2.5 7.3 %all-to-all-start = ((s32[32,1,32]{2,1,0:T(1,128)}), s32[32,1,32]{2,1,0:T(1,128)S(1)}, u32[]{:S(2)}, u32[]{:S(2)}) async-start(s32[32,1,32]{2,1,0:T(1,128)} %bitcast.2), calls=%async_computation | async-start | bytes 32768 | tf_op jit(solution)/shard_map/all_to_all | solution.py:778
  9.8 8.4 %attend_first.1 = (bf16[1024,256]{1,0:T(8,128)(2,1)}, bf16[1024,256]{1,0:T(8,128)(2,1)}, bf16[1024,256]{1,0:T(8,128)(2,1)}, bf16[1024,256]{1,0:T(8,128)(2,1)}, b...) custom-call(s32[1,2]{1,0:T(1,128)S(1)} %copy-done.18, s32[12]{0:T(128)S(1)} %copy-done.19, ...), custom_call_target="tpu_custom_call" | custom-call | flops 49999998976 | bytes 1 | tf_op jit(solution)/shard_map/attend_first/pallas_call | solution.py:102
  18.3 3.5 %cot_gather.1 = (bf16[1024,768]{1,0:T(8,128)(2,1)}, s32[1,1024]{1,0:T(1,128)S(1)}) custom-call(s32[32,32]{1,0:T(8,128)S(1)} %bitcast.13, bf16[896,768]{1,0:T(8,128)(2,1)S(1)} %copy-done.7, bf16[1024,256]{1,0:T(8,128)(2,1)} %get-tuple-element.97.refs_2_), custom_call_target="tpu_custom_call" | custom-call | flops 10000000000 | bytes 1 | tf_op jit(solution)/shard_map/cot_gather/pallas_call | solution.py:102
  21.8 6.1 %all-to-all-start.2 = ((bf16[32,32,768]{2,1,0:T(8,128)(2,1)}), bf16[32,32,768]{2,1,0:T(8,128)(2,1)}, u32[]{:S(2)}, u32[]{:S(2)}) async-start(bf16[32,32,768]{2,1,0:T(8,128)(2,1)} %bitcast.8), calls=%async_computation.2 | async-start | bytes 3145728 | tf_op jit(solution)/shard_map/all_to_all | solution.py:816
  28.0 19.7 %attend_rest.1 = (bf16[1024,512]{1,0:T(8,128)(2,1)}, bf16[1024,512]{1,0:T(8,128)(2,1)}, bf16[1024,512]{1,0:T(8,128)(2,1)}, bf16[8,2,512,512]{3,2,1,0:T(8,128)(2,...) custom-call(s32[1,2]{1,0:T(1,128)S(1)} %copy-done.18, ...), custom_call_target="tpu_custom_call" | custom-call | flops 49999998976 | bytes 1 | tf_op jit(solution)/shard_map/attend_rest/pallas_call | solution.py:102
  47.8 20.1 %ffn.1 = (bf16[1024,3072]{1,0:T(8,128)(2,1)}, bf16[1024,3072]{1,0:T(8,128)(2,1)}, bf16[1024,768]{1,0:T(8,128)(2,1)}, f32[1024,1]{1,0:T(8,128)}, bf16[1024,768]{1,0:T(8,128)(2,1)S(1)}) custom-call(bf16[1024,768]{1,0:T(8,128)(2,1)} %get-tuple-element.100.refs_0_.refs_1_, bf16[768,3072]{1,0:T(8,128)(2,1)} %refs_2_.9, f32[3072]{0:T(1024)S(1)} %copy-done.9, ...), custom_call_target="tpu_custom_call" | custom-call | flops 49999998976 | bytes 1 | tf_op jit(solution)/shard_map/ffn/pallas_call | solution.py:102
  67.9 3.0 %mixed_slots.1.refs_5_ = bf16[1024,768]{1,0:T(8,128)(2,1)} custom-call(s32[1,1024]{1,0:T(1,128)S(1)} %get-tuple-element.96.refs_7_.refs_0_, bf16[1024,768]{1,0:T(8,128)(2,1)S(1)} %get-tuple-element.102.refs_1_, f32[1024,1]{1,0:T(8,128)} %get-tuple-element.103.refs_2_.refs_3_), custom_call_target="tpu_custom_call" | custom-call | flops 49999998976 | bytes 1 | tf_op jit(solution)/shard_map/mixed_slots/pallas_call | solution.py:102
  70.9 6.3 %all-to-all-start.1 = ((bf16[32,32,768]{2,1,0:T(8,128)(2,1)}), bf16[32,32,768]{2,1,0:T(8,128)(2,1)}, u32[]{:S(2)}, u32[]{:S(2)}) async-start(bf16[32,32,768]{2,1,0:T(8,128)(2,1)} %bitcast.4), calls=%async_computation.1 | async-start | bytes 3145728 | tf_op jit(solution)/shard_map/all_to_all | solution.py:866
  77.1 5.4 %cot_back.1 = (f32[1024,768]{1,0:T(8,128)S(1)}, bf16[1024,768]{1,0:T(8,128)(2,1)S(1)}, f32[8,768]{1,0:T(8,128)S(1)}) custom-call(s32[1,1024]{1,0:T(1,128)S(1)} %get-tuple-element.96.refs_7_.refs_0_, bf16[1024,768]{1,0:T(8,128)(2,1)} %bitcast.9.refs_1_, bf16[1024,768]{1,0:T(8,128)(2,1)} %get-tuple-element.109.refs_2_, ...), custom_call_target="tpu_custom_call" | custom-call | flops 49999998976 | bytes 1 | tf_op jit(solution)/shard_map/cot_back/pallas_call | solution.py:102
  82.5 14.1 %down_back.1 = (bf16[1024,3072]{1,0:T(8,128)(2,1)S(1)}, f32[1,3072]{1,0:T(1,128)S(1)}, bf16[2,768,768]{2,1,0:T(8,128)(2,1)S(1)}, bf16[2,768,768]{2,1,0:T(8,128)(2,1)S(1)}) custom-call(s32[2]{0:T(128)S(1)} %pad_add_fusion.refs_0_, bf16[1024,768]{1,0:T(8,128)(2,1)S(1)} %get-tuple-element.111.refs_1_, bf16[3072,768]{1,0:T(8,128)(2,1)} %refs_2_.8, ...), custom_call_target="tpu_custom_call" | custom-call | flops 49999998976 | bytes 1 | tf_op jit(solution)/shard_map/down_back/pallas_call | solution.py:102
  97.1 7.0 %in_back.1 = (bf16[384,3072]{1,0:T(8,128)(2,1)S(1)}, bf16[384,3072]{1,0:T(8,128)(2,1)S(1)}) custom-call(s32[2]{0:T(128)S(1)} %pad_add_fusion.refs_0_, bf16[1024,768]{1,0:T(8,128)(2,1)S(1)} %copy-done.25, bf16[1024,3072]{1,0:T(8,128)(2,1)S(1)} %get-tuple-element.115.refs_2_.refs_1_, f32[1,3072]{1,0:T(1,128)S(1)} %get-tuple-element.119.refs_3_.refs_6_), custom_call_target="tpu_custom_call" | custom-call | flops 49999998976 | bytes 1 | tf_op jit(solution)/shard_map/in_back/pallas_call | solution.py:102
  112.6 13.7 %first_back.1 = (f32[1024,768]{1,0:T(8,128)}, bf16[1024,768]{1,0:T(8,128)(2,1)S(1)}, bf16[1024,768]{1,0:T(8,128)(2,1)S(1)}, f32[8,768]{1,0:T(8,128)S(1)}) custom-call(f32[1024,768]{1,0:T(8,128)S(1)} %get-tuple-element.110.refs_0_, bf16[1024,3072]{1,0:T(8,128)(2,1)S(1)} %get-tuple-element.115.refs_2_.refs_1_, bf16[768,3072]{1,0:T(8,128)(2,1)} %refs_2_.9, ...), custom_call_target="tpu_custom_call" | custom-call | flops 49999998976 | bytes 1 | tf_op jit(solution)/shard_map/first_back/pallas_call | solution.py:102
  128.2 7.6 %attend_back.3 = (bf16[1024,768]{1,0:T(8,128)(2,1)S(1)}, f32[1,768]{1,0:T(1,128)S(1)}) custom-call(s32[1,2]{1,0:T(1,128)S(1)} %copy-done.18, s32[12]{0:T(128)S(1)} %copy-done.19, bf16[1024,256]{1,0:T(8,128)(2,1)} %get-tuple-element.97.refs_2_, bf16[1024,256]{1,0:T(8,128)(2,1)} %get-tuple-element.134.refs_3_, bf16[1024,256]{1,0:T(8,128)(2,1)} %get-tuple-element.135.refs_4_, ...), custom_call_target="tpu_custom_call" | custom-call | flops 49999998976 | bytes 1 | tf_op jit(solution)/shard_map/attend_back/pallas_call | solution.py:102
  135.9 4.5 %attn_a_w.1 = (bf16[768,768]{1,0:T(8,128)(2,1)S(1)}, bf16[768,768]{1,0:T(8,128)(2,1)S(1)}) custom-call(s32[2]{0:T(128)S(1)} %pad_add_fusion.refs_0_, bf16[1024,768]{1,0:T(8,128)(2,1)S(1)} %copy-done.24, bf16[1024,768]{1,0:T(8,128)(2,1)S(1)} %get-tuple-element.133.refs_2_, bf16[1024,768]{1,0:T(8,128)(2,1)S(1)} %copy-done, ...), custom_call_target="tpu_custom_call" | custom-call | flops 49999998976 | bytes 1 | tf_op jit(solution)/shard_map/attn_a_w/pallas_call | solution.py:102
  147.4 7.7 %attend_back.4 = (bf16[1024,768]{1,0:T(8,128)(2,1)S(1)}, f32[1,768]{1,0:T(1,128)S(1)}) custom-call(s32[1,2]{1,0:T(1,128)S(1)} %copy-done.18, s32[12]{0:T(128)S(1)} %copy-done.19, bf16[1024,512]{1,0:T(8,128)(2,1)} %get-tuple-element.104.refs_2_, bf16[1024,512]{1,0:T(8,128)(2,1)} %get-tuple-element.105.refs_3_, bf16[1024,512]{1,0:T(8,128)(2,1)} %get-tuple-element.106.refs_4_, ...), custom_call_target="tpu_custom_call" | custom-call | flops 49999998976 | bytes 1 | tf_op jit(solution)/shard_map/attend_back/pallas_call | solution.py:102
  160.9 7.5 %attend_back.5 = (bf16[1024,768]{1,0:T(8,128)(2,1)S(1)}, f32[1,768]{1,0:T(1,128)S(1)}) custom-call(s32[1,2]{1,0:T(1,128)S(1)} %copy-done.18, s32[12]{0:T(128)S(1)} %copy-done.19, bf16[1024,512]{1,0:T(8,128)(2,1)} %get-tuple-element.104.refs_2_, bf16[1024,512]{1,0:T(8,128)(2,1)} %get-tuple-element.105.refs_3_, bf16[1024,512]{1,0:T(8,128)(2,1)} %get-tuple-element.106.refs_4_, ...), custom_call_target="tpu_custom_call" | custom-call | flops 49999998976 | bytes 1 | tf_op jit(solution)/shard_map/attend_back/pallas_call | solution.py:102
  170.6 4.7 %attn_b_w.1 = (bf16[832,768]{1,0:T(8,128)(2,1)S(1)}, bf16[832,768]{1,0:T(8,128)(2,1)S(1)}) custom-call(s32[2]{0:T(128)S(1)} %pad_add_fusion.refs_0_, bf16[1024,768]{1,0:T(8,128)(2,1)S(1)} %copy-done, bf16[1024,768]{1,0:T(8,128)(2,1)S(1)} %get-tuple-element.142.refs_2_.refs_1_, bf16[1024,768]{1,0:T(8,128)(2,1)S(1)} %copy-done, ...), custom_call_target="tpu_custom_call" | custom-call | flops 1000000000 | bytes 1 | tf_op jit(solution)/shard_map/attn_b_w/pallas_call | solution.py:102
  181.1 8.3 %input_grad.1.refs_3_ = bf16[1024,768]{1,0:T(8,128)(2,1)} custom-call(bf16[1024,768]{1,0:T(8,128)(2,1)S(1)} %copy-done.23, bf16[1024,768]{1,0:T(8,128)(2,1)S(1)} %get-tuple-element.142.refs_2_.refs_1_, bf16[1024,768]{1,0:T(8,128)(2,1)S(1)} %get-tuple-element.149.refs_4_.refs_2_, bf16[768,2304]{1,0:T(8,128)(2,1)} %refs_5_.9, bf16[768,2304]{1,0:T(8,128)(2,1)} %refs_5_.9, ...), custom_call_target="tpu_custom_call" | custom-call | flops 49999998976 | bytes 1 | tf_op jit(solution)/shard_map/input_grad/pallas_call | solution.py:102
  193.0 4.1 %mixed_place.1.refs_3_ = bf16[896,768]{1,0:T(8,128)(2,1)} custom-call(s32[1,1024]{1,0:T(1,128)S(1)} %copy-done.28, bf16[1024,768]{1,0:T(8,128)(2,1)} %bitcast.5.refs_1_, bf16[416,384]{1,0:T(8,128)(2,1)S(1)} %get-tuple-element.161.refs_2_.refs_1_), custom_call_target="tpu_custom_call" | custom-call | flops 10000000000 | bytes 1 | tf_op jit(solution)/shard_map/mixed_place/pallas_call | solution.py:102
  204.2 7.0 %collective-permute-done.20.refs_1_ = bf16[208,384]{1,0:T(8,128)(2,1)S(1)} collective-permute-done((bf16[208,384]{1,0:T(8,128)(2,1)S(1)}, bf16[208,384]{1,0:T(8,128)(2,1)S(1)}, u32[]{:S(2)}, u32[]{:S(2)}) %collective-permute-start.20) | collective-permute-done | bytes 159776 | tf_op jit(solution)/shard_map/ppermute | solution.py:656
  211.3 4.2 %collective-permute-done.19.refs_2_ = bf16[96,1536]{1,0:T(8,128)(2,1)S(1)} collective-permute-done((bf16[96,1536]{1,0:T(8,128)(2,1)S(1)}, bf16[96,1536]{1,0:T(8,128)(2,1)S(1)}, u32[]{:S(2)}, u32[]{:S(2)}) %collective-permute-start.19) | collective-permute-done | bytes 294944 | tf_op jit(solution)/shard_map/ppermute | solution.py:656
  227.5 4.9 %collective-permute-done.27.refs_2_ = bf16[192,1536]{1,0:T(8,128)(2,1)S(1)} collective-permute-done((bf16[192,1536]{1,0:T(8,128)(2,1)S(1)}, bf16[192,1536]{1,0:T(8,128)(2,1)S(1)}, u32[]{:S(2)}, u32[]{:S(2)}) %collective-permute-start.27) | collective-permute-done | bytes 589856 | tf_op jit(solution)/shard_map/ppermute | solution.py:656
  234.6 4.1 %collective-permute-done.24.refs_2_ = bf16[384,384]{1,0:T(8,128)(2,1)S(1)} collective-permute-done((bf16[384,384]{1,0:T(8,128)(2,1)S(1)}, bf16[384,384]{1,0:T(8,128)(2,1)S(1)}, u32[]{:S(2)}, u32[]{:S(2)}) %collective-permute-start.24) | collective-permute-done | bytes 294944 | tf_op jit(solution)/shard_map/ppermute | solution.py:656
  238.7 3.9 %collective-permute-done.26.refs_4_ = bf16[416,384]{1,0:T(8,128)(2,1)S(1)} collective-permute-done((bf16[416,384]{1,0:T(8,128)(2,1)S(1)}, bf16[416,384]{1,0:T(8,128)(2,1)S(1)}, u32[]{:S(2)}, u32[]{:S(2)}) %collective-permute-start.26) | collective-permute-done | bytes 319520 | tf_op jit(solution)/shard_map/ppermute | solution.py:656
  (141 shorter events, 60.6 us)
Async XLA Ops:
  2.5 15.8 %all-to-all-start = ((s32[32,1,32]{2,1,0:T(1,128)}), s32[32,1,32]{2,1,0:T(1,128)S(1)}, u32[]{:S(2)}, u32[]{:S(2)}) async-start(s32[32,1,32]{2,1,0:T(1,128)} %bitcast.2), calls=%async_computation | async-start | bytes 32768 | tf_op jit(solution)/shard_map/all_to_all | solution.py:778
  21.8 49.1 %all-to-all-start.2 = ((bf16[32,32,768]{2,1,0:T(8,128)(2,1)}), bf16[32,32,768]{2,1,0:T(8,128)(2,1)}, u32[]{:S(2)}, u32[]{:S(2)}) async-start(bf16[32,32,768]{2,1,0:T(8,128)(2,1)} %bitcast.8), calls=%async_computation.2 | async-start | bytes 3145728 | tf_op jit(solution)/shard_map/all_to_all | solution.py:816
  70.9 122.2 %all-to-all-start.1 = ((bf16[32,32,768]{2,1,0:T(8,128)(2,1)}), bf16[32,32,768]{2,1,0:T(8,128)(2,1)}, u32[]{:S(2)}, u32[]{:S(2)}) async-start(bf16[32,32,768]{2,1,0:T(8,128)(2,1)} %bitcast.4), calls=%async_computation.1 | async-start | bytes 3145728 | tf_op jit(solution)/shard_map/all_to_all | solution.py:866
  105.6 20.7 %collective-permute-start.3 = (bf16[1536,384]{1,0:T(8,128)(2,1)S(1)}, bf16[1536,384]{1,0:T(8,128)(2,1)S(1)}, u32[]{:S(2)}, u32[]{:S(2)}) collective-permute-start(bf16[1536,384]{1,0:T(8,128)(2,1)S(1)} %get-tuple-element.129), channel_id=1, source_target_pairs={{0,16},{1,17},{2,18},{3,19},{4,20},{5,21},{6,22},{7,23},{8,9},{9,8... | collective-permute-start | bytes 3538952 | tf_op jit(solution)/shard_map/ppermute | solution.py:666
  110.9 34.3 %collective-permute-start.2 = (bf16[384,1536]{1,0:T(8,128)(2,1)}, bf16[384,1536]{1,0:T(8,128)(2,1)}, u32[]{:S(2)}, u32[]{:S(2)}) collective-permute-start(bf16[384,1536]{1,0:T(8,128)(2,1)} %get-tuple-element.128), channel_id=1, source_target_pairs={{0,16},{1,17},{2,18},{3,19},{4,20},{5,21},{6,22},{7,23},{8,9},{9,8... | collective-permute-start | bytes 3538952 | tf_op jit(solution)/shard_map/ppermute | solution.py:666
  126.6 15.3 %collective-permute-start.4 = (bf16[768,384]{1,0:T(8,128)(2,1)S(1)}, bf16[768,384]{1,0:T(8,128)(2,1)S(1)}, u32[]{:S(2)}, u32[]{:S(2)}) collective-permute-start(bf16[768,384]{1,0:T(8,128)(2,1)S(1)} %get-tuple-element.132), channel_id=1, source_target_pairs={{0,1},{1,0},{2,3},{3,2},{4,5},{5,4},{6,7},{7,6},{8,24},{9,25},{10,... | collective-permute-start | bytes 1769480 | tf_op jit(solution)/shard_map/ppermute | solution.py:666
  140.3 18.3 %collective-permute-start.5 = (bf16[768,768]{1,0:T(8,128)(2,1)S(1)}, bf16[768,768]{1,0:T(8,128)(2,1)S(1)}, u32[]{:S(2)}, u32[]{:S(2)}) collective-permute-start(bf16[768,768]{1,0:T(8,128)(2,1)S(1)} %get-tuple-element.139.refs_3_), channel_id=1, source_target_pairs={{0,8},{8,0},{16,24},{24,16},{1,9},{9,1},{17,25},{25,17},{2,10},{10... | collective-permute-start | bytes 3538952 | tf_op jit(solution)/shard_map/ppermute | solution.py:656
  142.7 12.4 %collective-permute-start.7 = (bf16[384,384]{1,0:T(8,128)(2,1)S(1)}, bf16[384,384]{1,0:T(8,128)(2,1)S(1)}, u32[]{:S(2)}, u32[]{:S(2)}) collective-permute-start(bf16[384,384]{1,0:T(8,128)(2,1)S(1)} %get-tuple-element.145), channel_id=1, source_target_pairs={{0,2},{1,3},{2,0},{3,1},{4,6},{5,7},{6,4},{7,5},{8,10},{9,11},{10,... | collective-permute-start | bytes 884744 | tf_op jit(solution)/shard_map/ppermute | solution.py:656
  146.7 11.1 %collective-permute-start.6 = (bf16[192,1536]{1,0:T(8,128)(2,1)S(1)}, bf16[192,1536]{1,0:T(8,128)(2,1)S(1)}, u32[]{:S(2)}, u32[]{:S(2)}) collective-permute-start(bf16[192,1536]{1,0:T(8,128)(2,1)S(1)} %get-tuple-element.144), channel_id=1, source_target_pairs={{0,1},{1,0},{2,3},{3,2},{4,5},{5,4},{6,7},{7,6},{8,24},{9,25},{10,... | collective-permute-start | bytes 1769480 | tf_op jit(solution)/shard_map/ppermute | solution.py:666
  155.2 21.8 %collective-permute-start.10 = (bf16[384,384]{1,0:T(8,128)(2,1)S(1)}, bf16[384,384]{1,0:T(8,128)(2,1)S(1)}, u32[]{:S(2)}, u32[]{:S(2)}) collective-permute-start(bf16[384,384]{1,0:T(8,128)(2,1)S(1)} %w_down_a.1.refs_3_.refs_0_), channel_id=1, source_target_pairs={{0,4},{1,5},{2,6},{3,7},{4,0},{5,1},{6,2},{7,3},{8,12},{9,13},{10,... | collective-permute-start | bytes 884744 | tf_op jit(solution)/shard_map/ppermute | solution.py:656
  158.6 16.8 %collective-permute-start.11 = (bf16[96,1536]{1,0:T(8,128)(2,1)S(1)}, bf16[96,1536]{1,0:T(8,128)(2,1)S(1)}, u32[]{:S(2)}, u32[]{:S(2)}) collective-permute-start(bf16[96,1536]{1,0:T(8,128)(2,1)S(1)} %get-tuple-element.155), channel_id=1, source_target_pairs={{0,2},{1,3},{2,0},{3,1},{4,6},{5,7},{6,4},{7,5},{8,10},{9,11},{10,... | collective-permute-start | bytes 884744 | tf_op jit(solution)/shard_map/ppermute | solution.py:656
  159.6 9.9 %collective-permute-start.8 = (bf16[768,384]{1,0:T(8,128)(2,1)S(1)}, bf16[768,384]{1,0:T(8,128)(2,1)S(1)}, u32[]{:S(2)}, u32[]{:S(2)}) collective-permute-start(bf16[768,384]{1,0:T(8,128)(2,1)S(1)} %get-tuple-element.151), channel_id=1, source_target_pairs={{0,16},{1,17},{2,18},{3,19},{4,20},{5,21},{6,22},{7,23},{8,9},{9,8... | collective-permute-start | bytes 1769480 | tf_op jit(solution)/shard_map/ppermute | solution.py:666
  169.7 19.7 %collective-permute-start.13 = (bf16[384,384]{1,0:T(8,128)(2,1)S(1)}, bf16[384,384]{1,0:T(8,128)(2,1)S(1)}, u32[]{:S(2)}, u32[]{:S(2)}) collective-permute-start(bf16[384,384]{1,0:T(8,128)(2,1)S(1)} %get-tuple-element.158), channel_id=1, source_target_pairs={{0,1},{1,0},{2,3},{3,2},{4,5},{5,4},{6,7},{7,6},{8,24},{9,25},{10,... | collective-permute-start | bytes 884744 | tf_op jit(solution)/shard_map/ppermute | solution.py:666
  175.4 26.1 %collective-permute-start.15 = (bf16[96,1536]{1,0:T(8,128)(2,1)S(1)}, bf16[96,1536]{1,0:T(8,128)(2,1)S(1)}, u32[]{:S(2)}, u32[]{:S(2)}) collective-permute-start(bf16[96,1536]{1,0:T(8,128)(2,1)S(1)} %w_in_a.1.refs_2_.refs_0_), channel_id=1, source_target_pairs={{0,4},{1,5},{2,6},{3,7},{4,0},{5,1},{6,2},{7,3},{8,12},{9,13},{10,... | collective-permute-start | bytes 884744 | tf_op jit(solution)/shard_map/ppermute | solution.py:656
  177.0 23.1 %collective-permute-start.16 = (bf16[384,384]{1,0:T(8,128)(2,1)S(1)}, bf16[384,384]{1,0:T(8,128)(2,1)S(1)}, u32[]{:S(2)}, u32[]{:S(2)}) collective-permute-start(bf16[384,384]{1,0:T(8,128)(2,1)S(1)} %w_down_f.1.refs_3_.refs_1_), channel_id=1, source_target_pairs={{0,2},{1,3},{2,0},{3,1},{4,6},{5,7},{6,4},{7,5},{8,10},{9,11},{10,... | collective-permute-start | bytes 884744 | tf_op jit(solution)/shard_map/ppermute | solution.py:656
  179.8 11.5 %collective-permute-start.12 = (bf16[832,384]{1,0:T(8,128)(2,1)S(1)}, bf16[832,384]{1,0:T(8,128)(2,1)S(1)}, u32[]{:S(2)}, u32[]{:S(2)}) collective-permute-start(bf16[832,384]{1,0:T(8,128)(2,1)S(1)} %get-tuple-element.157), channel_id=1, source_target_pairs={{0,16},{1,17},{2,18},{3,19},{4,20},{5,21},{6,22},{7,23},{8,9},{9,8... | collective-permute-start | bytes 1916936 | tf_op jit(solution)/shard_map/ppermute | solution.py:666
  190.0 13.5 %collective-permute-start.14 = (bf16[192,384]{1,0:T(8,128)(2,1)S(1)}, bf16[192,384]{1,0:T(8,128)(2,1)S(1)}, u32[]{:S(2)}, u32[]{:S(2)}) collective-permute-start(bf16[192,384]{1,0:T(8,128)(2,1)S(1)} %get-tuple-element.162), channel_id=1, source_target_pairs={{0,2},{1,3},{2,0},{3,1},{4,6},{5,7},{6,4},{7,5},{8,10},{9,11},{10,... | collective-permute-start | bytes 442376 | tf_op jit(solution)/shard_map/ppermute | solution.py:656
  199.1 12.0 %collective-permute-start.20 = (bf16[208,384]{1,0:T(8,128)(2,1)S(1)}, bf16[208,384]{1,0:T(8,128)(2,1)S(1)}, u32[]{:S(2)}, u32[]{:S(2)}) collective-permute-start(bf16[208,384]{1,0:T(8,128)(2,1)S(1)} %get-tuple-element.165), channel_id=1, source_target_pairs={{0,2},{1,3},{2,0},{3,1},{4,6},{5,7},{6,4},{7,5},{8,10},{9,11},{10,... | collective-permute-start | bytes 479240 | tf_op jit(solution)/shard_map/ppermute | solution.py:656
  200.7 16.4 %collective-permute-start.23 = (bf16[768,384]{1,0:T(8,128)(2,1)S(1)}, bf16[768,384]{1,0:T(8,128)(2,1)S(1)}, u32[]{:S(2)}, u32[]{:S(2)}) collective-permute-start(bf16[768,384]{1,0:T(8,128)(2,1)S(1)} %w_down_g.1.refs_2_.refs_1_), channel_id=1, source_target_pairs={{0,1},{1,0},{2,3},{3,2},{4,5},{5,4},{6,7},{7,6},{8,9},{9,8},{10,11... | collective-permute-start | bytes 1769480 | tf_op jit(solution)/shard_map/ppermute | solution.py:656
  201.7 13.8 %collective-permute-start.19 = (bf16[96,1536]{1,0:T(8,128)(2,1)S(1)}, bf16[96,1536]{1,0:T(8,128)(2,1)S(1)}, u32[]{:S(2)}, u32[]{:S(2)}) collective-permute-start(bf16[96,1536]{1,0:T(8,128)(2,1)S(1)} %w_in_f.1.refs_2_.refs_1_), channel_id=1, source_target_pairs={{0,2},{1,3},{2,0},{3,1},{4,6},{5,7},{6,4},{7,5},{8,10},{9,11},{10,... | collective-permute-start | bytes 884744 | tf_op jit(solution)/shard_map/ppermute | solution.py:656
  203.6 13.4 %collective-permute-start.18 = (bf16[192,384]{1,0:T(8,128)(2,1)S(1)}, bf16[192,384]{1,0:T(8,128)(2,1)S(1)}, u32[]{:S(2)}, u32[]{:S(2)}) collective-permute-start(bf16[192,384]{1,0:T(8,128)(2,1)S(1)} %attn_a_a.1.refs_2_.refs_0_), channel_id=1, source_target_pairs={{0,4},{1,5},{2,6},{3,7},{4,0},{5,1},{6,2},{7,3},{8,12},{9,13},{10,... | collective-permute-start | bytes 442376 | tf_op jit(solution)/shard_map/ppermute | solution.py:656
  216.0 16.3 %collective-permute-start.27 = (bf16[192,1536]{1,0:T(8,128)(2,1)S(1)}, bf16[192,1536]{1,0:T(8,128)(2,1)S(1)}, u32[]{:S(2)}, u32[]{:S(2)}) collective-permute-start(bf16[192,1536]{1,0:T(8,128)(2,1)S(1)} %w_in_g.1.refs_2_.refs_1_), channel_id=1, source_target_pairs={{0,1},{1,0},{2,3},{3,2},{4,5},{5,4},{6,7},{7,6},{8,9},{9,8},{10,11... | collective-permute-start | bytes 1769480 | tf_op jit(solution)/shard_map/ppermute | solution.py:656
  224.0 14.7 %collective-permute-start.24 = (bf16[384,384]{1,0:T(8,128)(2,1)S(1)}, bf16[384,384]{1,0:T(8,128)(2,1)S(1)}, u32[]{:S(2)}, u32[]{:S(2)}) collective-permute-start(bf16[384,384]{1,0:T(8,128)(2,1)S(1)} %attn_a_g.1.refs_3_.refs_1_), channel_id=1, source_target_pairs={{0,1},{1,0},{2,3},{3,2},{4,5},{5,4},{6,7},{7,6},{8,9},{9,8},{10,11... | collective-permute-start | bytes 884744 | tf_op jit(solution)/shard_map/ppermute | solution.py:656
  226.2 16.3 %collective-permute-start.26 = (bf16[416,384]{1,0:T(8,128)(2,1)S(1)}, bf16[416,384]{1,0:T(8,128)(2,1)S(1)}, u32[]{:S(2)}, u32[]{:S(2)}) collective-permute-start(bf16[416,384]{1,0:T(8,128)(2,1)S(1)} %attn_b_g.1.refs_3_), channel_id=1, source_target_pairs={{0,1},{1,0},{2,3},{3,2},{4,5},{5,4},{6,7},{7,6},{8,9},{9,8},{10,11... | collective-permute-start | bytes 958472 | tf_op jit(solution)/shard_map/ppermute | solution.py:656
  (36 other events, 265.4 us)

commit v5 on v4

--- a/solution.py
+++ b/solution.py
@@ -416,37 +416,25 @@
 
 def first_back_kernel(
     pre2_ref, act_ref, wi_ref, normed_ref, inv_ref, gain_ref, wo_ref, linv0_ref, linv_ref,
-    pre1_ref, gattn_ref, gctx_ref, vec_ref, acc_ref,
+    pre1_ref, gattn_ref, gctx_ref, vec_ref,
 ):
-    step = pl.program_id(0)
-    part_sum = mm(act_ref[:, block_cols(step, wi_ref.shape[1])], wi_ref[...], NT)
-
-    @pl.when(step == 0)
-    def _():
-        acc_ref[...] = part_sum
-
-    @pl.when(step > 0)
-    def _():
-        acc_ref[...] += part_sum
-
-    @pl.when(step == pl.num_programs(0) - 1)
-    def _():
-        g_first = (pre2_ref[...] + acc_ref[...]).astype(BF).astype(F32)
-        normed = normed_ref[...].astype(F32)
-        g_pre = norm_back(g_first, normed, inv_ref[...], gain_ref[...].reshape(1, -1))
-        pre1_ref[...] = g_pre
-        g_attn = g_pre.astype(BF)
-        put_rows(
-            vec_ref,
-            jnp.sum(g_first * normed, axis=0, keepdims=True),
-            jnp.sum(g_first, axis=0, keepdims=True),
-            jnp.sum(g_attn.astype(F32), axis=0, keepdims=True),
-        )
-        g_ctx = mm(g_attn, wo_ref[...], NT)
-        cols = linv0_ref.shape[1]
-        gctx_ref[:, :cols] = (g_ctx[:, :cols] * linv0_ref[...]).astype(BF)
-        gctx_ref[:, cols:] = (g_ctx[:, cols:] * linv_ref[...]).astype(BF)
-        gattn_ref[...] = g_attn
+    g_first = pre2_ref[...] + mm(act_ref[...], wi_ref[...], NT)
+    g_first = g_first.astype(BF).astype(F32)
+    normed = normed_ref[...].astype(F32)
+    g_pre = norm_back(g_first, normed, inv_ref[...], gain_ref[...].reshape(1, -1))
+    pre1_ref[...] = g_pre
+    g_attn = g_pre.astype(BF)
+    put_rows(
+        vec_ref,
+        jnp.sum(g_first * normed, axis=0, keepdims=True),
+        jnp.sum(g_first, axis=0, keepdims=True),
+        jnp.sum(g_attn.astype(F32), axis=0, keepdims=True),
+    )
+    g_ctx = mm(g_attn, wo_ref[...], NT)
+    cols = linv0_ref.shape[1]
+    gctx_ref[:, :cols] = (g_ctx[:, :cols] * linv0_ref[...]).astype(BF)
+    gctx_ref[:, cols:] = (g_ctx[:, cols:] * linv_ref[...]).astype(BF)
+    gattn_ref[...] = g_attn
 
 
 def attend_back_kernel(
@@ -918,10 +906,10 @@
         first_back_kernel,
         "first_back",
         vmem=32,
-        grid=(4,),
+        grid=(1,),
         in_specs=[
             whole_block(bf_rows), whole_block(act_shape),
-            pl.BlockSpec((width, blk), lambda j: (0, j)),
+            whole_block((width, ff)),
             whole_block(bf_rows), whole_block((rows, 1)), vec_spec,
             whole_block((width, width)), whole_block(linv0.shape), whole_block(linv_rest.shape),
         ],
@@ -930,8 +918,7 @@
             whole_block((8, width)),
         ],
         out_shape=[hbm(bf_rows, F32), vmem(bf_rows, BF), vmem(bf_rows, BF), sds((8, width), F32)],
-        scratch=[pltpu.VMEM(bf_rows, F32)],
-        free=(0, 3, 6, 7, 8),
+        free=(0, 2, 3, 6, 7, 8),
     )(g_pre2, g_act, w_in, normed1, inv1, norm1_gain, w_out, linv0, linv_rest)
 
     projs, vecs = [], []
@@ -1017,12 +1004,12 @@
     (mixed,) = simple(
         chain, place_kernel, "mixed_place", (in_row, mixed_in), [hbm((ffn_rows, width), BF)]
     )
-    share_b.step_z()
     down_share.step_wide()
     in_share.step_back()
+    share_b.step_z()
     share_a.step_far()
+    in_share.step_wide()
     share_b.step_far()
-    in_share.step_wide()
     share_a.step_back()
     g_w_down = down_share.join()
     share_b.step_back()

time: 250 us -> 244 us (0.976)
  waiting for transfers between devices: 31.5 us -> 28.2 us
    ppermute x20, waiting for transfers between devices: 27.4 us -> 24.4 us  [exchange(): return lax.ppermute(values, axis, [(i, i ^ mask) for i in range(count)])]
  transfers between devices with their start and end apart: 31 -> 31, of which waited for: 11 -> 8; matrix products, arithmetic and copies ran while one was open for 0% -> 0% of each run, Pallas kernels for 63% -> 63%
where the time goes in v5:
time: 244 us; the launch traced here: 239 us
  Pallas kernels  158 us (65%)
  starting transfers between devices  50.4 us (21%)
  waiting for transfers between devices  28.2 us (12%)
    pallas_call x44, Pallas kernels, run(): outs = kernel(*placed, *[chain.place(a) for a in before])  158 us
    ppermute x20, waiting for transfers between devices, exchange(): return lax.ppermute(values, axis, [(i, i ^ mask) for i in range(count)])  24.4 us
    ppermute x20, starting transfers between devices, exchange(): return lax.ppermute(values, axis, [(i, i ^ mask) for i in range(count)])  19.5 us
    ppermute x8, starting transfers between devices, exchange_mixed(): return lax.ppermute(values, ('seq', 'batch'), pairs)  11 us
    all_to_all x1, starting transfers between devices, body(): lax.all_to_all(out_target, ('seq', 'batch'), split_axis=0, concat_axis=0,...  7.29 us
    all_to_all x1, starting transfers between devices, body(): lax.all_to_all(mixed_out, ('seq', 'batch'), split_axis=0, concat_axis=0,...  6.47 us
    all_to_all x1, starting transfers between devices, body(): lax.all_to_all(cot_out, ('seq', 'batch'), split_axis=0, concat_axis=0, ti...  6.13 us
  transfers between devices with their start and end apart: 31, of which 8 were waited for; matrix products, arithmetic and copies ran while one was open for 0% of the time, Pallas kernels for 63%

profile of v5, /device:TPU:0, one launch (start us, length us, event | category | flops | bytes accessed | tf_op | source)
XLA Modules:
  0.0 239.1 jit_solution(7431406119820886846)
XLA Ops:
  2.5 7.3 %all-to-all-start = ((s32[32,1,32]{2,1,0:T(1,128)}), s32[32,1,32]{2,1,0:T(1,128)S(1)}, u32[]{:S(2)}, u32[]{:S(2)}) async-start(s32[32,1,32]{2,1,0:T(1,128)} %bitcast.2), calls=%async_computation | async-start | bytes 32768 | tf_op jit(solution)/shard_map/all_to_all | solution.py:766
  9.8 8.4 %attend_first.1 = (bf16[1024,256]{1,0:T(8,128)(2,1)}, bf16[1024,256]{1,0:T(8,128)(2,1)}, bf16[1024,256]{1,0:T(8,128)(2,1)}, bf16[1024,256]{1,0:T(8,128)(2,1)}, b...) custom-call(s32[1,2]{1,0:T(1,128)S(1)} %copy-done.18, s32[12]{0:T(128)S(1)} %copy-done.19, ...), custom_call_target="tpu_custom_call" | custom-call | flops 49999998976 | bytes 1 | tf_op jit(solution)/shard_map/attend_first/pallas_call | solution.py:102
  18.3 3.5 %cot_gather.1 = (bf16[1024,768]{1,0:T(8,128)(2,1)}, s32[1,1024]{1,0:T(1,128)S(1)}) custom-call(s32[32,32]{1,0:T(8,128)S(1)} %bitcast.13, bf16[896,768]{1,0:T(8,128)(2,1)S(1)} %copy-done.7, bf16[1024,256]{1,0:T(8,128)(2,1)} %get-tuple-element.97.refs_2_), custom_call_target="tpu_custom_call" | custom-call | flops 10000000000 | bytes 1 | tf_op jit(solution)/shard_map/cot_gather/pallas_call | solution.py:102
  21.8 6.1 %all-to-all-start.2 = ((bf16[32,32,768]{2,1,0:T(8,128)(2,1)}), bf16[32,32,768]{2,1,0:T(8,128)(2,1)}, u32[]{:S(2)}, u32[]{:S(2)}) async-start(bf16[32,32,768]{2,1,0:T(8,128)(2,1)} %bitcast.8), calls=%async_computation.2 | async-start | bytes 3145728 | tf_op jit(solution)/shard_map/all_to_all | solution.py:804
  28.0 19.7 %attend_rest.1 = (bf16[1024,512]{1,0:T(8,128)(2,1)}, bf16[1024,512]{1,0:T(8,128)(2,1)}, bf16[1024,512]{1,0:T(8,128)(2,1)}, bf16[8,2,512,512]{3,2,1,0:T(8,128)(2,...) custom-call(s32[1,2]{1,0:T(1,128)S(1)} %copy-done.18, ...), custom_call_target="tpu_custom_call" | custom-call | flops 49999998976 | bytes 1 | tf_op jit(solution)/shard_map/attend_rest/pallas_call | solution.py:102
  47.8 20.1 %ffn.1 = (bf16[1024,3072]{1,0:T(8,128)(2,1)}, bf16[1024,3072]{1,0:T(8,128)(2,1)}, bf16[1024,768]{1,0:T(8,128)(2,1)}, f32[1024,1]{1,0:T(8,128)}, bf16[1024,768]{1,0:T(8,128)(2,1)S(1)}) custom-call(bf16[1024,768]{1,0:T(8,128)(2,1)} %get-tuple-element.100.refs_0_.refs_1_, bf16[768,3072]{1,0:T(8,128)(2,1)} %refs_2_.9, f32[3072]{0:T(1024)S(1)} %copy-done.9, ...), custom_call_target="tpu_custom_call" | custom-call | flops 49999998976 | bytes 1 | tf_op jit(solution)/shard_map/ffn/pallas_call | solution.py:102
  67.9 3.0 %mixed_slots.1.refs_5_ = bf16[1024,768]{1,0:T(8,128)(2,1)} custom-call(s32[1,1024]{1,0:T(1,128)S(1)} %get-tuple-element.96.refs_7_.refs_0_, bf16[1024,768]{1,0:T(8,128)(2,1)S(1)} %get-tuple-element.102.refs_1_, f32[1024,1]{1,0:T(8,128)} %get-tuple-element.103.refs_2_.refs_3_), custom_call_target="tpu_custom_call" | custom-call | flops 49999998976 | bytes 1 | tf_op jit(solution)/shard_map/mixed_slots/pallas_call | solution.py:102
  70.9 6.5 %all-to-all-start.1 = ((bf16[32,32,768]{2,1,0:T(8,128)(2,1)}), bf16[32,32,768]{2,1,0:T(8,128)(2,1)}, u32[]{:S(2)}, u32[]{:S(2)}) async-start(bf16[32,32,768]{2,1,0:T(8,128)(2,1)} %bitcast.4), calls=%async_computation.1 | async-start | bytes 3145728 | tf_op jit(solution)/shard_map/all_to_all | solution.py:854
  77.3 5.4 %cot_back.1 = (f32[1024,768]{1,0:T(8,128)S(1)}, bf16[1024,768]{1,0:T(8,128)(2,1)S(1)}, f32[8,768]{1,0:T(8,128)S(1)}) custom-call(s32[1,1024]{1,0:T(1,128)S(1)} %get-tuple-element.96.refs_7_.refs_0_, bf16[1024,768]{1,0:T(8,128)(2,1)} %bitcast.9.refs_1_, bf16[1024,768]{1,0:T(8,128)(2,1)} %get-tuple-element.109.refs_2_, ...), custom_call_target="tpu_custom_call" | custom-call | flops 49999998976 | bytes 1 | tf_op jit(solution)/shard_map/cot_back/pallas_call | solution.py:102
  82.7 14.1 %down_back.1 = (bf16[1024,3072]{1,0:T(8,128)(2,1)S(1)}, f32[1,3072]{1,0:T(1,128)S(1)}, bf16[2,768,768]{2,1,0:T(8,128)(2,1)S(1)}, bf16[2,768,768]{2,1,0:T(8,128)(2,1)S(1)}) custom-call(s32[2]{0:T(128)S(1)} %pad_add_fusion.refs_0_, bf16[1024,768]{1,0:T(8,128)(2,1)S(1)} %get-tuple-element.111.refs_1_, bf16[3072,768]{1,0:T(8,128)(2,1)} %refs_2_.8, ...), custom_call_target="tpu_custom_call" | custom-call | flops 49999998976 | bytes 1 | tf_op jit(solution)/shard_map/down_back/pallas_call | solution.py:102
  97.3 7.0 %in_back.1 = (bf16[384,3072]{1,0:T(8,128)(2,1)S(1)}, bf16[384,3072]{1,0:T(8,128)(2,1)S(1)}) custom-call(s32[2]{0:T(128)S(1)} %pad_add_fusion.refs_0_, bf16[1024,768]{1,0:T(8,128)(2,1)S(1)} %copy-done.25, bf16[1024,3072]{1,0:T(8,128)(2,1)S(1)} %get-tuple-element.115.refs_2_.refs_1_, f32[1,3072]{1,0:T(1,128)S(1)} %get-tuple-element.119.refs_3_.refs_6_), custom_call_target="tpu_custom_call" | custom-call | flops 49999998976 | bytes 1 | tf_op jit(solution)/shard_map/in_back/pallas_call | solution.py:102
  112.8 12.0 %first_back.1 = (f32[1024,768]{1,0:T(8,128)}, bf16[1024,768]{1,0:T(8,128)(2,1)S(1)}, bf16[1024,768]{1,0:T(8,128)(2,1)S(1)}, f32[8,768]{1,0:T(8,128)S(1)}) custom-call(f32[1024,768]{1,0:T(8,128)S(1)} %get-tuple-element.110.refs_0_, bf16[1024,3072]{1,0:T(8,128)(2,1)S(1)} %get-tuple-element.115.refs_2_.refs_1_, bf16[768,3072]{1,0:T(8,128)(2,1)} %refs_2_.9, ...), custom_call_target="tpu_custom_call" | custom-call | flops 49999998976 | bytes 1 | tf_op jit(solution)/shard_map/first_back/pallas_call | solution.py:102
  126.6 7.8 %attend_back.3 = (bf16[1024,768]{1,0:T(8,128)(2,1)S(1)}, f32[1,768]{1,0:T(1,128)S(1)}) custom-call(s32[1,2]{1,0:T(1,128)S(1)} %copy-done.18, s32[12]{0:T(128)S(1)} %copy-done.19, bf16[1024,256]{1,0:T(8,128)(2,1)} %get-tuple-element.97.refs_2_, bf16[1024,256]{1,0:T(8,128)(2,1)} %get-tuple-element.134.refs_3_, bf16[1024,256]{1,0:T(8,128)(2,1)} %get-tuple-element.135.refs_4_, ...), custom_call_target="tpu_custom_call" | custom-call | flops 49999998976 | bytes 1 | tf_op jit(solution)/shard_map/attend_back/pallas_call | solution.py:102
  134.5 4.5 %attn_a_w.1 = (bf16[768,768]{1,0:T(8,128)(2,1)S(1)}, bf16[768,768]{1,0:T(8,128)(2,1)S(1)}) custom-call(s32[2]{0:T(128)S(1)} %pad_add_fusion.refs_0_, bf16[1024,768]{1,0:T(8,128)(2,1)S(1)} %copy-done.24, bf16[1024,768]{1,0:T(8,128)(2,1)S(1)} %get-tuple-element.133.refs_2_, bf16[1024,768]{1,0:T(8,128)(2,1)S(1)} %copy-done, ...), custom_call_target="tpu_custom_call" | custom-call | flops 49999998976 | bytes 1 | tf_op jit(solution)/shard_map/attn_a_w/pallas_call | solution.py:102
  146.7 7.5 %attend_back.4 = (bf16[1024,768]{1,0:T(8,128)(2,1)S(1)}, f32[1,768]{1,0:T(1,128)S(1)}) custom-call(s32[1,2]{1,0:T(1,128)S(1)} %copy-done.18, s32[12]{0:T(128)S(1)} %copy-done.19, bf16[1024,512]{1,0:T(8,128)(2,1)} %get-tuple-element.104.refs_2_, bf16[1024,512]{1,0:T(8,128)(2,1)} %get-tuple-element.105.refs_3_, bf16[1024,512]{1,0:T(8,128)(2,1)} %get-tuple-element.106.refs_4_, ...), custom_call_target="tpu_custom_call" | custom-call | flops 49999998976 | bytes 1 | tf_op jit(solution)/shard_map/attend_back/pallas_call | solution.py:102
  154.4 2.5 %collective-permute-start.10 = (bf16[384,384]{1,0:T(8,128)(2,1)S(1)}, bf16[384,384]{1,0:T(8,128)(2,1)S(1)}, u32[]{:S(2)}, u32[]{:S(2)}) collective-permute-start(bf16[384,384]{1,0:T(8,128)(2,1)S(1)} %w_down_a.1.refs_3_.refs_0_), channel_id=1, source_target_pairs={{0,4},{1,5},{2,6},{3,7},{4,0},{5,1},{6,2},{7,3},{8,12},{9,13},{10,... | collective-permute-start | bytes 884744 | tf_op jit(solution)/shard_map/ppermute | solution.py:644
  160.0 7.5 %attend_back.5 = (bf16[1024,768]{1,0:T(8,128)(2,1)S(1)}, f32[1,768]{1,0:T(1,128)S(1)}) custom-call(s32[1,2]{1,0:T(1,128)S(1)} %copy-done.18, s32[12]{0:T(128)S(1)} %copy-done.19, bf16[1024,512]{1,0:T(8,128)(2,1)} %get-tuple-element.104.refs_2_, bf16[1024,512]{1,0:T(8,128)(2,1)} %get-tuple-element.105.refs_3_, bf16[1024,512]{1,0:T(8,128)(2,1)} %get-tuple-element.106.refs_4_, ...), custom_call_target="tpu_custom_call" | custom-call | flops 49999998976 | bytes 1 | tf_op jit(solution)/shard_map/attend_back/pallas_call | solution.py:102
  170.1 4.9 %attn_b_w.1 = (bf16[832,768]{1,0:T(8,128)(2,1)S(1)}, bf16[832,768]{1,0:T(8,128)(2,1)S(1)}) custom-call(s32[2]{0:T(128)S(1)} %pad_add_fusion.refs_0_, bf16[1024,768]{1,0:T(8,128)(2,1)S(1)} %copy-done, bf16[1024,768]{1,0:T(8,128)(2,1)S(1)} %get-tuple-element.142.refs_2_.refs_1_, bf16[1024,768]{1,0:T(8,128)(2,1)S(1)} %copy-done, ...), custom_call_target="tpu_custom_call" | custom-call | flops 1000000000 | bytes 1 | tf_op jit(solution)/shard_map/attn_b_w/pallas_call | solution.py:102
  180.2 8.1 %input_grad.1.refs_3_ = bf16[1024,768]{1,0:T(8,128)(2,1)} custom-call(bf16[1024,768]{1,0:T(8,128)(2,1)S(1)} %copy-done.23, bf16[1024,768]{1,0:T(8,128)(2,1)S(1)} %get-tuple-element.142.refs_2_.refs_1_, bf16[1024,768]{1,0:T(8,128)(2,1)S(1)} %get-tuple-element.149.refs_4_.refs_2_, bf16[768,2304]{1,0:T(8,128)(2,1)} %refs_5_.9, bf16[768,2304]{1,0:T(8,128)(2,1)} %refs_5_.9, ...), custom_call_target="tpu_custom_call" | custom-call | flops 49999998976 | bytes 1 | tf_op jit(solution)/shard_map/input_grad/pallas_call | solution.py:102
  191.7 4.1 %mixed_place.1.refs_3_ = bf16[896,768]{1,0:T(8,128)(2,1)} custom-call(s32[1,1024]{1,0:T(1,128)S(1)} %copy-done.28, bf16[1024,768]{1,0:T(8,128)(2,1)} %bitcast.5.refs_1_, bf16[416,384]{1,0:T(8,128)(2,1)S(1)} %get-tuple-element.161.refs_2_.refs_1_), custom_call_target="tpu_custom_call" | custom-call | flops 10000000000 | bytes 1 | tf_op jit(solution)/shard_map/mixed_place/pallas_call | solution.py:102
  201.5 8.5 %collective-permute-done.20.refs_2_ = bf16[96,1536]{1,0:T(8,128)(2,1)S(1)} collective-permute-done((bf16[96,1536]{1,0:T(8,128)(2,1)S(1)}, bf16[96,1536]{1,0:T(8,128)(2,1)S(1)}, u32[]{:S(2)}, u32[]{:S(2)}) %collective-permute-start.20) | collective-permute-done | bytes 294944 | tf_op jit(solution)/shard_map/ppermute | solution.py:644
  216.7 3.7 %collective-permute-done.22.refs_1_ = bf16[208,384]{1,0:T(8,128)(2,1)S(1)} collective-permute-done((bf16[208,384]{1,0:T(8,128)(2,1)S(1)}, bf16[208,384]{1,0:T(8,128)(2,1)S(1)}, u32[]{:S(2)}, u32[]{:S(2)}) %collective-permute-start.22) | collective-permute-done | bytes 159776 | tf_op jit(solution)/shard_map/ppermute | solution.py:644
  222.1 3.7 %collective-permute-done.25.refs_2_ = bf16[208,384]{1,0:T(8,128)(2,1)S(1)} collective-permute-done((bf16[208,384]{1,0:T(8,128)(2,1)S(1)}, bf16[208,384]{1,0:T(8,128)(2,1)S(1)}, u32[]{:S(2)}, u32[]{:S(2)}) %collective-permute-start.25) | collective-permute-done | bytes 159776 | tf_op jit(solution)/shard_map/ppermute | solution.py:644
  231.2 5.6 %collective-permute-done.26.refs_4_ = bf16[416,384]{1,0:T(8,128)(2,1)S(1)} collective-permute-done((bf16[416,384]{1,0:T(8,128)(2,1)S(1)}, bf16[416,384]{1,0:T(8,128)(2,1)S(1)}, u32[]{:S(2)}, u32[]{:S(2)}) %collective-permute-start.26) | collective-permute-done | bytes 319520 | tf_op jit(solution)/shard_map/ppermute | solution.py:644
  (141 shorter events, 56.2 us)
Async XLA Ops:
  2.5 15.8 %all-to-all-start = ((s32[32,1,32]{2,1,0:T(1,128)}), s32[32,1,32]{2,1,0:T(1,128)S(1)}, u32[]{:S(2)}, u32[]{:S(2)}) async-start(s32[32,1,32]{2,1,0:T(1,128)} %bitcast.2), calls=%async_computation | async-start | bytes 32768 | tf_op jit(solution)/shard_map/all_to_all | solution.py:766
  21.8 49.1 %all-to-all-start.2 = ((bf16[32,32,768]{2,1,0:T(8,128)(2,1)}), bf16[32,32,768]{2,1,0:T(8,128)(2,1)}, u32[]{:S(2)}, u32[]{:S(2)}) async-start(bf16[32,32,768]{2,1,0:T(8,128)(2,1)} %bitcast.8), calls=%async_computation.2 | async-start | bytes 3145728 | tf_op jit(solution)/shard_map/all_to_all | solution.py:804
  70.9 120.9 %all-to-all-start.1 = ((bf16[32,32,768]{2,1,0:T(8,128)(2,1)}), bf16[32,32,768]{2,1,0:T(8,128)(2,1)}, u32[]{:S(2)}, u32[]{:S(2)}) async-start(bf16[32,32,768]{2,1,0:T(8,128)(2,1)} %bitcast.4), calls=%async_computation.1 | async-start | bytes 3145728 | tf_op jit(solution)/shard_map/all_to_all | solution.py:854
  105.8 18.9 %collective-permute-start.3 = (bf16[1536,384]{1,0:T(8,128)(2,1)S(1)}, bf16[1536,384]{1,0:T(8,128)(2,1)S(1)}, u32[]{:S(2)}, u32[]{:S(2)}) collective-permute-start(bf16[1536,384]{1,0:T(8,128)(2,1)S(1)} %get-tuple-element.129), channel_id=1, source_target_pairs={{0,16},{1,17},{2,18},{3,19},{4,20},{5,21},{6,22},{7,23},{8,9},{9,8... | collective-permute-start | bytes 3538952 | tf_op jit(solution)/shard_map/ppermute | solution.py:654
  111.1 32.5 %collective-permute-start.2 = (bf16[384,1536]{1,0:T(8,128)(2,1)}, bf16[384,1536]{1,0:T(8,128)(2,1)}, u32[]{:S(2)}, u32[]{:S(2)}) collective-permute-start(bf16[384,1536]{1,0:T(8,128)(2,1)} %get-tuple-element.128), channel_id=1, source_target_pairs={{0,16},{1,17},{2,18},{3,19},{4,20},{5,21},{6,22},{7,23},{8,9},{9,8... | collective-permute-start | bytes 3538952 | tf_op jit(solution)/shard_map/ppermute | solution.py:654
  125.1 16.3 %collective-permute-start.4 = (bf16[768,384]{1,0:T(8,128)(2,1)S(1)}, bf16[768,384]{1,0:T(8,128)(2,1)S(1)}, u32[]{:S(2)}, u32[]{:S(2)}) collective-permute-start(bf16[768,384]{1,0:T(8,128)(2,1)S(1)} %get-tuple-element.132), channel_id=1, source_target_pairs={{0,1},{1,0},{2,3},{3,2},{4,5},{5,4},{6,7},{7,6},{8,24},{9,25},{10,... | collective-permute-start | bytes 1769480 | tf_op jit(solution)/shard_map/ppermute | solution.py:654
  139.0 19.2 %collective-permute-start.5 = (bf16[768,768]{1,0:T(8,128)(2,1)S(1)}, bf16[768,768]{1,0:T(8,128)(2,1)S(1)}, u32[]{:S(2)}, u32[]{:S(2)}) collective-permute-start(bf16[768,768]{1,0:T(8,128)(2,1)S(1)} %get-tuple-element.139.refs_3_), channel_id=1, source_target_pairs={{0,8},{8,0},{16,24},{24,16},{1,9},{9,1},{17,25},{25,17},{2,10},{10... | collective-permute-start | bytes 3538952 | tf_op jit(solution)/shard_map/ppermute | solution.py:644
  142.1 12.2 %collective-permute-start.7 = (bf16[384,384]{1,0:T(8,128)(2,1)S(1)}, bf16[384,384]{1,0:T(8,128)(2,1)S(1)}, u32[]{:S(2)}, u32[]{:S(2)}) collective-permute-start(bf16[384,384]{1,0:T(8,128)(2,1)S(1)} %get-tuple-element.145), channel_id=1, source_target_pairs={{0,2},{1,3},{2,0},{3,1},{4,6},{5,7},{6,4},{7,5},{8,10},{9,11},{10,... | collective-permute-start | bytes 884744 | tf_op jit(solution)/shard_map/ppermute | solution.py:644
  145.2 11.7 %collective-permute-start.6 = (bf16[192,1536]{1,0:T(8,128)(2,1)S(1)}, bf16[192,1536]{1,0:T(8,128)(2,1)S(1)}, u32[]{:S(2)}, u32[]{:S(2)}) collective-permute-start(bf16[192,1536]{1,0:T(8,128)(2,1)S(1)} %get-tuple-element.144), channel_id=1, source_target_pairs={{0,1},{1,0},{2,3},{3,2},{4,5},{5,4},{6,7},{7,6},{8,24},{9,25},{10,... | collective-permute-start | bytes 1769480 | tf_op jit(solution)/shard_map/ppermute | solution.py:654
  154.4 22.2 %collective-permute-start.10 = (bf16[384,384]{1,0:T(8,128)(2,1)S(1)}, bf16[384,384]{1,0:T(8,128)(2,1)S(1)}, u32[]{:S(2)}, u32[]{:S(2)}) collective-permute-start(bf16[384,384]{1,0:T(8,128)(2,1)S(1)} %w_down_a.1.refs_3_.refs_0_), channel_id=1, source_target_pairs={{0,4},{1,5},{2,6},{3,7},{4,0},{5,1},{6,2},{7,3},{8,12},{9,13},{10,... | collective-permute-start | bytes 884744 | tf_op jit(solution)/shard_map/ppermute | solution.py:644
  157.6 17.5 %collective-permute-start.11 = (bf16[96,1536]{1,0:T(8,128)(2,1)S(1)}, bf16[96,1536]{1,0:T(8,128)(2,1)S(1)}, u32[]{:S(2)}, u32[]{:S(2)}) collective-permute-start(bf16[96,1536]{1,0:T(8,128)(2,1)S(1)} %get-tuple-element.155), channel_id=1, source_target_pairs={{0,2},{1,3},{2,0},{3,1},{4,6},{5,7},{6,4},{7,5},{8,10},{9,11},{10,... | collective-permute-start | bytes 884744 | tf_op jit(solution)/shard_map/ppermute | solution.py:644
  159.1 9.9 %collective-permute-start.8 = (bf16[768,384]{1,0:T(8,128)(2,1)S(1)}, bf16[768,384]{1,0:T(8,128)(2,1)S(1)}, u32[]{:S(2)}, u32[]{:S(2)}) collective-permute-start(bf16[768,384]{1,0:T(8,128)(2,1)S(1)} %get-tuple-element.151), channel_id=1, source_target_pairs={{0,16},{1,17},{2,18},{3,19},{4,20},{5,21},{6,22},{7,23},{8,9},{9,8... | collective-permute-start | bytes 1769480 | tf_op jit(solution)/shard_map/ppermute | solution.py:654
  169.2 19.1 %collective-permute-start.13 = (bf16[384,384]{1,0:T(8,128)(2,1)S(1)}, bf16[384,384]{1,0:T(8,128)(2,1)S(1)}, u32[]{:S(2)}, u32[]{:S(2)}) collective-permute-start(bf16[384,384]{1,0:T(8,128)(2,1)S(1)} %get-tuple-element.158), channel_id=1, source_target_pairs={{0,1},{1,0},{2,3},{3,2},{4,5},{5,4},{6,7},{7,6},{8,24},{9,25},{10,... | collective-permute-start | bytes 884744 | tf_op jit(solution)/shard_map/ppermute | solution.py:654
  175.1 21.9 %collective-permute-start.16 = (bf16[96,1536]{1,0:T(8,128)(2,1)S(1)}, bf16[96,1536]{1,0:T(8,128)(2,1)S(1)}, u32[]{:S(2)}, u32[]{:S(2)}) collective-permute-start(bf16[96,1536]{1,0:T(8,128)(2,1)S(1)} %w_in_a.1.refs_2_.refs_0_), channel_id=1, source_target_pairs={{0,4},{1,5},{2,6},{3,7},{4,0},{5,1},{6,2},{7,3},{8,12},{9,13},{10,... | collective-permute-start | bytes 884744 | tf_op jit(solution)/shard_map/ppermute | solution.py:644
  176.6 19.2 %collective-permute-start.17 = (bf16[384,384]{1,0:T(8,128)(2,1)S(1)}, bf16[384,384]{1,0:T(8,128)(2,1)S(1)}, u32[]{:S(2)}, u32[]{:S(2)}) collective-permute-start(bf16[384,384]{1,0:T(8,128)(2,1)S(1)} %w_down_f.1.refs_3_.refs_1_), channel_id=1, source_target_pairs={{0,2},{1,3},{2,0},{3,1},{4,6},{5,7},{6,4},{7,5},{8,10},{9,11},{10,... | collective-permute-start | bytes 884744 | tf_op jit(solution)/shard_map/ppermute | solution.py:644
  179.2 10.8 %collective-permute-start.12 = (bf16[832,384]{1,0:T(8,128)(2,1)S(1)}, bf16[832,384]{1,0:T(8,128)(2,1)S(1)}, u32[]{:S(2)}, u32[]{:S(2)}) collective-permute-start(bf16[832,384]{1,0:T(8,128)(2,1)S(1)} %get-tuple-element.157), channel_id=1, source_target_pairs={{0,16},{1,17},{2,18},{3,19},{4,20},{5,21},{6,22},{7,23},{8,9},{9,8... | collective-permute-start | bytes 1916936 | tf_op jit(solution)/shard_map/ppermute | solution.py:654
  188.9 9.9 %collective-permute-start.14 = (bf16[192,384]{1,0:T(8,128)(2,1)S(1)}, bf16[192,384]{1,0:T(8,128)(2,1)S(1)}, u32[]{:S(2)}, u32[]{:S(2)}) collective-permute-start(bf16[192,384]{1,0:T(8,128)(2,1)S(1)} %get-tuple-element.162), channel_id=1, source_target_pairs={{0,2},{1,3},{2,0},{3,1},{4,6},{5,7},{6,4},{7,5},{8,10},{9,11},{10,... | collective-permute-start | bytes 442376 | tf_op jit(solution)/shard_map/ppermute | solution.py:644
  196.4 18.1 %collective-permute-start.23 = (bf16[768,384]{1,0:T(8,128)(2,1)S(1)}, bf16[768,384]{1,0:T(8,128)(2,1)S(1)}, u32[]{:S(2)}, u32[]{:S(2)}) collective-permute-start(bf16[768,384]{1,0:T(8,128)(2,1)S(1)} %w_down_g.1.refs_2_.refs_1_), channel_id=1, source_target_pairs={{0,1},{1,0},{2,3},{3,2},{4,5},{5,4},{6,7},{7,6},{8,9},{9,8},{10,11... | collective-permute-start | bytes 1769480 | tf_op jit(solution)/shard_map/ppermute | solution.py:644
  197.1 13.0 %collective-permute-start.20 = (bf16[96,1536]{1,0:T(8,128)(2,1)S(1)}, bf16[96,1536]{1,0:T(8,128)(2,1)S(1)}, u32[]{:S(2)}, u32[]{:S(2)}) collective-permute-start(bf16[96,1536]{1,0:T(8,128)(2,1)S(1)} %w_in_f.1.refs_3_.refs_1_), channel_id=1, source_target_pairs={{0,2},{1,3},{2,0},{3,1},{4,6},{5,7},{6,4},{7,5},{8,10},{9,11},{10,... | collective-permute-start | bytes 884744 | tf_op jit(solution)/shard_map/ppermute | solution.py:644
  198.9 14.5 %collective-permute-start.18 = (bf16[192,384]{1,0:T(8,128)(2,1)S(1)}, bf16[192,384]{1,0:T(8,128)(2,1)S(1)}, u32[]{:S(2)}, u32[]{:S(2)}) collective-permute-start(bf16[192,384]{1,0:T(8,128)(2,1)S(1)} %attn_a_a.1.refs_3_.refs_0_), channel_id=1, source_target_pairs={{0,4},{1,5},{2,6},{3,7},{4,0},{5,1},{6,2},{7,3},{8,12},{9,13},{10,... | collective-permute-start | bytes 442376 | tf_op jit(solution)/shard_map/ppermute | solution.py:644
  200.2 11.9 %collective-permute-start.19 = (bf16[208,384]{1,0:T(8,128)(2,1)S(1)}, bf16[208,384]{1,0:T(8,128)(2,1)S(1)}, u32[]{:S(2)}, u32[]{:S(2)}) collective-permute-start(bf16[208,384]{1,0:T(8,128)(2,1)S(1)} %get-tuple-element.165), channel_id=1, source_target_pairs={{0,2},{1,3},{2,0},{3,1},{4,6},{5,7},{6,4},{7,5},{8,10},{9,11},{10,... | collective-permute-start | bytes 479240 | tf_op jit(solution)/shard_map/ppermute | solution.py:644
  210.7 16.7 %collective-permute-start.27 = (bf16[192,1536]{1,0:T(8,128)(2,1)S(1)}, bf16[192,1536]{1,0:T(8,128)(2,1)S(1)}, u32[]{:S(2)}, u32[]{:S(2)}) collective-permute-start(bf16[192,1536]{1,0:T(8,128)(2,1)S(1)} %w_in_g.1.refs_2_.refs_1_), channel_id=1, source_target_pairs={{0,1},{1,0},{2,3},{3,2},{4,5},{5,4},{6,7},{7,6},{8,9},{9,8},{10,11... | collective-permute-start | bytes 1769480 | tf_op jit(solution)/shard_map/ppermute | solution.py:644
  221.2 10.0 %collective-permute-start.24 = (bf16[384,384]{1,0:T(8,128)(2,1)S(1)}, bf16[384,384]{1,0:T(8,128)(2,1)S(1)}, u32[]{:S(2)}, u32[]{:S(2)}) collective-permute-start(bf16[384,384]{1,0:T(8,128)(2,1)S(1)} %attn_a_g.1.refs_3_.refs_1_), channel_id=1, source_target_pairs={{0,1},{1,0},{2,3},{3,2},{4,5},{5,4},{6,7},{7,6},{8,9},{9,8},{10,11... | collective-permute-start | bytes 884744 | tf_op jit(solution)/shard_map/ppermute | solution.py:644
  226.4 10.4 %collective-permute-start.26 = (bf16[416,384]{1,0:T(8,128)(2,1)S(1)}, bf16[416,384]{1,0:T(8,128)(2,1)S(1)}, u32[]{:S(2)}, u32[]{:S(2)}) collective-permute-start(bf16[416,384]{1,0:T(8,128)(2,1)S(1)} %attn_b_g.1.refs_3_), channel_id=1, source_target_pairs={{0,1},{1,0},{2,3},{3,2},{4,5},{5,4},{6,7},{7,6},{8,9},{9,8},{10,11... | collective-permute-start | bytes 958472 | tf_op jit(solution)/shard_map/ppermute | solution.py:644
  (36 other events, 266.2 us)

commit v6 on v5

--- a/solution.py
+++ b/solution.py
@@ -870,7 +870,7 @@
         chain,
         down_back_kernel,
         "down_back",
-        vmem=24,
+        vmem=18,
         grid=(4,),
         in_specs=[whole_block(bf_rows), quarter_rows, quarter_cols, quarter_cols],
         out_specs=[
@@ -905,7 +905,7 @@
         chain,
         first_back_kernel,
         "first_back",
-        vmem=32,
+        vmem=20,
         grid=(1,),
         in_specs=[
             whole_block(bf_rows), whole_block(act_shape),
@@ -917,7 +917,7 @@
             whole_block(bf_rows), whole_block(bf_rows), whole_block(bf_rows),
             whole_block((8, width)),
         ],
-        out_shape=[hbm(bf_rows, F32), vmem(bf_rows, BF), vmem(bf_rows, BF), sds((8, width), F32)],
+        out_shape=[vmem(bf_rows, F32), vmem(bf_rows, BF), vmem(bf_rows, BF), sds((8, width), F32)],
         free=(0, 2, 3, 6, 7, 8),
     )(g_pre2, g_act, w_in, normed1, inv1, norm1_gain, w_out, linv0, linv_rest)
 
@@ -932,7 +932,7 @@
             chain,
             functools.partial(attend_back_kernel, g * heads, pair),
             "attend_back",
-            vmem=20,
+            vmem=14,
             grid=(steps,),
             in_specs=[
                 smem(), smem(), head_col, head_col, head_col,
@@ -986,7 +986,7 @@
         chain,
         functools.partial(input_grad_kernel, groups),
         "input_grad",
-        vmem=24,
+        vmem=18,
         grid=(groups,),
         in_specs=[whole_block((rows, 3 * cols))] * groups
         + [

time: 244 us -> 244 us (level)
  transfers between devices with their start and end apart: 31 -> 31, of which waited for: 8 -> 8; matrix products, arithmetic and copies ran while one was open for 0% -> 0% of each run, Pallas kernels for 63% -> 62%
where the time goes in v6:
time: 244 us; the launch traced here: 239 us
  Pallas kernels  156 us (64%)
  starting transfers between devices  51.4 us (21%)
  waiting for transfers between devices  28.7 us (12%)
    pallas_call x44, Pallas kernels, run(): outs = kernel(*placed, *[chain.place(a) for a in before])  156 us
    ppermute x20, waiting for transfers between devices, exchange(): return lax.ppermute(values, axis, [(i, i ^ mask) for i in range(count)])  25.7 us
    ppermute x20, starting transfers between devices, exchange(): return lax.ppermute(values, axis, [(i, i ^ mask) for i in range(count)])  18.6 us
    ppermute x8, starting transfers between devices, exchange_mixed(): return lax.ppermute(values, ('seq', 'batch'), pairs)  12.9 us
    all_to_all x1, starting transfers between devices, body(): lax.all_to_all(out_target, ('seq', 'batch'), split_axis=0, concat_axis=0,...  7.29 us
    all_to_all x1, starting transfers between devices, body(): lax.all_to_all(mixed_out, ('seq', 'batch'), split_axis=0, concat_axis=0,...  6.46 us
    all_to_all x1, starting transfers between devices, body(): lax.all_to_all(cot_out, ('seq', 'batch'), split_axis=0, concat_axis=0, ti...  6.13 us
  transfers between devices with their start and end apart: 31, of which 8 were waited for; matrix products, arithmetic and copies ran while one was open for 0% of the time, Pallas kernels for 62%

profile of v6, /device:TPU:0, one launch (start us, length us, event | category | flops | bytes accessed | tf_op | source)
XLA Modules:
  0.0 238.9 jit_solution(17928192787763141397)
XLA Ops:
  2.5 7.3 %all-to-all-start = ((s32[32,1,32]{2,1,0:T(1,128)}), s32[32,1,32]{2,1,0:T(1,128)S(1)}, u32[]{:S(2)}, u32[]{:S(2)}) async-start(s32[32,1,32]{2,1,0:T(1,128)} %bitcast.2), calls=%async_computation | async-start | bytes 32768 | tf_op jit(solution)/shard_map/all_to_all | solution.py:766
  9.8 8.4 %attend_first.1 = (bf16[1024,256]{1,0:T(8,128)(2,1)}, bf16[1024,256]{1,0:T(8,128)(2,1)}, bf16[1024,256]{1,0:T(8,128)(2,1)}, bf16[1024,256]{1,0:T(8,128)(2,1)}, b...) custom-call(s32[1,2]{1,0:T(1,128)S(1)} %copy-done.18, s32[12]{0:T(128)S(1)} %copy-done.19, ...), custom_call_target="tpu_custom_call" | custom-call | flops 49999998976 | bytes 1 | tf_op jit(solution)/shard_map/attend_first/pallas_call | solution.py:102
  18.3 3.5 %cot_gather.1 = (bf16[1024,768]{1,0:T(8,128)(2,1)}, s32[1,1024]{1,0:T(1,128)S(1)}) custom-call(s32[32,32]{1,0:T(8,128)S(1)} %bitcast.13, bf16[896,768]{1,0:T(8,128)(2,1)S(1)} %copy-done.7, bf16[1024,256]{1,0:T(8,128)(2,1)} %get-tuple-element.97.refs_2_), custom_call_target="tpu_custom_call" | custom-call | flops 10000000000 | bytes 1 | tf_op jit(solution)/shard_map/cot_gather/pallas_call | solution.py:102
  21.8 6.1 %all-to-all-start.2 = ((bf16[32,32,768]{2,1,0:T(8,128)(2,1)}), bf16[32,32,768]{2,1,0:T(8,128)(2,1)}, u32[]{:S(2)}, u32[]{:S(2)}) async-start(bf16[32,32,768]{2,1,0:T(8,128)(2,1)} %bitcast.8), calls=%async_computation.2 | async-start | bytes 3145728 | tf_op jit(solution)/shard_map/all_to_all | solution.py:804
  28.0 19.7 %attend_rest.1 = (bf16[1024,512]{1,0:T(8,128)(2,1)}, bf16[1024,512]{1,0:T(8,128)(2,1)}, bf16[1024,512]{1,0:T(8,128)(2,1)}, bf16[8,2,512,512]{3,2,1,0:T(8,128)(2,...) custom-call(s32[1,2]{1,0:T(1,128)S(1)} %copy-done.18, ...), custom_call_target="tpu_custom_call" | custom-call | flops 49999998976 | bytes 1 | tf_op jit(solution)/shard_map/attend_rest/pallas_call | solution.py:102
  47.8 20.1 %ffn.1 = (bf16[1024,3072]{1,0:T(8,128)(2,1)}, bf16[1024,3072]{1,0:T(8,128)(2,1)}, bf16[1024,768]{1,0:T(8,128)(2,1)}, f32[1024,1]{1,0:T(8,128)}, bf16[1024,768]{1,0:T(8,128)(2,1)S(1)}) custom-call(bf16[1024,768]{1,0:T(8,128)(2,1)} %get-tuple-element.100.refs_0_.refs_1_, bf16[768,3072]{1,0:T(8,128)(2,1)} %refs_2_.9, f32[3072]{0:T(1024)S(1)} %copy-done.9, ...), custom_call_target="tpu_custom_call" | custom-call | flops 49999998976 | bytes 1 | tf_op jit(solution)/shard_map/ffn/pallas_call | solution.py:102
  67.8 3.0 %mixed_slots.1.refs_5_ = bf16[1024,768]{1,0:T(8,128)(2,1)} custom-call(s32[1,1024]{1,0:T(1,128)S(1)} %get-tuple-element.96.refs_7_.refs_0_, bf16[1024,768]{1,0:T(8,128)(2,1)S(1)} %get-tuple-element.102.refs_1_, f32[1024,1]{1,0:T(8,128)} %get-tuple-element.103.refs_2_.refs_3_), custom_call_target="tpu_custom_call" | custom-call | flops 49999998976 | bytes 1 | tf_op jit(solution)/shard_map/mixed_slots/pallas_call | solution.py:102
  70.8 6.5 %all-to-all-start.1 = ((bf16[32,32,768]{2,1,0:T(8,128)(2,1)}), bf16[32,32,768]{2,1,0:T(8,128)(2,1)}, u32[]{:S(2)}, u32[]{:S(2)}) async-start(bf16[32,32,768]{2,1,0:T(8,128)(2,1)} %bitcast.4), calls=%async_computation.1 | async-start | bytes 3145728 | tf_op jit(solution)/shard_map/all_to_all | solution.py:854
  77.3 5.4 %cot_back.1 = (f32[1024,768]{1,0:T(8,128)S(1)}, bf16[1024,768]{1,0:T(8,128)(2,1)S(1)}, f32[8,768]{1,0:T(8,128)S(1)}) custom-call(s32[1,1024]{1,0:T(1,128)S(1)} %get-tuple-element.96.refs_7_.refs_0_, bf16[1024,768]{1,0:T(8,128)(2,1)} %bitcast.9.refs_1_, bf16[1024,768]{1,0:T(8,128)(2,1)} %get-tuple-element.109.refs_2_, ...), custom_call_target="tpu_custom_call" | custom-call | flops 49999998976 | bytes 1 | tf_op jit(solution)/shard_map/cot_back/pallas_call | solution.py:102
  82.7 14.1 %down_back.1 = (bf16[1024,3072]{1,0:T(8,128)(2,1)S(1)}, f32[1,3072]{1,0:T(1,128)S(1)}, bf16[2,768,768]{2,1,0:T(8,128)(2,1)S(1)}, bf16[2,768,768]{2,1,0:T(8,128)(2,1)S(1)}) custom-call(s32[2]{0:T(128)S(1)} %pad_add_fusion.refs_0_, bf16[1024,768]{1,0:T(8,128)(2,1)S(1)} %get-tuple-element.111.refs_1_, bf16[3072,768]{1,0:T(8,128)(2,1)} %refs_2_.8, ...), custom_call_target="tpu_custom_call" | custom-call | flops 49999998976 | bytes 1 | tf_op jit(solution)/shard_map/down_back/pallas_call | solution.py:102
  97.3 7.0 %in_back.1 = (bf16[384,3072]{1,0:T(8,128)(2,1)S(1)}, bf16[384,3072]{1,0:T(8,128)(2,1)S(1)}) custom-call(s32[2]{0:T(128)S(1)} %pad_add_fusion.refs_0_, bf16[1024,768]{1,0:T(8,128)(2,1)S(1)} %copy-done.27, bf16[1024,3072]{1,0:T(8,128)(2,1)S(1)} %get-tuple-element.115.refs_2_.refs_1_, f32[1,3072]{1,0:T(1,128)S(1)} %get-tuple-element.119.refs_3_.refs_6_), custom_call_target="tpu_custom_call" | custom-call | flops 49999998976 | bytes 1 | tf_op jit(solution)/shard_map/in_back/pallas_call | solution.py:102
  113.7 10.6 %first_back.1 = (f32[1024,768]{1,0:T(8,128)S(1)}, bf16[1024,768]{1,0:T(8,128)(2,1)S(1)}, bf16[1024,768]{1,0:T(8,128)(2,1)S(1)}, f32[8,768]{1,0:T(8,128)S(1)}) custom-call(f32[1024,768]{1,0:T(8,128)S(1)} %get-tuple-element.110.refs_0_, bf16[1024,3072]{1,0:T(8,128)(2,1)S(1)} %copy-done.21, bf16[768,3072]{1,0:T(8,128)(2,1)S(1)} %bitcast.15, ...), custom_call_target="tpu_custom_call" | custom-call | flops 49999998976 | bytes 1 | tf_op jit(solution)/shard_map/first_back/pallas_call | solution.py:102
  126.4 7.8 %attend_back.3 = (bf16[1024,768]{1,0:T(8,128)(2,1)S(1)}, f32[1,768]{1,0:T(1,128)S(1)}) custom-call(s32[1,2]{1,0:T(1,128)S(1)} %copy-done.18, s32[12]{0:T(128)S(1)} %copy-done.19, bf16[1024,256]{1,0:T(8,128)(2,1)} %get-tuple-element.97.refs_2_, bf16[1024,256]{1,0:T(8,128)(2,1)} %get-tuple-element.134.refs_3_, bf16[1024,256]{1,0:T(8,128)(2,1)} %get-tuple-element.135.refs_4_, ...), custom_call_target="tpu_custom_call" | custom-call | flops 49999998976 | bytes 1 | tf_op jit(solution)/shard_map/attend_back/pallas_call | solution.py:102
  134.2 4.5 %attn_a_w.1 = (bf16[768,768]{1,0:T(8,128)(2,1)S(1)}, bf16[768,768]{1,0:T(8,128)(2,1)S(1)}) custom-call(s32[2]{0:T(128)S(1)} %pad_add_fusion.refs_0_, bf16[1024,768]{1,0:T(8,128)(2,1)S(1)} %copy-done.26, bf16[1024,768]{1,0:T(8,128)(2,1)S(1)} %get-tuple-element.133.refs_2_, bf16[1024,768]{1,0:T(8,128)(2,1)S(1)} %copy-done, ...), custom_call_target="tpu_custom_call" | custom-call | flops 49999998976 | bytes 1 | tf_op jit(solution)/shard_map/attn_a_w/pallas_call | solution.py:102
  146.5 7.5 %attend_back.4 = (bf16[1024,768]{1,0:T(8,128)(2,1)S(1)}, f32[1,768]{1,0:T(1,128)S(1)}) custom-call(s32[1,2]{1,0:T(1,128)S(1)} %copy-done.18, s32[12]{0:T(128)S(1)} %copy-done.19, bf16[1024,512]{1,0:T(8,128)(2,1)} %get-tuple-element.104.refs_2_, bf16[1024,512]{1,0:T(8,128)(2,1)} %get-tuple-element.105.refs_3_, bf16[1024,512]{1,0:T(8,128)(2,1)} %get-tuple-element.106.refs_4_, ...), custom_call_target="tpu_custom_call" | custom-call | flops 49999998976 | bytes 1 | tf_op jit(solution)/shard_map/attend_back/pallas_call | solution.py:102
  154.2 2.4 %collective-permute-start.10 = (bf16[384,384]{1,0:T(8,128)(2,1)S(1)}, bf16[384,384]{1,0:T(8,128)(2,1)S(1)}, u32[]{:S(2)}, u32[]{:S(2)}) collective-permute-start(bf16[384,384]{1,0:T(8,128)(2,1)S(1)} %w_down_a.1.refs_3_.refs_0_), channel_id=1, source_target_pairs={{0,4},{1,5},{2,6},{3,7},{4,0},{5,1},{6,2},{7,3},{8,12},{9,13},{10,... | collective-permute-start | bytes 884744 | tf_op jit(solution)/shard_map/ppermute | solution.py:644
  160.4 7.5 %attend_back.5 = (bf16[1024,768]{1,0:T(8,128)(2,1)S(1)}, f32[1,768]{1,0:T(1,128)S(1)}) custom-call(s32[1,2]{1,0:T(1,128)S(1)} %copy-done.18, s32[12]{0:T(128)S(1)} %copy-done.19, bf16[1024,512]{1,0:T(8,128)(2,1)} %get-tuple-element.104.refs_2_, bf16[1024,512]{1,0:T(8,128)(2,1)} %get-tuple-element.105.refs_3_, bf16[1024,512]{1,0:T(8,128)(2,1)} %get-tuple-element.106.refs_4_, ...), custom_call_target="tpu_custom_call" | custom-call | flops 49999998976 | bytes 1 | tf_op jit(solution)/shard_map/attend_back/pallas_call | solution.py:102
  170.1 4.9 %attn_b_w.1 = (bf16[832,768]{1,0:T(8,128)(2,1)S(1)}, bf16[832,768]{1,0:T(8,128)(2,1)S(1)}) custom-call(s32[2]{0:T(128)S(1)} %pad_add_fusion.refs_0_, bf16[1024,768]{1,0:T(8,128)(2,1)S(1)} %copy-done, bf16[1024,768]{1,0:T(8,128)(2,1)S(1)} %get-tuple-element.142.refs_2_.refs_1_, bf16[1024,768]{1,0:T(8,128)(2,1)S(1)} %copy-done, ...), custom_call_target="tpu_custom_call" | custom-call | flops 1000000000 | bytes 1 | tf_op jit(solution)/shard_map/attn_b_w/pallas_call | solution.py:102
  180.6 7.0 %input_grad.1.refs_3_ = bf16[1024,768]{1,0:T(8,128)(2,1)} custom-call(bf16[1024,768]{1,0:T(8,128)(2,1)S(1)} %copy-done.25, bf16[1024,768]{1,0:T(8,128)(2,1)S(1)} %get-tuple-element.142.refs_2_.refs_1_, bf16[1024,768]{1,0:T(8,128)(2,1)S(1)} %get-tuple-element.149.refs_4_.refs_2_, bf16[768,2304]{1,0:T(8,128)(2,1)} %refs_5_.9, bf16[768,2304]{1,0:T(8,128)(2,1)} %refs_5_.9, ...), custom_call_target="tpu_custom_call" | custom-call | flops 49999998976 | bytes 1 | tf_op jit(solution)/shard_map/input_grad/pallas_call | solution.py:102
  191.5 4.1 %mixed_place.1.refs_3_ = bf16[896,768]{1,0:T(8,128)(2,1)} custom-call(s32[1,1024]{1,0:T(1,128)S(1)} %copy-done.30, bf16[1024,768]{1,0:T(8,128)(2,1)} %bitcast.5.refs_1_, bf16[416,384]{1,0:T(8,128)(2,1)S(1)} %get-tuple-element.161.refs_2_.refs_1_), custom_call_target="tpu_custom_call" | custom-call | flops 10000000000 | bytes 1 | tf_op jit(solution)/shard_map/mixed_place/pallas_call | solution.py:102
  200.9 9.0 %collective-permute-done.20.refs_2_ = bf16[96,1536]{1,0:T(8,128)(2,1)S(1)} collective-permute-done((bf16[96,1536]{1,0:T(8,128)(2,1)S(1)}, bf16[96,1536]{1,0:T(8,128)(2,1)S(1)}, u32[]{:S(2)}, u32[]{:S(2)}) %collective-permute-start.20) | collective-permute-done | bytes 294944 | tf_op jit(solution)/shard_map/ppermute | solution.py:644
  216.4 4.6 %collective-permute-done.22.refs_1_ = bf16[208,384]{1,0:T(8,128)(2,1)S(1)} collective-permute-done((bf16[208,384]{1,0:T(8,128)(2,1)S(1)}, bf16[208,384]{1,0:T(8,128)(2,1)S(1)}, u32[]{:S(2)}, u32[]{:S(2)}) %collective-permute-start.22) | collective-permute-done | bytes 159776 | tf_op jit(solution)/shard_map/ppermute | solution.py:644
  222.3 4.1 %collective-permute-done.25.refs_2_ = bf16[208,384]{1,0:T(8,128)(2,1)S(1)} collective-permute-done((bf16[208,384]{1,0:T(8,128)(2,1)S(1)}, bf16[208,384]{1,0:T(8,128)(2,1)S(1)}, u32[]{:S(2)}, u32[]{:S(2)}) %collective-permute-start.25) | collective-permute-done | bytes 159776 | tf_op jit(solution)/shard_map/ppermute | solution.py:644
  232.1 4.5 %collective-permute-done.26.refs_4_ = bf16[416,384]{1,0:T(8,128)(2,1)S(1)} collective-permute-done((bf16[416,384]{1,0:T(8,128)(2,1)S(1)}, bf16[416,384]{1,0:T(8,128)(2,1)S(1)}, u32[]{:S(2)}, u32[]{:S(2)}) %collective-permute-start.26) | collective-permute-done | bytes 319520 | tf_op jit(solution)/shard_map/ppermute | solution.py:644
  (150 shorter events, 57.9 us)
Async XLA Ops:
  2.5 15.8 %all-to-all-start = ((s32[32,1,32]{2,1,0:T(1,128)}), s32[32,1,32]{2,1,0:T(1,128)S(1)}, u32[]{:S(2)}, u32[]{:S(2)}) async-start(s32[32,1,32]{2,1,0:T(1,128)} %bitcast.2), calls=%async_computation | async-start | bytes 32768 | tf_op jit(solution)/shard_map/all_to_all | solution.py:766
  21.8 49.0 %all-to-all-start.2 = ((bf16[32,32,768]{2,1,0:T(8,128)(2,1)}), bf16[32,32,768]{2,1,0:T(8,128)(2,1)}, u32[]{:S(2)}, u32[]{:S(2)}) async-start(bf16[32,32,768]{2,1,0:T(8,128)(2,1)} %bitcast.8), calls=%async_computation.2 | async-start | bytes 3145728 | tf_op jit(solution)/shard_map/all_to_all | solution.py:804
  70.8 120.7 %all-to-all-start.1 = ((bf16[32,32,768]{2,1,0:T(8,128)(2,1)}), bf16[32,32,768]{2,1,0:T(8,128)(2,1)}, u32[]{:S(2)}, u32[]{:S(2)}) async-start(bf16[32,32,768]{2,1,0:T(8,128)(2,1)} %bitcast.4), calls=%async_computation.1 | async-start | bytes 3145728 | tf_op jit(solution)/shard_map/all_to_all | solution.py:854
  105.8 18.5 %collective-permute-start.3 = (bf16[1536,384]{1,0:T(8,128)(2,1)S(1)}, bf16[1536,384]{1,0:T(8,128)(2,1)S(1)}, u32[]{:S(2)}, u32[]{:S(2)}) collective-permute-start(bf16[1536,384]{1,0:T(8,128)(2,1)S(1)} %get-tuple-element.129), channel_id=1, source_target_pairs={{0,16},{1,17},{2,18},{3,19},{4,20},{5,21},{6,22},{7,23},{8,9},{9,8... | collective-permute-start | bytes 3538952 | tf_op jit(solution)/shard_map/ppermute | solution.py:654
  111.2 32.2 %collective-permute-start.2 = (bf16[384,1536]{1,0:T(8,128)(2,1)}, bf16[384,1536]{1,0:T(8,128)(2,1)}, u32[]{:S(2)}, u32[]{:S(2)}) collective-permute-start(bf16[384,1536]{1,0:T(8,128)(2,1)} %get-tuple-element.128), channel_id=1, source_target_pairs={{0,16},{1,17},{2,18},{3,19},{4,20},{5,21},{6,22},{7,23},{8,9},{9,8... | collective-permute-start | bytes 3538952 | tf_op jit(solution)/shard_map/ppermute | solution.py:654
  124.6 16.3 %collective-permute-start.4 = (bf16[768,384]{1,0:T(8,128)(2,1)S(1)}, bf16[768,384]{1,0:T(8,128)(2,1)S(1)}, u32[]{:S(2)}, u32[]{:S(2)}) collective-permute-start(bf16[768,384]{1,0:T(8,128)(2,1)S(1)} %get-tuple-element.132), channel_id=1, source_target_pairs={{0,1},{1,0},{2,3},{3,2},{4,5},{5,4},{6,7},{7,6},{8,24},{9,25},{10,... | collective-permute-start | bytes 1769480 | tf_op jit(solution)/shard_map/ppermute | solution.py:654
  138.7 19.1 %collective-permute-start.5 = (bf16[768,768]{1,0:T(8,128)(2,1)S(1)}, bf16[768,768]{1,0:T(8,128)(2,1)S(1)}, u32[]{:S(2)}, u32[]{:S(2)}) collective-permute-start(bf16[768,768]{1,0:T(8,128)(2,1)S(1)} %get-tuple-element.139.refs_3_), channel_id=1, source_target_pairs={{0,8},{8,0},{16,24},{24,16},{1,9},{9,1},{17,25},{25,17},{2,10},{10... | collective-permute-start | bytes 3538952 | tf_op jit(solution)/shard_map/ppermute | solution.py:644
  141.7 12.4 %collective-permute-start.7 = (bf16[384,384]{1,0:T(8,128)(2,1)S(1)}, bf16[384,384]{1,0:T(8,128)(2,1)S(1)}, u32[]{:S(2)}, u32[]{:S(2)}) collective-permute-start(bf16[384,384]{1,0:T(8,128)(2,1)S(1)} %get-tuple-element.145), channel_id=1, source_target_pairs={{0,2},{1,3},{2,0},{3,1},{4,6},{5,7},{6,4},{7,5},{8,10},{9,11},{10,... | collective-permute-start | bytes 884744 | tf_op jit(solution)/shard_map/ppermute | solution.py:644
  144.9 11.7 %collective-permute-start.6 = (bf16[192,1536]{1,0:T(8,128)(2,1)S(1)}, bf16[192,1536]{1,0:T(8,128)(2,1)S(1)}, u32[]{:S(2)}, u32[]{:S(2)}) collective-permute-start(bf16[192,1536]{1,0:T(8,128)(2,1)S(1)} %get-tuple-element.144), channel_id=1, source_target_pairs={{0,1},{1,0},{2,3},{3,2},{4,5},{5,4},{6,7},{7,6},{8,24},{9,25},{10,... | collective-permute-start | bytes 1769480 | tf_op jit(solution)/shard_map/ppermute | solution.py:654
  154.2 22.2 %collective-permute-start.10 = (bf16[384,384]{1,0:T(8,128)(2,1)S(1)}, bf16[384,384]{1,0:T(8,128)(2,1)S(1)}, u32[]{:S(2)}, u32[]{:S(2)}) collective-permute-start(bf16[384,384]{1,0:T(8,128)(2,1)S(1)} %w_down_a.1.refs_3_.refs_0_), channel_id=1, source_target_pairs={{0,4},{1,5},{2,6},{3,7},{4,0},{5,1},{6,2},{7,3},{8,12},{9,13},{10,... | collective-permute-start | bytes 884744 | tf_op jit(solution)/shard_map/ppermute | solution.py:644
  157.3 17.7 %collective-permute-start.11 = (bf16[96,1536]{1,0:T(8,128)(2,1)S(1)}, bf16[96,1536]{1,0:T(8,128)(2,1)S(1)}, u32[]{:S(2)}, u32[]{:S(2)}) collective-permute-start(bf16[96,1536]{1,0:T(8,128)(2,1)S(1)} %get-tuple-element.155), channel_id=1, source_target_pairs={{0,2},{1,3},{2,0},{3,1},{4,6},{5,7},{6,4},{7,5},{8,10},{9,11},{10,... | collective-permute-start | bytes 884744 | tf_op jit(solution)/shard_map/ppermute | solution.py:644
  158.8 9.9 %collective-permute-start.8 = (bf16[768,384]{1,0:T(8,128)(2,1)S(1)}, bf16[768,384]{1,0:T(8,128)(2,1)S(1)}, u32[]{:S(2)}, u32[]{:S(2)}) collective-permute-start(bf16[768,384]{1,0:T(8,128)(2,1)S(1)} %get-tuple-element.151), channel_id=1, source_target_pairs={{0,16},{1,17},{2,18},{3,19},{4,20},{5,21},{6,22},{7,23},{8,9},{9,8... | collective-permute-start | bytes 1769480 | tf_op jit(solution)/shard_map/ppermute | solution.py:654
  168.9 18.6 %collective-permute-start.13 = (bf16[384,384]{1,0:T(8,128)(2,1)S(1)}, bf16[384,384]{1,0:T(8,128)(2,1)S(1)}, u32[]{:S(2)}, u32[]{:S(2)}) collective-permute-start(bf16[384,384]{1,0:T(8,128)(2,1)S(1)} %get-tuple-element.158), channel_id=1, source_target_pairs={{0,1},{1,0},{2,3},{3,2},{4,5},{5,4},{6,7},{7,6},{8,24},{9,25},{10,... | collective-permute-start | bytes 884744 | tf_op jit(solution)/shard_map/ppermute | solution.py:654
  175.1 21.7 %collective-permute-start.16 = (bf16[96,1536]{1,0:T(8,128)(2,1)S(1)}, bf16[96,1536]{1,0:T(8,128)(2,1)S(1)}, u32[]{:S(2)}, u32[]{:S(2)}) collective-permute-start(bf16[96,1536]{1,0:T(8,128)(2,1)S(1)} %w_in_a.1.refs_2_.refs_0_), channel_id=1, source_target_pairs={{0,4},{1,5},{2,6},{3,7},{4,0},{5,1},{6,2},{7,3},{8,12},{9,13},{10,... | collective-permute-start | bytes 884744 | tf_op jit(solution)/shard_map/ppermute | solution.py:644
  176.4 19.1 %collective-permute-start.17 = (bf16[384,384]{1,0:T(8,128)(2,1)S(1)}, bf16[384,384]{1,0:T(8,128)(2,1)S(1)}, u32[]{:S(2)}, u32[]{:S(2)}) collective-permute-start(bf16[384,384]{1,0:T(8,128)(2,1)S(1)} %w_down_f.1.refs_3_.refs_1_), channel_id=1, source_target_pairs={{0,2},{1,3},{2,0},{3,1},{4,6},{5,7},{6,4},{7,5},{8,10},{9,11},{10,... | collective-permute-start | bytes 884744 | tf_op jit(solution)/shard_map/ppermute | solution.py:644
  179.0 10.8 %collective-permute-start.12 = (bf16[832,384]{1,0:T(8,128)(2,1)S(1)}, bf16[832,384]{1,0:T(8,128)(2,1)S(1)}, u32[]{:S(2)}, u32[]{:S(2)}) collective-permute-start(bf16[832,384]{1,0:T(8,128)(2,1)S(1)} %get-tuple-element.157), channel_id=1, source_target_pairs={{0,16},{1,17},{2,18},{3,19},{4,20},{5,21},{6,22},{7,23},{8,9},{9,8... | collective-permute-start | bytes 1916936 | tf_op jit(solution)/shard_map/ppermute | solution.py:654
  188.2 10.1 %collective-permute-start.14 = (bf16[192,384]{1,0:T(8,128)(2,1)S(1)}, bf16[192,384]{1,0:T(8,128)(2,1)S(1)}, u32[]{:S(2)}, u32[]{:S(2)}) collective-permute-start(bf16[192,384]{1,0:T(8,128)(2,1)S(1)} %get-tuple-element.162), channel_id=1, source_target_pairs={{0,2},{1,3},{2,0},{3,1},{4,6},{5,7},{6,4},{7,5},{8,10},{9,11},{10,... | collective-permute-start | bytes 442376 | tf_op jit(solution)/shard_map/ppermute | solution.py:644
  196.2 18.0 %collective-permute-start.23 = (bf16[768,384]{1,0:T(8,128)(2,1)S(1)}, bf16[768,384]{1,0:T(8,128)(2,1)S(1)}, u32[]{:S(2)}, u32[]{:S(2)}) collective-permute-start(bf16[768,384]{1,0:T(8,128)(2,1)S(1)} %w_down_g.1.refs_2_.refs_1_), channel_id=1, source_target_pairs={{0,1},{1,0},{2,3},{3,2},{4,5},{5,4},{6,7},{7,6},{8,9},{9,8},{10,11... | collective-permute-start | bytes 1769480 | tf_op jit(solution)/shard_map/ppermute | solution.py:644
  196.9 13.0 %collective-permute-start.20 = (bf16[96,1536]{1,0:T(8,128)(2,1)S(1)}, bf16[96,1536]{1,0:T(8,128)(2,1)S(1)}, u32[]{:S(2)}, u32[]{:S(2)}) collective-permute-start(bf16[96,1536]{1,0:T(8,128)(2,1)S(1)} %w_in_f.1.refs_3_.refs_1_), channel_id=1, source_target_pairs={{0,2},{1,3},{2,0},{3,1},{4,6},{5,7},{6,4},{7,5},{8,10},{9,11},{10,... | collective-permute-start | bytes 884744 | tf_op jit(solution)/shard_map/ppermute | solution.py:644
  198.3 15.2 %collective-permute-start.18 = (bf16[192,384]{1,0:T(8,128)(2,1)S(1)}, bf16[192,384]{1,0:T(8,128)(2,1)S(1)}, u32[]{:S(2)}, u32[]{:S(2)}) collective-permute-start(bf16[192,384]{1,0:T(8,128)(2,1)S(1)} %attn_a_a.1.refs_3_.refs_0_), channel_id=1, source_target_pairs={{0,4},{1,5},{2,6},{3,7},{4,0},{5,1},{6,2},{7,3},{8,12},{9,13},{10,... | collective-permute-start | bytes 442376 | tf_op jit(solution)/shard_map/ppermute | solution.py:644
  200.0 11.9 %collective-permute-start.19 = (bf16[208,384]{1,0:T(8,128)(2,1)S(1)}, bf16[208,384]{1,0:T(8,128)(2,1)S(1)}, u32[]{:S(2)}, u32[]{:S(2)}) collective-permute-start(bf16[208,384]{1,0:T(8,128)(2,1)S(1)} %get-tuple-element.165), channel_id=1, source_target_pairs={{0,2},{1,3},{2,0},{3,1},{4,6},{5,7},{6,4},{7,5},{8,10},{9,11},{10,... | collective-permute-start | bytes 479240 | tf_op jit(solution)/shard_map/ppermute | solution.py:644
  210.5 17.0 %collective-permute-start.27 = (bf16[192,1536]{1,0:T(8,128)(2,1)S(1)}, bf16[192,1536]{1,0:T(8,128)(2,1)S(1)}, u32[]{:S(2)}, u32[]{:S(2)}) collective-permute-start(bf16[192,1536]{1,0:T(8,128)(2,1)S(1)} %w_in_g.1.refs_2_.refs_1_), channel_id=1, source_target_pairs={{0,1},{1,0},{2,3},{3,2},{4,5},{5,4},{6,7},{7,6},{8,9},{9,8},{10,11... | collective-permute-start | bytes 1769480 | tf_op jit(solution)/shard_map/ppermute | solution.py:644
  222.0 10.0 %collective-permute-start.24 = (bf16[384,384]{1,0:T(8,128)(2,1)S(1)}, bf16[384,384]{1,0:T(8,128)(2,1)S(1)}, u32[]{:S(2)}, u32[]{:S(2)}) collective-permute-start(bf16[384,384]{1,0:T(8,128)(2,1)S(1)} %attn_a_g.1.refs_3_.refs_1_), channel_id=1, source_target_pairs={{0,1},{1,0},{2,3},{3,2},{4,5},{5,4},{6,7},{7,6},{8,9},{9,8},{10,11... | collective-permute-start | bytes 884744 | tf_op jit(solution)/shard_map/ppermute | solution.py:644
  227.0 9.6 %collective-permute-start.26 = (bf16[416,384]{1,0:T(8,128)(2,1)S(1)}, bf16[416,384]{1,0:T(8,128)(2,1)S(1)}, u32[]{:S(2)}, u32[]{:S(2)}) collective-permute-start(bf16[416,384]{1,0:T(8,128)(2,1)S(1)} %attn_b_g.1.refs_3_), channel_id=1, source_target_pairs={{0,1},{1,0},{2,3},{3,2},{4,5},{5,4},{6,7},{7,6},{8,9},{9,8},{10,11... | collective-permute-start | bytes 958472 | tf_op jit(solution)/shard_map/ppermute | solution.py:644
  (40 other events, 305.8 us)
